TPU v7x, 512 devices: a whole 4x4x16 slice. The times are simulated.
512 devices in a mesh: band: 16 (over x, z_lo), mesh: 32 (over z_hi, y, core).
Axes of the slice: x: 4, y: 4, z: 16 (z_hi: 4, z_lo: 4; z = z_hi * 4 + z_lo), core: 2. Of those that a mesh axis runs over, the one named last changes fastest.
Arguments:
- vectors: float32 [512, 65536], P('band', 'mesh'), may hold values from -6 to 6
- potential: float32 [65536], P('mesh'), may hold values from 0.5 to 3
- cell_scale: float32 [256], P('mesh'), may hold values from 0.5 to 2
- cell_matrix: float32 [343, 343], replicated, may hold values from -1 to 2, as said below
- cell_nodes: int32 [256, 343], P('mesh'), may hold values from 0 to 2559
- send_list: int32 [32, 4, 128], P('mesh'), may hold values from 0 to 2047, as said below
- node_count: int32 [32], P('mesh'), may hold values from 1024 to 2048, as said below
- filter_bounds: float32 [3], replicated, may hold values from -1 to 30, as said below
Outputs:
- filtered: float32 [512, 65536], P('band', 'mesh')
- hproj: float32 [512, 512], P('band')
Inputs may be any that keep to these rules, and one draw needn't show every extreme that they name: Partition p's live nodes are its local indices below node_count[p]; some partition has all 2048 live. send_list[q, k, :] are distinct live local nodes of partition q, sent to partition (q - o_k) mod 32 with o = (-2, -1, 1, 2). `cell_matrix`: symmetric. filter_bounds[0] lies in [-1, 0], filter_bounds[1] in [6, 8], filter_bounds[2] in [24, 30].
All inputs are finite; a program needn't handle non-finite values.
Results may differ from a plain program's by a relative error of at most 0.0001.
Values sent between devices are 32-bit elements; how exact they have to be, the bound alone decides.
No kernel may reach another device: no remote copies, remote signals or barrier semaphores. Data moves between devices by JAX's collectives and lax.ppermute only.
A program may use at most 64 MiB of HBM per device.

v0:
```python
import jax
import jax.numpy as jnp
from jax import lax
from jax.sharding import PartitionSpec as P

DEGREE = 3


OFFSETS = (-2, -1, 1, 2)
HIGHEST = lax.Precision.HIGHEST


def passed_along(block, axis, distance):
    devices = range(lax.axis_size(axis))
    route = [((i - distance) % len(devices), i) for i in devices]
    return lax.ppermute(block, axis, route)


def send_ghosts(outgoing, slot_count):
    pieces = []
    for which_list in range(4):
        piece = outgoing[:, which_list * slot_count : (which_list + 1) * slot_count]
        pieces.append(passed_along(piece, "mesh", -OFFSETS[which_list]))
    return jnp.concatenate(pieces, axis=1)


def return_sums(ghost_sums, slot_count):
    pieces = []
    for which_list in range(4):
        piece = ghost_sums[:, which_list * slot_count : (which_list + 1) * slot_count]
        pieces.append(passed_along(piece, "mesh", OFFSETS[which_list]))
    return jnp.concatenate(pieces, axis=1)


def cell_product(values, cell_matrix):
    return jnp.einsum("bcn,nm->bcm", values, cell_matrix, precision=HIGHEST)


def apply_operator(vectors, potential, cell_scale, cell_matrix, cell_index, send_rows, slot_count):
    band_count = vectors.shape[0]
    node_width = vectors.shape[1]
    cell_count = cell_index.shape[0]
    per_cell = cell_index.shape[1]
    outgoing = jnp.take(vectors, send_rows, axis=1)
    ghosts = send_ghosts(outgoing, slot_count)
    flat_index = cell_index.reshape(-1)
    extended = jnp.concatenate([vectors, ghosts], axis=1)
    cell_values = jnp.take(extended, flat_index, axis=1).reshape(band_count, cell_count, per_cell)
    products = cell_product(cell_values, cell_matrix) * cell_scale[None, :, None]
    sums = (
        jnp.zeros((band_count, node_width + 4 * slot_count), jnp.float32)
        .at[:, flat_index]
        .add(products.reshape(band_count, -1))
    )
    arrived = return_sums(sums[:, node_width:], slot_count)
    own_sums = sums[:, :node_width].at[:, send_rows].add(arrived)
    return own_sums + potential[None, :] * vectors


def filter_pass(vectors, operator, filter_bounds):
    lowest = filter_bounds[0]
    wanted_top = filter_bounds[1]
    upper = filter_bounds[2]
    half_width = (upper - wanted_top) / 2.0
    centre = (upper + wanted_top) / 2.0
    sigma_now = half_width / (lowest - centre)
    gamma_ratio = 2.0 / sigma_now
    previous = vectors
    current = sigma_now / half_width * (operator(vectors) - centre * vectors)
    for degree_step in range(DEGREE - 1):
        sigma_next = 1.0 / (gamma_ratio - sigma_now)
        following = (
            2.0 * sigma_next / half_width * (operator(current) - centre * current)
            - sigma_now * sigma_next * previous
        )
        previous = current
        current = following
        sigma_now = sigma_next
    return current


def row_products(left_rows, right_rows):
    return lax.dot_general(left_rows, right_rows, (((1,), (1,)), ((), ())), precision=HIGHEST)


def body(
    vectors, potential, cell_scale, cell_matrix, cell_nodes, send_list, node_count, filter_bounds
):
    band_rows = vectors.shape[0]
    node_width = vectors.shape[1]
    slot_count = send_list.shape[2]
    send_rows = send_list[0].reshape(-1)
    positions = jnp.arange(node_width, dtype=jnp.int32)
    start_vectors = jnp.where(
        (positions < node_count[0])[None, :], vectors, jnp.zeros_like(vectors)
    )

    def operator(field):
        return apply_operator(
            field, potential, cell_scale, cell_matrix, cell_nodes, send_rows, slot_count
        )

    filtered = filter_pass(start_vectors, operator, filter_bounds)
    filtered = filter_pass(filtered, operator, filter_bounds)
    applied = operator(filtered)
    band_size = lax.axis_size("band")
    band_index = lax.axis_index("band")
    row_block_sums = jnp.zeros((band_rows, band_rows * band_size), jnp.float32)
    row_block_sums = lax.dynamic_update_slice_in_dim(
        row_block_sums, row_products(applied, filtered), band_index * band_rows, 1
    )

    def turn(turn_number, loop_state):
        band_block, block_sums = loop_state
        band_block = passed_along(band_block, "band", 1)
        source = (band_index - turn_number) % band_size
        block_sums = lax.dynamic_update_slice_in_dim(
            block_sums, row_products(applied, band_block), source * band_rows, 1
        )
        return (band_block, block_sums)

    partial_rows = lax.fori_loop(1, band_size, turn, (filtered, row_block_sums))[1]
    node_total = node_width * lax.axis_size("mesh")
    hproj = lax.psum(partial_rows, "mesh") / node_total
    return (filtered, hproj)


def solution(mesh):
    placed = (
        P("band", "mesh"),
        P("mesh"),
        P("mesh"),
        P(),
        P("mesh", None),
        P("mesh", None, None),
        P("mesh"),
        P(),
    )
    return jax.shard_map(
        body,
        mesh=mesh,
        in_specs=placed,
        out_specs=(P("band", "mesh"), P("band", None)),
        check_vma=False,
    )
```

profile of v0, /device:TPU:1, one launch (start us, length us, event | category | flops | bytes accessed | tf_op | source)
XLA Modules:
  0.0 1172.5 jit_solution(1827097597473391386)
XLA Ops:
  27.1 9.7 collective-permute-start.4
  51.9 16.8 %scatter_custom_fusion = f32[32,2560]{0,1:T(8,128)} fusion(s32[2744]{0:T(1024)S(1)} %fusion.28, f32[32,2744]{0,1:T(8,128)S(1)} %copy.143, f32[]{:T(128)} %constant.109.clone.1), kind=kCustom, calls=%fused_computation.40 | custom fusion | flops 87808 | bytes 1732612 | tf_op jit(solution)/shard_map/scatter-add | solution.py:53
  69.7 11.3 collective-permute-start.5
  91.7 6.3 collective-permute-done.8
  115.1 10.1 collective-permute-start.12
  127.8 7.3 gather_fusion.3
  143.1 16.9 %scatter_custom_fusion.2 = f32[32,2560]{0,1:T(8,128)} fusion(s32[2744]{0:T(1024)S(1)} %fusion.28, f32[32,2744]{0,1:T(8,128)} %copy.150, f32[]{:T(128)} %constant.109.clone.1), kind=kCustom, calls=%fused_computation.38 | custom fusion | flops 87808 | bytes 678916 | tf_op jit(solution)/shard_map/scatter-add | solution.py:53
  161.0 10.0 collective-permute-start.13
  182.5 6.4 collective-permute-done.16
  207.0 9.8 collective-permute-start.20
  219.3 7.3 gather_fusion.5
  234.7 17.0 %scatter_custom_fusion.4 = f32[32,2560]{0,1:T(8,128)} fusion(s32[2744]{0:T(1024)S(1)} %fusion.28, f32[32,2744]{0,1:T(8,128)} %copy.157, f32[]{:T(128)} %constant.109.clone.1), kind=kCustom, calls=%fused_computation.36 | custom fusion | flops 87808 | bytes 678916 | tf_op jit(solution)/shard_map/scatter-add | solution.py:53
  252.6 8.9 collective-permute-start.21
  273.5 6.3 collective-permute-done.24
  296.7 9.9 collective-permute-start.28
  318.3 16.8 %scatter_custom_fusion.6 = f32[32,2560]{0,1:T(8,128)} fusion(s32[2744]{0:T(1024)S(1)} %fusion.28, f32[32,2744]{0,1:T(8,128)S(1)} %copy.164, f32[]{:T(128)} %constant.109.clone.1), kind=kCustom, calls=%fused_computation.34 | custom fusion | flops 87808 | bytes 1732612 | tf_op jit(solution)/shard_map/scatter-add | solution.py:53
  336.0 9.7 collective-permute-start.29
  358.3 6.4 collective-permute-done.32
  381.0 9.9 collective-permute-start.36
  393.5 7.3 gather_fusion.9
  408.8 16.9 %scatter_custom_fusion.8 = f32[32,2560]{0,1:T(8,128)} fusion(s32[2744]{0:T(1024)S(1)} %fusion.28, f32[32,2744]{0,1:T(8,128)} %copy.171, f32[]{:T(128)} %constant.109.clone.1), kind=kCustom, calls=%fused_computation.32 | custom fusion | flops 87808 | bytes 678916 | tf_op jit(solution)/shard_map/scatter-add | solution.py:53
  426.7 8.8 collective-permute-start.37
  472.0 10.1 collective-permute-start.44
  494.8 17.0 %scatter_custom_fusion.10 = f32[32,2560]{0,1:T(8,128)} fusion(s32[2744]{0:T(1024)S(1)} %fusion.28, f32[32,2744]{0,1:T(8,128)} %copy.178, f32[]{:T(128)} %constant.109.clone.1), kind=kCustom, calls=%fused_computation.30 | custom fusion | flops 87808 | bytes 678916 | tf_op jit(solution)/shard_map/scatter-add | solution.py:53
  512.7 9.7 collective-permute-start.45
  534.4 6.5 collective-permute-done.48
  557.9 9.8 collective-permute-start.52
  570.3 7.3 gather_fusion.13
  585.6 16.9 %scatter_custom_fusion.12 = f32[32,2560]{0,1:T(8,128)} fusion(s32[2744]{0:T(1024)S(1)} %fusion.28, f32[32,2744]{0,1:T(8,128)} %copy.185, f32[]{:T(128)} %constant.109.clone.1), kind=kCustom, calls=%fused_computation.28 | custom fusion | flops 87808 | bytes 678916 | tf_op jit(solution)/shard_map/scatter-add | solution.py:53
  603.5 9.0 collective-permute-start.53
  623.9 7.4 collective-permute-done.56
  637.9 193.7 %while.17 = (s32[]{:T(128)}, f32[32,2048]{1,0:T(8,128)S(1)}, f32[32,512]{1,0:T(8,128)S(1)}, f32[32,2048]{1,0:T(8,128)S(1)}, s32[]{:T(128)}, /*index=5*/s32[]{:T(...) while((s32[]{:T(128)}, f32[32,2048]{1,0:T(8,128)S(1)}, f32[32,512]{1,0:T(8,128)S(1)}, ...), condition=%wide.region_15.18_spmd, body=%wide.region_14.17_spmd.sunk | while | flops 25165824 | bytes 2109760 | solution.py:122
  639.8 16.8 %collective-permute-done = f32[32,2048]{1,0:T(8,128)S(1)} collective-permute-done((f32[32,2048]{1,0:T(8,128)S(1)}, f32[32,2048]{1,0:T(8,128)S(1)}, u32[]{:S(2)}, u32[]{:S(2)}) %collective-permute-start) | collective-permute-done | bytes 262176 | tf_op jit(solution)/shard_map/while/body/eval_jaxpr/ppermute | solution.py:16
  659.3 9.6 collective-permute-done
  671.6 9.1 collective-permute-done
  683.4 9.1 collective-permute-done
  695.1 9.1 collective-permute-done
  706.9 9.1 collective-permute-done
  718.8 9.1 collective-permute-done
  730.7 9.1 collective-permute-done
  742.4 9.3 collective-permute-done
  754.5 10.3 collective-permute-done
  767.6 11.4 collective-permute-done
  781.8 11.5 collective-permute-done
  796.0 10.5 collective-permute-done
  809.2 9.7 collective-permute-done
  821.7 9.1 collective-permute-done
  832.3 331.7 %all-reduce.2.cloned.1.call-done = f32[32,512]{1,0:T(8,128)} async-done(((f32[32,512]{1,0:T(8,128)}), f32[32,512]{1,0:T(8,128)}) %all-reduce.2.cloned.1.call-update) | async-done | bytes 65552 | tf_op jit(solution)/shard_map/psum | solution.py:124
  (367 shorter events, 343.3 us)
Async XLA Ops:
  7.2 1156.8 %all-reduce.2.cloned.1.call-start = ((), (), s32[]{:S(2)}) async-start(), calls=%async_computation | async-start | bytes 131072 | tf_op jit(solution)/shard_map/psum | solution.py:124
  14.4 26.5 %collective-permute-start.1 = (f32[32,128]{0,1:T(8,128)S(1)}, f32[32,128]{0,1:T(8,128)S(1)}, u32[]{:S(2)}, u32[]{:S(2)}) collective-permute-start(f32[32,128]{0,1:T(8,128)S(1)} %get-tuple-element.245), channel_id=1, source_target_pairs={{30,0},{31,1},{0,2},{1,3},{2,4},{3,5},{4,6},{5,7},{6,8},{7,9},{8,1... | collective-permute-start | bytes 49160 | tf_op jit(solution)/shard_map/ppermute | solution.py:16
  18.5 22.5 %collective-permute-start.2 = (f32[32,128]{0,1:T(8,128)S(1)}, f32[32,128]{0,1:T(8,128)S(1)}, u32[]{:S(2)}, u32[]{:S(2)}) collective-permute-start(f32[32,128]{0,1:T(8,128)S(1)} %get-tuple-element.244), channel_id=1, source_target_pairs={{31,0},{0,1},{1,2},{2,3},{3,4},{4,5},{5,6},{6,7},{7,8},{8,9},{9,10... | collective-permute-start | bytes 49160 | tf_op jit(solution)/shard_map/ppermute | solution.py:16
  22.5 18.5 %collective-permute-start.3 = (f32[32,128]{0,1:T(8,128)S(1)}, f32[32,128]{0,1:T(8,128)S(1)}, u32[]{:S(2)}, u32[]{:S(2)}) collective-permute-start(f32[32,128]{0,1:T(8,128)S(1)} %get-tuple-element.243), channel_id=1, source_target_pairs={{1,0},{2,1},{3,2},{4,3},{5,4},{6,5},{7,6},{8,7},{9,8},{10,9},{11,1... | collective-permute-start | bytes 49160 | tf_op jit(solution)/shard_map/ppermute | solution.py:16
  27.1 14.1 %collective-permute-start.4 = (f32[32,128]{0,1:T(8,128)S(1)}, f32[32,128]{0,1:T(8,128)S(1)}, u32[]{:S(2)}, u32[]{:S(2)}) collective-permute-start(f32[32,128]{0,1:T(8,128)S(1)} %get-tuple-element.242), channel_id=1, source_target_pairs={{2,0},{3,1},{4,2},{5,3},{6,4},{7,5},{8,6},{9,7},{10,8},{11,9},{12,... | collective-permute-start | bytes 49160 | tf_op jit(solution)/shard_map/ppermute | solution.py:16
  69.7 21.8 %collective-permute-start.5 = (f32[32,128]{0,1:T(8,128)S(1)}, f32[32,128]{0,1:T(8,128)S(1)}, u32[]{:S(2)}, u32[]{:S(2)}) collective-permute-start(f32[32,128]{0,1:T(8,128)S(1)} %get-tuple-element.214), channel_id=1, source_target_pairs={{2,0},{3,1},{4,2},{5,3},{6,4},{7,5},{8,6},{9,7},{10,8},{11,9},{12,... | collective-permute-start | bytes 49160 | tf_op jit(solution)/shard_map/ppermute | solution.py:16
  107.0 18.2 %collective-permute-start.9 = (f32[32,128]{0,1:T(8,128)S(1)}, f32[32,128]{0,1:T(8,128)S(1)}, u32[]{:S(2)}, u32[]{:S(2)}) collective-permute-start(f32[32,128]{0,1:T(8,128)S(1)} %get-tuple-element.241), channel_id=1, source_target_pairs={{30,0},{31,1},{0,2},{1,3},{2,4},{3,5},{4,6},{5,7},{6,8},{7,9},{8,1... | collective-permute-start | bytes 49160 | tf_op jit(solution)/shard_map/ppermute | solution.py:16
  109.1 16.8 %collective-permute-start.10 = (f32[32,128]{0,1:T(8,128)S(1)}, f32[32,128]{0,1:T(8,128)S(1)}, u32[]{:S(2)}, u32[]{:S(2)}) collective-permute-start(f32[32,128]{0,1:T(8,128)S(1)} %get-tuple-element.240), channel_id=1, source_target_pairs={{31,0},{0,1},{1,2},{2,3},{3,4},{4,5},{5,6},{6,7},{7,8},{8,9},{9,10... | collective-permute-start | bytes 49160 | tf_op jit(solution)/shard_map/ppermute | solution.py:16
  111.0 15.5 %collective-permute-start.11 = (f32[32,128]{0,1:T(8,128)S(1)}, f32[32,128]{0,1:T(8,128)S(1)}, u32[]{:S(2)}, u32[]{:S(2)}) collective-permute-start(f32[32,128]{0,1:T(8,128)S(1)} %get-tuple-element.239), channel_id=1, source_target_pairs={{1,0},{2,1},{3,2},{4,3},{5,4},{6,5},{7,6},{8,7},{9,8},{10,9},{11,1... | collective-permute-start | bytes 49160 | tf_op jit(solution)/shard_map/ppermute | solution.py:16
  115.1 12.1 %collective-permute-start.12 = (f32[32,128]{0,1:T(8,128)S(1)}, f32[32,128]{0,1:T(8,128)S(1)}, u32[]{:S(2)}, u32[]{:S(2)}) collective-permute-start(f32[32,128]{0,1:T(8,128)S(1)} %get-tuple-element.238), channel_id=1, source_target_pairs={{2,0},{3,1},{4,2},{5,3},{6,4},{7,5},{8,6},{9,7},{10,8},{11,9},{12,... | collective-permute-start | bytes 49160 | tf_op jit(solution)/shard_map/ppermute | solution.py:16
  161.0 21.3 %collective-permute-start.13 = (f32[32,128]{0,1:T(8,128)S(1)}, f32[32,128]{0,1:T(8,128)S(1)}, u32[]{:S(2)}, u32[]{:S(2)}) collective-permute-start(f32[32,128]{0,1:T(8,128)S(1)} %get-tuple-element.210), channel_id=1, source_target_pairs={{2,0},{3,1},{4,2},{5,3},{6,4},{7,5},{8,6},{9,7},{10,8},{11,9},{12,... | collective-permute-start | bytes 49160 | tf_op jit(solution)/shard_map/ppermute | solution.py:16
  171.1 11.3 collective-permute-start.14
  199.5 17.3 %collective-permute-start.17 = (f32[32,128]{0,1:T(8,128)S(1)}, f32[32,128]{0,1:T(8,128)S(1)}, u32[]{:S(2)}, u32[]{:S(2)}) collective-permute-start(f32[32,128]{0,1:T(8,128)S(1)} %get-tuple-element.237), channel_id=1, source_target_pairs={{30,0},{31,1},{0,2},{1,3},{2,4},{3,5},{4,6},{5,7},{6,8},{7,9},{8,1... | collective-permute-start | bytes 49160 | tf_op jit(solution)/shard_map/ppermute | solution.py:16
  201.5 15.9 %collective-permute-start.18 = (f32[32,128]{0,1:T(8,128)S(1)}, f32[32,128]{0,1:T(8,128)S(1)}, u32[]{:S(2)}, u32[]{:S(2)}) collective-permute-start(f32[32,128]{0,1:T(8,128)S(1)} %get-tuple-element.236), channel_id=1, source_target_pairs={{31,0},{0,1},{1,2},{2,3},{3,4},{4,5},{5,6},{6,7},{7,8},{8,9},{9,10... | collective-permute-start | bytes 49160 | tf_op jit(solution)/shard_map/ppermute | solution.py:16
  203.4 14.6 %collective-permute-start.19 = (f32[32,128]{0,1:T(8,128)S(1)}, f32[32,128]{0,1:T(8,128)S(1)}, u32[]{:S(2)}, u32[]{:S(2)}) collective-permute-start(f32[32,128]{0,1:T(8,128)S(1)} %get-tuple-element.235), channel_id=1, source_target_pairs={{1,0},{2,1},{3,2},{4,3},{5,4},{6,5},{7,6},{8,7},{9,8},{10,9},{11,1... | collective-permute-start | bytes 49160 | tf_op jit(solution)/shard_map/ppermute | solution.py:16
  207.0 11.8 %collective-permute-start.20 = (f32[32,128]{0,1:T(8,128)S(1)}, f32[32,128]{0,1:T(8,128)S(1)}, u32[]{:S(2)}, u32[]{:S(2)}) collective-permute-start(f32[32,128]{0,1:T(8,128)S(1)} %get-tuple-element.234), channel_id=1, source_target_pairs={{2,0},{3,1},{4,2},{5,3},{6,4},{7,5},{8,6},{9,7},{10,8},{11,9},{12,... | collective-permute-start | bytes 49160 | tf_op jit(solution)/shard_map/ppermute | solution.py:16
  252.6 20.7 %collective-permute-start.21 = (f32[32,128]{0,1:T(8,128)S(1)}, f32[32,128]{0,1:T(8,128)S(1)}, u32[]{:S(2)}, u32[]{:S(2)}) collective-permute-start(f32[32,128]{0,1:T(8,128)S(1)} %get-tuple-element.206), channel_id=1, source_target_pairs={{2,0},{3,1},{4,2},{5,3},{6,4},{7,5},{8,6},{9,7},{10,8},{11,9},{12,... | collective-permute-start | bytes 49160 | tf_op jit(solution)/shard_map/ppermute | solution.py:16
  261.6 11.8 %collective-permute-start.22 = (f32[32,128]{0,1:T(8,128)S(1)}, f32[32,128]{0,1:T(8,128)S(1)}, u32[]{:S(2)}, u32[]{:S(2)}) collective-permute-start(f32[32,128]{0,1:T(8,128)S(1)} %get-tuple-element.209), channel_id=1, source_target_pairs={{1,0},{2,1},{3,2},{4,3},{5,4},{6,5},{7,6},{8,7},{9,8},{10,9},{11,1... | collective-permute-start | bytes 49160 | tf_op jit(solution)/shard_map/ppermute | solution.py:16
  289.3 17.3 %collective-permute-start.25 = (f32[32,128]{0,1:T(8,128)S(1)}, f32[32,128]{0,1:T(8,128)S(1)}, u32[]{:S(2)}, u32[]{:S(2)}) collective-permute-start(f32[32,128]{0,1:T(8,128)S(1)} %get-tuple-element.233), channel_id=1, source_target_pairs={{30,0},{31,1},{0,2},{1,3},{2,4},{3,5},{4,6},{5,7},{6,8},{7,9},{8,1... | collective-permute-start | bytes 49160 | tf_op jit(solution)/shard_map/ppermute | solution.py:16
  291.2 15.4 %collective-permute-start.26 = (f32[32,128]{0,1:T(8,128)S(1)}, f32[32,128]{0,1:T(8,128)S(1)}, u32[]{:S(2)}, u32[]{:S(2)}) collective-permute-start(f32[32,128]{0,1:T(8,128)S(1)} %get-tuple-element.232), channel_id=1, source_target_pairs={{31,0},{0,1},{1,2},{2,3},{3,4},{4,5},{5,6},{6,7},{7,8},{8,9},{9,10... | collective-permute-start | bytes 49160 | tf_op jit(solution)/shard_map/ppermute | solution.py:16
  293.1 13.5 %collective-permute-start.27 = (f32[32,128]{0,1:T(8,128)S(1)}, f32[32,128]{0,1:T(8,128)S(1)}, u32[]{:S(2)}, u32[]{:S(2)}) collective-permute-start(f32[32,128]{0,1:T(8,128)S(1)} %get-tuple-element.231), channel_id=1, source_target_pairs={{1,0},{2,1},{3,2},{4,3},{5,4},{6,5},{7,6},{8,7},{9,8},{10,9},{11,1... | collective-permute-start | bytes 49160 | tf_op jit(solution)/shard_map/ppermute | solution.py:16
  336.0 22.0 %collective-permute-start.29 = (f32[32,128]{0,1:T(8,128)S(1)}, f32[32,128]{0,1:T(8,128)S(1)}, u32[]{:S(2)}, u32[]{:S(2)}) collective-permute-start(f32[32,128]{0,1:T(8,128)S(1)} %get-tuple-element.202), channel_id=1, source_target_pairs={{2,0},{3,1},{4,2},{5,3},{6,4},{7,5},{8,6},{9,7},{10,8},{11,9},{12,... | collective-permute-start | bytes 49160 | tf_op jit(solution)/shard_map/ppermute | solution.py:16
  345.8 12.4 %collective-permute-start.30 = (f32[32,128]{0,1:T(8,128)S(1)}, f32[32,128]{0,1:T(8,128)S(1)}, u32[]{:S(2)}, u32[]{:S(2)}) collective-permute-start(f32[32,128]{0,1:T(8,128)S(1)} %get-tuple-element.205), channel_id=1, source_target_pairs={{1,0},{2,1},{3,2},{4,3},{5,4},{6,5},{7,6},{8,7},{9,8},{10,9},{11,1... | collective-permute-start | bytes 49160 | tf_op jit(solution)/shard_map/ppermute | solution.py:16
  373.7 17.2 %collective-permute-start.33 = (f32[32,128]{0,1:T(8,128)S(1)}, f32[32,128]{0,1:T(8,128)S(1)}, u32[]{:S(2)}, u32[]{:S(2)}) collective-permute-start(f32[32,128]{0,1:T(8,128)S(1)} %get-tuple-element.229), channel_id=1, source_target_pairs={{30,0},{31,1},{0,2},{1,3},{2,4},{3,5},{4,6},{5,7},{6,8},{7,9},{8,1... | collective-permute-start | bytes 49160 | tf_op jit(solution)/shard_map/ppermute | solution.py:16
  375.6 16.0 %collective-permute-start.34 = (f32[32,128]{0,1:T(8,128)S(1)}, f32[32,128]{0,1:T(8,128)S(1)}, u32[]{:S(2)}, u32[]{:S(2)}) collective-permute-start(f32[32,128]{0,1:T(8,128)S(1)} %get-tuple-element.228), channel_id=1, source_target_pairs={{31,0},{0,1},{1,2},{2,3},{3,4},{4,5},{5,6},{6,7},{7,8},{8,9},{9,10... | collective-permute-start | bytes 49160 | tf_op jit(solution)/shard_map/ppermute | solution.py:16
  377.5 14.7 %collective-permute-start.35 = (f32[32,128]{0,1:T(8,128)S(1)}, f32[32,128]{0,1:T(8,128)S(1)}, u32[]{:S(2)}, u32[]{:S(2)}) collective-permute-start(f32[32,128]{0,1:T(8,128)S(1)} %get-tuple-element.227), channel_id=1, source_target_pairs={{1,0},{2,1},{3,2},{4,3},{5,4},{6,5},{7,6},{8,7},{9,8},{10,9},{11,1... | collective-permute-start | bytes 49160 | tf_op jit(solution)/shard_map/ppermute | solution.py:16
  381.0 11.8 %collective-permute-start.36 = (f32[32,128]{0,1:T(8,128)S(1)}, f32[32,128]{0,1:T(8,128)S(1)}, u32[]{:S(2)}, u32[]{:S(2)}) collective-permute-start(f32[32,128]{0,1:T(8,128)S(1)} %get-tuple-element.226), channel_id=1, source_target_pairs={{2,0},{3,1},{4,2},{5,3},{6,4},{7,5},{8,6},{9,7},{10,8},{11,9},{12,... | collective-permute-start | bytes 49160 | tf_op jit(solution)/shard_map/ppermute | solution.py:16
  426.7 20.6 %collective-permute-start.37 = (f32[32,128]{0,1:T(8,128)S(1)}, f32[32,128]{0,1:T(8,128)S(1)}, u32[]{:S(2)}, u32[]{:S(2)}) collective-permute-start(f32[32,128]{0,1:T(8,128)S(1)} %get-tuple-element.198), channel_id=1, source_target_pairs={{2,0},{3,1},{4,2},{5,3},{6,4},{7,5},{8,6},{9,7},{10,8},{11,9},{12,... | collective-permute-start | bytes 49160 | tf_op jit(solution)/shard_map/ppermute | solution.py:16
  435.5 11.8 %collective-permute-start.38 = (f32[32,128]{0,1:T(8,128)S(1)}, f32[32,128]{0,1:T(8,128)S(1)}, u32[]{:S(2)}, u32[]{:S(2)}) collective-permute-start(f32[32,128]{0,1:T(8,128)S(1)} %get-tuple-element.201), channel_id=1, source_target_pairs={{1,0},{2,1},{3,2},{4,3},{5,4},{6,5},{7,6},{8,7},{9,8},{10,9},{11,1... | collective-permute-start | bytes 49160 | tf_op jit(solution)/shard_map/ppermute | solution.py:16
  464.5 17.6 %collective-permute-start.41 = (f32[32,128]{0,1:T(8,128)S(1)}, f32[32,128]{0,1:T(8,128)S(1)}, u32[]{:S(2)}, u32[]{:S(2)}) collective-permute-start(f32[32,128]{0,1:T(8,128)S(1)} %get-tuple-element.225), channel_id=1, source_target_pairs={{30,0},{31,1},{0,2},{1,3},{2,4},{3,5},{4,6},{5,7},{6,8},{7,9},{8,1... | collective-permute-start | bytes 49160 | tf_op jit(solution)/shard_map/ppermute | solution.py:16
  466.5 15.7 %collective-permute-start.42 = (f32[32,128]{0,1:T(8,128)S(1)}, f32[32,128]{0,1:T(8,128)S(1)}, u32[]{:S(2)}, u32[]{:S(2)}) collective-permute-start(f32[32,128]{0,1:T(8,128)S(1)} %get-tuple-element.224), channel_id=1, source_target_pairs={{31,0},{0,1},{1,2},{2,3},{3,4},{4,5},{5,6},{6,7},{7,8},{8,9},{9,10... | collective-permute-start | bytes 49160 | tf_op jit(solution)/shard_map/ppermute | solution.py:16
  468.4 13.8 %collective-permute-start.43 = (f32[32,128]{0,1:T(8,128)S(1)}, f32[32,128]{0,1:T(8,128)S(1)}, u32[]{:S(2)}, u32[]{:S(2)}) collective-permute-start(f32[32,128]{0,1:T(8,128)S(1)} %get-tuple-element.223), channel_id=1, source_target_pairs={{1,0},{2,1},{3,2},{4,3},{5,4},{6,5},{7,6},{8,7},{9,8},{10,9},{11,1... | collective-permute-start | bytes 49160 | tf_op jit(solution)/shard_map/ppermute | solution.py:16
  512.7 21.5 %collective-permute-start.45 = (f32[32,128]{0,1:T(8,128)S(1)}, f32[32,128]{0,1:T(8,128)S(1)}, u32[]{:S(2)}, u32[]{:S(2)}) collective-permute-start(f32[32,128]{0,1:T(8,128)S(1)} %get-tuple-element.194), channel_id=1, source_target_pairs={{2,0},{3,1},{4,2},{5,3},{6,4},{7,5},{8,6},{9,7},{10,8},{11,9},{12,... | collective-permute-start | bytes 49160 | tf_op jit(solution)/shard_map/ppermute | solution.py:16
  522.4 11.8 %collective-permute-start.46 = (f32[32,128]{0,1:T(8,128)S(1)}, f32[32,128]{0,1:T(8,128)S(1)}, u32[]{:S(2)}, u32[]{:S(2)}) collective-permute-start(f32[32,128]{0,1:T(8,128)S(1)} %get-tuple-element.197), channel_id=1, source_target_pairs={{1,0},{2,1},{3,2},{4,3},{5,4},{6,5},{7,6},{8,7},{9,8},{10,9},{11,1... | collective-permute-start | bytes 49160 | tf_op jit(solution)/shard_map/ppermute | solution.py:16
  550.3 17.4 %collective-permute-start.49 = (f32[32,128]{0,1:T(8,128)S(1)}, f32[32,128]{0,1:T(8,128)S(1)}, u32[]{:S(2)}, u32[]{:S(2)}) collective-permute-start(f32[32,128]{0,1:T(8,128)S(1)} %get-tuple-element.221), channel_id=1, source_target_pairs={{30,0},{31,1},{0,2},{1,3},{2,4},{3,5},{4,6},{5,7},{6,8},{7,9},{8,1... | collective-permute-start | bytes 49160 | tf_op jit(solution)/shard_map/ppermute | solution.py:16
  552.5 15.8 %collective-permute-start.50 = (f32[32,128]{0,1:T(8,128)S(1)}, f32[32,128]{0,1:T(8,128)S(1)}, u32[]{:S(2)}, u32[]{:S(2)}) collective-permute-start(f32[32,128]{0,1:T(8,128)S(1)} %get-tuple-element.220), channel_id=1, source_target_pairs={{31,0},{0,1},{1,2},{2,3},{3,4},{4,5},{5,6},{6,7},{7,8},{8,9},{9,10... | collective-permute-start | bytes 49160 | tf_op jit(solution)/shard_map/ppermute | solution.py:16
  554.5 14.5 %collective-permute-start.51 = (f32[32,128]{0,1:T(8,128)S(1)}, f32[32,128]{0,1:T(8,128)S(1)}, u32[]{:S(2)}, u32[]{:S(2)}) collective-permute-start(f32[32,128]{0,1:T(8,128)S(1)} %get-tuple-element.219), channel_id=1, source_target_pairs={{1,0},{2,1},{3,2},{4,3},{5,4},{6,5},{7,6},{8,7},{9,8},{10,9},{11,1... | collective-permute-start | bytes 49160 | tf_op jit(solution)/shard_map/ppermute | solution.py:16
  557.9 11.8 %collective-permute-start.52 = (f32[32,128]{0,1:T(8,128)S(1)}, f32[32,128]{0,1:T(8,128)S(1)}, u32[]{:S(2)}, u32[]{:S(2)}) collective-permute-start(f32[32,128]{0,1:T(8,128)S(1)} %get-tuple-element.218), channel_id=1, source_target_pairs={{2,0},{3,1},{4,2},{5,3},{6,4},{7,5},{8,6},{9,7},{10,8},{11,9},{12,... | collective-permute-start | bytes 49160 | tf_op jit(solution)/shard_map/ppermute | solution.py:16
  603.5 20.3 %collective-permute-start.53 = (f32[32,128]{0,1:T(8,128)S(1)}, f32[32,128]{0,1:T(8,128)S(1)}, u32[]{:S(2)}, u32[]{:S(2)}) collective-permute-start(f32[32,128]{0,1:T(8,128)S(1)} %get-tuple-element.190), channel_id=1, source_target_pairs={{2,0},{3,1},{4,2},{5,3},{6,4},{7,5},{8,6},{9,7},{10,8},{11,9},{12,... | collective-permute-start | bytes 49160 | tf_op jit(solution)/shard_map/ppermute | solution.py:16
  612.5 11.3 collective-permute-start.54
  637.9 18.7 %collective-permute-start = (f32[32,2048]{1,0:T(8,128)S(1)}, f32[32,2048]{1,0:T(8,128)S(1)}, u32[]{:S(2)}, u32[]{:S(2)}) collective-permute-start(f32[32,2048]{1,0:T(8,128)S(1)} %get-tuple-element.292), channel_id=1, source_target_pairs={{480,0},{0,32},{32,64},{64,96},{96,128},{128,160},{160,192},{192,2... | collective-permute-start | bytes 786440 | tf_op jit(solution)/shard_map/while/body/eval_jaxpr/ppermute | solution.py:16
  657.4 11.5 collective-permute-start
  740.5 11.3 collective-permute-start
  752.6 12.2 %collective-permute-start = (f32[32,2048]{1,0:T(8,128)S(1)}, f32[32,2048]{1,0:T(8,128)S(1)}, u32[]{:S(2)}, u32[]{:S(2)}) collective-permute-start(f32[32,2048]{1,0:T(8,128)S(1)} %get-tuple-element.292), channel_id=1, source_target_pairs={{480,0},{0,32},{32,64},{64,96},{96,128},{128,160},{160,192},{192,2... | collective-permute-start | bytes 786440 | tf_op jit(solution)/shard_map/while/body/eval_jaxpr/ppermute | solution.py:16
  765.7 13.3 %collective-permute-start = (f32[32,2048]{1,0:T(8,128)S(1)}, f32[32,2048]{1,0:T(8,128)S(1)}, u32[]{:S(2)}, u32[]{:S(2)}) collective-permute-start(f32[32,2048]{1,0:T(8,128)S(1)} %get-tuple-element.292), channel_id=1, source_target_pairs={{480,0},{0,32},{32,64},{64,96},{96,128},{128,160},{160,192},{192,2... | collective-permute-start | bytes 786440 | tf_op jit(solution)/shard_map/while/body/eval_jaxpr/ppermute | solution.py:16
  779.8 13.5 %collective-permute-start = (f32[32,2048]{1,0:T(8,128)S(1)}, f32[32,2048]{1,0:T(8,128)S(1)}, u32[]{:S(2)}, u32[]{:S(2)}) collective-permute-start(f32[32,2048]{1,0:T(8,128)S(1)} %get-tuple-element.292), channel_id=1, source_target_pairs={{480,0},{0,32},{32,64},{64,96},{96,128},{128,160},{160,192},{192,2... | collective-permute-start | bytes 786440 | tf_op jit(solution)/shard_map/while/body/eval_jaxpr/ppermute | solution.py:16
  794.0 12.4 %collective-permute-start = (f32[32,2048]{1,0:T(8,128)S(1)}, f32[32,2048]{1,0:T(8,128)S(1)}, u32[]{:S(2)}, u32[]{:S(2)}) collective-permute-start(f32[32,2048]{1,0:T(8,128)S(1)} %get-tuple-element.292), channel_id=1, source_target_pairs={{480,0},{0,32},{32,64},{64,96},{96,128},{128,160},{160,192},{192,2... | collective-permute-start | bytes 786440 | tf_op jit(solution)/shard_map/while/body/eval_jaxpr/ppermute | solution.py:16
  807.3 11.6 collective-permute-start
  (39 other events, 603.5 us)
Sparse Core Ops, SparseCore 0:
  832.4 331.5 all-reduce.1
where the time goes:
time: 1190 us; the launch traced here: 1170 us
  waiting for transfers between devices  532 us (45%)
  starting transfers between devices  286 us (24%)
  other arithmetic  213 us (18%)
  local copies, waits for them, and re-layouts  107 us (9%)
  between operations  19.8 us (2%)
  matrix products  12.8 us (1%)
    psum x1, waiting for transfers between devices, body(): hproj = lax.psum(partial_rows, 'mesh') / node_total  332 us
    ppermute x71, starting transfers between devices, passed_along(): return lax.ppermute(block, axis, route)  286 us
    ppermute x71, waiting for transfers between devices, passed_along(): return lax.ppermute(block, axis, route)  200 us
    scatter-add x7, other arithmetic, apply_operator(): sums = jnp.zeros((band_count, node_width + 4 * slot_count), jnp.float32)....  118 us
    gather x7, local copies, waits for them, and re-layouts, apply_operator(): jnp.take(extended, flat_index, axis=1)  46.9 us
    scatter-add x7, other arithmetic, apply_operator(): own_sums = sums[:, :node_width].at[:, send_rows].add(arrived)  34.9 us
  transfers between devices with their start and end apart: 72, of which 26 were waited for; matrix products, arithmetic and copies ran while one was open for 2% of the time, Pallas kernels for 0%

commit v1 on v0

v1 whole, which is shorter than its diff:
```python
import jax
import jax.numpy as jnp
from jax import lax
from jax.experimental import pallas as pl
from jax.experimental.pallas import tpu as pltpu
from jax.sharding import PartitionSpec as P

DEGREE = 3
OFFSETS = (-2, -1, 1, 2)
HIGHEST = lax.Precision.HIGHEST

PARTS = 32
GROUPS = PARTS // 8
NODES = 2048
SLOTS = 128
GHOSTS = 4 * SLOTS
EXT = GHOSTS + NODES
CELLS = 8
NPC = 343
NPC_PAD = 384
CELL_CHUNKS = NPC_PAD // 128
ENTRIES = CELLS * NPC + GHOSTS
ENTRY_CHUNKS = 26
ENTRY_PAD = ENTRY_CHUNKS * 128
PAD_KEY = 4000

IDX_AT = 0
POS_AT = IDX_AT + CELLS * CELL_CHUNKS
KEY_AT = POS_AT + ENTRY_CHUNKS
END_AT = KEY_AT + ENTRY_CHUNKS
SEND_AT = END_AT + EXT // 128
POT_AT = SEND_AT + GHOSTS // 128
MISC_AT = POT_AT + NODES // 128
TABLE_CHUNKS = MISC_AT + 1


def groups_of(size, bits):
    mask = sum(bits)
    members = {}
    for i in range(size):
        members.setdefault(i & ~mask, []).append(i)
    return list(members.values())


def spread(block, axis, size, bits):
    members = groups_of(size, bits)
    copies = jnp.broadcast_to(block[None], (len(members[0]),) + block.shape)
    return lax.all_to_all(copies, axis, 0, 0, axis_index_groups=members)


def partition_table(cell_nodes, send_list, potential, cell_scale, node_count):
    shifted = jnp.where(cell_nodes >= NODES, cell_nodes - NODES, cell_nodes + GHOSTS)
    slots = jnp.pad(shifted, ((0, 0), (0, NPC_PAD - NPC))).reshape(-1)
    send = send_list.reshape(-1)
    keys = jnp.concatenate([shifted.reshape(-1), send + GHOSTS])
    tagged = keys * 4096 + lax.iota(jnp.int32, ENTRIES)
    ordered = lax.sort(tagged)
    entry = ordered & 4095
    sorted_key = ordered >> 12
    from_slot = (entry // NPC) * NPC_PAD + entry % NPC
    position = jnp.where(entry < CELLS * NPC, from_slot, entry + (CELLS * NPC_PAD - CELLS * NPC))
    position = jnp.pad(position, (0, ENTRY_PAD - ENTRIES))
    sorted_key = jnp.pad(sorted_key, (0, ENTRY_PAD - ENTRIES), constant_values=PAD_KEY)
    nodes = lax.iota(jnp.int32, EXT)
    up_to = jnp.sum((keys[None, :] <= nodes[:, None]).astype(jnp.int32), axis=1)
    before = jnp.concatenate([jnp.zeros((1,), jnp.int32), up_to[:-1]])
    end = jnp.where(up_to > before, up_to - 1, -1)
    misc = jnp.concatenate([cell_scale, node_count.astype(jnp.float32), jnp.zeros((119,), jnp.float32)])
    ints = jnp.concatenate([slots, position, sorted_key, end, send]).astype(jnp.float32)
    return jnp.concatenate([ints, potential, misc]).reshape(TABLE_CHUNKS, 128)


def chunk(c):
    return pl.ds(c * 128, 128)


def rows(g):
    return pl.ds(pl.multiple_of(g * 8, 8), 8)


def picked(sources, index):
    low = index & 127
    high = index >> 7
    total = jnp.zeros((8, 128), jnp.float32)
    for j, source in enumerate(sources):
        total = jnp.where(high == j, jnp.take_along_axis(source, low, axis=1), total)
    return total


def filter_kernel(
    coef, table, start, matrix, f_ref, g_ref,
    mat_hi, mat_lo, idx, pos, off, cont, end, send, scale, cur, prev, ext, vals, prod, arrived, w, halo, sums,
):
    lane = lax.broadcasted_iota(jnp.int32, (8, 128), 1)

    for k in range(CELL_CHUNKS):
        whole = matrix[k * 128 : (k + 1) * 128, :]
        high_part = whole.astype(jnp.bfloat16)
        low_part = (whole - high_part.astype(jnp.float32)).astype(jnp.bfloat16)
        mat_hi[k * 128 : (k + 1) * 128, :] = high_part
        mat_lo[k * 128 : (k + 1) * 128, :] = low_part

    def to_int(dest, first, count):
        def at(c, _):
            src = pl.ds(pl.multiple_of((first + c) * 128, 128), 128)
            dst = pl.ds(pl.multiple_of(c * 128, 128), 128)
            dest[:, dst] = table[:, src].astype(jnp.int32)
            return 0

        lax.fori_loop(0, count, at, 0)

    to_int(idx, IDX_AT, CELLS * CELL_CHUNKS)
    to_int(pos, POS_AT, ENTRY_CHUNKS)
    to_int(end, END_AT, EXT // 128)
    to_int(send, SEND_AT, GHOSTS // 128)
    for c in range(CELLS):
        column = table[:, MISC_AT * 128 + c : MISC_AT * 128 + c + 1]
        scale[c * 32 : (c + 1) * 32, :] = jnp.broadcast_to(column, (PARTS, 128))

    def run_of(q, _):
        here = pl.ds(pl.multiple_of((KEY_AT + q) * 128, 128), 128)
        back = pl.ds(pl.multiple_of((KEY_AT + jnp.maximum(q - 1, 0)) * 128, 128), 128)
        dst = pl.ds(pl.multiple_of(q * 128, 128), 128)
        for g in range(GROUPS):
            r = pl.ds(g * 8, 8)
            key = table[r, here]
            count = jnp.ones((8, 128), jnp.float32)
            for d in (1, 2, 4, 8, 16, 32, 64):
                same = (pltpu.roll(key, d, 1) == key) & (lane >= d)
                count = count + jnp.where(same, pltpu.roll(count, d, 1), 0.0)
            place = count.astype(jnp.int32) - 1
            off[r, dst] = place
            last = jnp.broadcast_to(table[r, back][:, 127:128], (8, 128))
            goes_on = (last == key) & (q > 0)
            cont[r, dst] = jnp.where(goes_on, 1.0, 0.0)
        return 0

    lax.fori_loop(0, ENTRY_CHUNKS, run_of, 0)
    keys = table[:, KEY_AT * 128 : (KEY_AT + ENTRY_CHUNKS) * 128]
    ghost_entries = jnp.sum(jnp.where(keys < GHOSTS, 1.0, 0.0), axis=1, keepdims=True)
    most = jnp.max(ghost_entries).astype(jnp.int32)
    least = jnp.min(ghost_entries).astype(jnp.int32)
    ghost_stop = (most + 127) // 128
    own_start = least // 128

    live = table[:, MISC_AT * 128 + 8 : MISC_AT * 128 + 9].astype(jnp.int32)
    node = lax.broadcasted_iota(jnp.int32, (PARTS, NODES), 1)
    cur[...] = jnp.where(node < live, start[...], 0.0)
    prev[...] = jnp.zeros((PARTS, NODES), jnp.float32)

    def wrap(values, k):
        c = chunk(k)
        halo[2:34, c] = values
        halo[0:2, c] = values[30:32]
        halo[34:36, c] = values[0:2]

    def into_order(first, stop, with_arrived):
        def group(g, _):
            r = rows(g)
            sources = [
                prod[pl.ds(pl.multiple_of(c * 32 + g * 8, 8), 8), chunk(k)]
                for c in range(CELLS)
                for k in range(CELL_CHUNKS)
            ]
            if with_arrived:
                sources += [arrived[r, chunk(k)] for k in range(4)]

            def at(q, _):
                here = pl.ds(pl.multiple_of(q * 128, 128), 128)
                w[r, here] = picked(sources, pos[r, here])
                return 0

            lax.fori_loop(first, stop, at, 0)
            return 0

        lax.fori_loop(0, GROUPS, group, 0)

        def along(q, carry):
            here = pl.ds(pl.multiple_of(q * 128, 128), 128)
            left = []
            for g in range(GROUPS):
                r = pl.ds(g * 8, 8)
                x = w[r, here]
                place = off[r, here]
                for d in (1, 2, 4, 8, 16, 32, 64):
                    x = x + jnp.where(place >= d, pltpu.roll(x, d, 1), 0.0)
                x = x + cont[r, here] * carry[g]
                w[r, here] = x
                left.append(jnp.broadcast_to(x[:, 127:128], (8, 128)))
            return tuple(left)

        none = jnp.zeros((8, 128), jnp.float32)
        lax.fori_loop(first, stop, along, (none,) * GROUPS)

    def run_ends(first, stop, node_first, node_count, dest):
        def group(g, _):
            r = rows(g)
            index = [end[r, chunk(node_first + n)] for n in range(node_count)]

            def at(q, totals):
                source = w[r, pl.ds(pl.multiple_of(q * 128, 128), 128)]
                return tuple(
                    jnp.where((i >> 7) == q, jnp.take_along_axis(source, i & 127, axis=1), t)
                    for i, t in zip(index, totals)
                )

            none = jnp.zeros((8, 128), jnp.float32)
            totals = lax.fori_loop(first, stop, at, (none,) * node_count)
            for n in range(node_count):
                dest[r, chunk(n)] = totals[n]
            return 0

        lax.fori_loop(0, GROUPS, group, 0)

    def step(i, _):
        def outgoing(g, _):
            r = rows(g)
            sources = [cur[r, chunk(j)] for j in range(NODES // 128)]
            for k in range(4):
                sums[r, chunk(k)] = picked(sources, send[r, chunk(k)])
            return 0

        lax.fori_loop(0, GROUPS, outgoing, 0)
        for k in range(4):
            wrap(sums[:, k * 128 : (k + 1) * 128], k)
        for k, o in enumerate(OFFSETS):
            ext[:, k * 128 : (k + 1) * 128] = halo[2 + o : 34 + o, k * 128 : (k + 1) * 128]
        ext[:, GHOSTS:] = cur[...]

        def gather(g, _):
            r = rows(g)
            sources = [ext[r, chunk(j)] for j in range(EXT // 128)]

            def cell(c, _):
                for k in range(CELL_CHUNKS):
                    here = pl.ds(pl.multiple_of(c * NPC_PAD + k * 128, 128), 128)
                    there = pl.ds(pl.multiple_of(c * 32 + g * 8, 8), 8)
                    vals[there, chunk(k)] = picked(sources, idx[r, here])
                return 0

            lax.fori_loop(0, CELLS, cell, 0)
            return 0

        lax.fori_loop(0, GROUPS, gather, 0)

        x = vals[...]
        high = x.astype(jnp.bfloat16)
        low = (x - high.astype(jnp.float32)).astype(jnp.bfloat16)

        def dot(a, b):
            return jnp.dot(a, b, preferred_element_type=jnp.float32)

        y = dot(high, mat_hi[...]) + (dot(low, mat_hi[...]) + dot(high, mat_lo[...]))
        for k in range(CELL_CHUNKS):
            prod[:, k * 128 : (k + 1) * 128] = y[:, k * 128 : (k + 1) * 128] * scale[...]

        into_order(0, ghost_stop, False)
        run_ends(0, ghost_stop, 0, 4, sums)
        for k in range(4):
            wrap(sums[:, k * 128 : (k + 1) * 128], k)
        for k, o in enumerate(OFFSETS):
            arrived[:, k * 128 : (k + 1) * 128] = halo[2 - o : 34 - o, k * 128 : (k + 1) * 128]

        into_order(own_start, ENTRY_CHUNKS, True)
        run_ends(own_start, ENTRY_CHUNKS, 4, 16, sums)

        degree = lax.rem(i, DEGREE)
        gain = coef[degree]
        back = coef[DEGREE + degree]
        centre = coef[2 * DEGREE]

        def blend(c, _):
            here = pl.ds(pl.multiple_of(c * 128, 128), 128)
            v = cur[:, here]
            pot = table[:, pl.ds(pl.multiple_of((POT_AT + c) * 128, 128), 128)]
            hv = sums[:, here] + pot * v
            before = prev[:, here]
            following = gain * (hv - centre * v)
            following = jnp.where(degree == 0, following, following - back * before)
            g_ref[:, here] = hv
            f_ref[:, here] = v
            prev[:, here] = v
            cur[:, here] = following
            return 0

        lax.fori_loop(0, NODES // 128, blend, 0)
        return 0

    lax.fori_loop(0, 2 * DEGREE + 1, step, 0)


def run_filter(coef, table, start, cell_matrix):
    padded = jnp.pad(cell_matrix, ((0, NPC_PAD - NPC), (0, NPC_PAD - NPC)))
    out = jax.ShapeDtypeStruct((PARTS, NODES), jnp.float32)
    vmem = pl.BlockSpec(memory_space=pltpu.VMEM)
    f32, i32 = jnp.float32, jnp.int32
    cells = CELLS * PARTS
    return pl.pallas_call(
        filter_kernel,
        out_shape=(out, out),
        in_specs=[pl.BlockSpec(memory_space=pltpu.SMEM)] + [vmem] * 3,
        out_specs=(vmem, vmem),
        scratch_shapes=[
            pltpu.VMEM((NPC_PAD, NPC_PAD), jnp.bfloat16),
            pltpu.VMEM((NPC_PAD, NPC_PAD), jnp.bfloat16),
            pltpu.VMEM((PARTS, CELLS * NPC_PAD), i32),
            pltpu.VMEM((PARTS, ENTRY_PAD), i32),
            pltpu.VMEM((PARTS, ENTRY_PAD), i32),
            pltpu.VMEM((PARTS, ENTRY_PAD), f32),
            pltpu.VMEM((PARTS, EXT), i32),
            pltpu.VMEM((PARTS, GHOSTS), i32),
            pltpu.VMEM((cells, 128), f32),
            pltpu.VMEM((PARTS, NODES), f32),
            pltpu.VMEM((PARTS, NODES), f32),
            pltpu.VMEM((PARTS, EXT), f32),
            pltpu.VMEM((cells, NPC_PAD), f32),
            pltpu.VMEM((cells, NPC_PAD), f32),
            pltpu.VMEM((PARTS, GHOSTS), f32),
            pltpu.VMEM((PARTS, ENTRY_PAD), f32),
            pltpu.VMEM((40, GHOSTS), f32),
            pltpu.VMEM((PARTS, NODES), f32),
        ],
        compiler_params=pltpu.CompilerParams(vmem_limit_bytes=48 * 1024 * 1024),
    )(coef, table, start, padded)


def coefficients(filter_bounds):
    lowest, wanted_top, upper = filter_bounds[0], filter_bounds[1], filter_bounds[2]
    half_width = (upper - wanted_top) / 2.0
    centre = (upper + wanted_top) / 2.0
    sigma = half_width / (lowest - centre)
    ratio = 2.0 / sigma
    gains, backs = [sigma / half_width], [jnp.zeros_like(sigma)]
    for _ in range(DEGREE - 1):
        following = 1.0 / (ratio - sigma)
        gains.append(2.0 * following / half_width)
        backs.append(sigma * following)
        sigma = following
    return jnp.stack(gains + backs + [centre, centre])


def body(vectors, potential, cell_scale, cell_matrix, cell_nodes, send_list, node_count, filter_bounds):
    own_table = partition_table(cell_nodes, send_list[0], potential, cell_scale, node_count)
    table = spread(own_table, "mesh", PARTS, (8, 16))
    table = spread(table, "mesh", PARTS, (2, 4))
    table = spread(table, "mesh", PARTS, (1,))
    table = table.transpose(2, 1, 0, 3, 4).reshape(PARTS, TABLE_CHUNKS * 128)

    start = lax.all_to_all(vectors, "mesh", 0, 0, tiled=True)
    f, g = run_filter(coefficients(filter_bounds), table, start, cell_matrix)
    filtered = lax.all_to_all(f, "mesh", 0, 0, tiled=True)
    applied = lax.all_to_all(g, "mesh", 0, 0, tiled=True)

    band_rows = filtered.shape[0]
    z_lo = groups_of(16, (1, 2))
    both = jnp.stack([filtered, applied]).reshape(2, band_rows, 4, NODES // 4)
    both = lax.all_to_all(both.transpose(2, 0, 1, 3), "band", 0, 0, axis_index_groups=z_lo)
    right = both[:, 0].reshape(4 * band_rows, NODES // 4)
    left = both[:, 1].reshape(4 * band_rows, NODES // 4)
    right = spread(right, "band", 16, (4, 8)).reshape(16 * band_rows, NODES // 4)
    partial = lax.dot_general(left, right, (((1,), (1,)), ((), ())), precision=HIGHEST)
    partial = partial.reshape(4, band_rows, 16 * band_rows)
    partial = lax.all_to_all(partial, "band", 0, 0, axis_index_groups=z_lo).sum(0)
    row = lax.all_to_all(partial, "mesh", 0, 0, tiled=True).sum(0, keepdims=True)
    row = row / (NODES * PARTS)
    hproj = lax.all_to_all(jnp.broadcast_to(row, partial.shape), "mesh", 0, 0, tiled=True)
    return filtered, hproj


def solution(mesh):
    placed = (
        P("band", "mesh"),
        P("mesh"),
        P("mesh"),
        P(),
        P("mesh", None),
        P("mesh", None, None),
        P("mesh"),
        P(),
    )
    return jax.shard_map(
        body,
        mesh=mesh,
        in_specs=placed,
        out_specs=(P("band", "mesh"), P("band", None)),
        check_vma=False,
    )
```

time: 1190 us -> 567 us (0.48); the launches traced: 1170 us -> 566 us
  waiting for transfers between devices: 532 us -> 90.7 us
  Pallas kernels: 0 us -> 317 us
  starting transfers between devices: 286 us -> 52.4 us
  other arithmetic: 213 us -> 12.1 us
  local copies, waits for them, and re-layouts: 107 us -> 11.5 us
  blocking collectives: 0 us -> 75.7 us
  between operations: 19.8 us -> 5.05 us
    psum x1 -> x0, waiting for transfers between devices: 332 us -> none  [body(): hproj = lax.psum(partial_rows, 'mesh') / node_total]
    pallas_call x0 -> x1, Pallas kernels: none -> 317 us  [run_filter(): pl.pallas_call(filter_kernel, out_shape=(out, out), in_specs=[pl.BlockSpe...]
    ppermute x71 -> x0, starting transfers between devices: 286 us -> none  [passed_along(): return lax.ppermute(block, axis, route)]
    ppermute x71 -> x0, waiting for transfers between devices: 200 us -> none  [passed_along(): return lax.ppermute(block, axis, route)]
    scatter-add x14 -> x0, other arithmetic: 153 us -> none  [the longest x7 118 us: apply_operator(): sums = jnp.zeros((band_count, node_width + 4 * slot_count), jnp.float32)....]
    all_to_all x0 -> x6, waiting for transfers between devices: none -> 90.7 us  [the longest x2 21.8 us: spread(): return lax.all_to_all(copies, axis, 0, 0, axis_index_groups=members)]
    all_to_all x0 -> x5, blocking collectives: none -> 75.7 us  [the longest x2 22.9 us: spread(): return lax.all_to_all(copies, axis, 0, 0, axis_index_groups=members)]
    gather x14 -> x0, local copies, waits for them, and re-layouts: 56.7 us -> none  [the longest x7 46.9 us: apply_operator(): jnp.take(extended, flat_index, axis=1)]
  transfers between devices with their start and end apart: 72 -> 6, of which waited for: 26 -> 6; matrix products, arithmetic and copies ran while one was open for 2% -> 1% of each run, Pallas kernels for 0% -> 0%
where the time goes in v1:
time: 567 us; the launch traced here: 566 us
  Pallas kernels  317 us (56%)
  waiting for transfers between devices  90.7 us (16%)
  blocking collectives  75.7 us (13%)
  starting transfers between devices  52.4 us (9%)
  other arithmetic  12.1 us (2%)
  local copies, waits for them, and re-layouts  11.5 us (2%)
    pallas_call x1, Pallas kernels, run_filter(): pl.pallas_call(filter_kernel, out_shape=(out, out), in_specs=[pl.BlockSpe...  317 us
    all_to_all x2, blocking collectives, spread(): return lax.all_to_all(copies, axis, 0, 0, axis_index_groups=members)  22.9 us
    all_to_all x2, waiting for transfers between devices, spread(): return lax.all_to_all(copies, axis, 0, 0, axis_index_groups=members)  21.8 us
    all_to_all x1, blocking collectives, body(): lax.all_to_all(both.transpose(2, 0, 1, 3), 'band', 0, 0, axis_index_group...  21.8 us
    all_to_all x1, blocking collectives, body(): lax.all_to_all(partial, 'mesh', 0, 0, tiled=True).sum(0, keepdims=True)  21.5 us
    all_to_all x1, waiting for transfers between devices, body(): start = lax.all_to_all(vectors, 'mesh', 0, 0, tiled=True)  20.5 us
    all_to_all x2, starting transfers between devices, spread(): return lax.all_to_all(copies, axis, 0, 0, axis_index_groups=members)  19.1 us
    all_to_all x1, waiting for transfers between devices, body(): applied = lax.all_to_all(g, 'mesh', 0, 0, tiled=True)  17.4 us
  transfers between devices with their start and end apart: 6, of which 6 were waited for; matrix products, arithmetic and copies ran while one was open for 1% of the time, Pallas kernels for 0%

profile of v1, /device:TPU:1, one launch (start us, length us, event | category | flops | bytes accessed | tf_op | source)
XLA Modules:
  0.0 566.0 jit_solution(9486548093134020681)
XLA Ops:
  0.6 0.7 add_select_fusion.2
  1.3 0.1 reshape.58
  1.4 0.7 bitcast_add_fusion
  2.1 0.1 pad_add_fusion
  2.2 5.9 %sort.14 = (s32[3256]{0:T(1024)S(1)}, s32[3256]{0:T(1024)}) sort(s32[3256]{0:T(1024)S(1)} %get-tuple-element.12, s32[3256]{0:T(1024)S(1)} %iota.11), dimensions={0}, to_apply=%region_0.1 | sort | flops 39072 | bytes 52096 | tf_op jit(solution)/shard_map/sort | solution.py:57
  8.2 3.3 convert_reduce_fusion
  11.6 0.7 constant_dynamic-update-slice_fusion
  12.9 0.8 concatenate.16
  13.7 0.7 broadcast_in_dim.20
  14.4 15.6 %all-to-all-start = ((f32[4,117,128]{2,1,0:T(8,128)}), f32[4,117,128]{2,1,0:T(8,128)S(1)}, u32[]{:S(2)}, u32[]{:S(2)}) async-start(f32[4,117,128]{2,1,0:T(8,128)} %broadcast_in_dim.20), calls=%async_computation | async-start | bytes 491520 | tf_op jit(solution)/shard_map/all_to_all | solution.py:48
  30.0 1.8 all_to_all.54
  31.9 11.8 %all-to-all-done = f32[4,117,128]{2,1,0:T(8,128)S(1)} async-done(((f32[4,117,128]{2,1,0:T(8,128)}), f32[4,117,128]{2,1,0:T(8,128)S(1)}, u32[]{:S(2)}, u32[]{:S(2)}) %all-to-all-start) | async-done | bytes 239648 | tf_op jit(solution)/shard_map/all_to_all | solution.py:48
  43.7 13.6 %all-to-all-start.3 = ((f32[32,1,2048]{2,1,0:T(1,128)}), f32[32,1,2048]{2,1,0:T(1,128)S(1)}, u32[]{:S(2)}, u32[]{:S(2)}) async-start(f32[32,1,2048]{2,1,0:T(1,128)} %all_to_all.54), calls=%async_computation.3 | async-start | bytes 524288 | tf_op jit(solution)/shard_map/all_to_all | solution.py:349
  57.3 20.5 %all-to-all-done.3 = f32[32,1,2048]{2,1,0:T(1,128)S(1)} async-done(((f32[32,1,2048]{2,1,0:T(1,128)}), f32[32,1,2048]{2,1,0:T(1,128)S(1)}, u32[]{:S(2)}, u32[]{:S(2)}) %all-to-all-start.3) | async-done | bytes 262176 | tf_op jit(solution)/shard_map/all_to_all | solution.py:349
  77.8 1.1 broadcast_in_dim.21
  78.9 3.5 all-to-all-start.1
  82.4 0.6 fusion.5
  86.6 0.1 stack.34.coef
  86.7 0.1 copy.45
  86.8 10.0 %all-to-all-done.1 = f32[4,4,117,128]{3,1,2,0:T(4,128)S(1)} async-done(((f32[4,4,117,128]{3,1,2,0:T(4,128)}), f32[4,4,117,128]{3,1,2,0:T(4,128)S(1)}, u32[]{:S(2)}, u32[]{:S(2)}) %all-to-all-start.1) | async-done | bytes 958496 | tf_op jit(solution)/shard_map/all_to_all | solution.py:48
  96.8 0.2 broadcast_in_dim.22
  97.0 5.6 all_to_all.80
  102.6 0.2 copy.28
  102.7 0.3 copy.43
  103.1 317.3 %shard_map.95 = (f32[32,2048]{1,0:T(8,128)S(1)}, f32[32,2048]{1,0:T(8,128)S(1)}) custom-call(f32[8]{0:T(128)S(1)} %stack.34.coef, f32[32,14976]{1,0:T(8,128)S(1)} %bitcast.41, f32[32,2048]{1,0:T(8,128)S(1)} %bitcast.42, f32[384,384]{1,0:T(8,128)S(1)} %pad.18.matrix), custom_call_target="tpu_custom_call" | custom-call | tf_op jit(solution)/shard_map/pallas_call | solution.py:298
  420.4 1.0 copy.29
  421.4 6.5 %all-to-all-start.4 = ((f32[32,1,2048]{2,1,0:T(1,128)}), f32[32,1,2048]{2,1,0:T(1,128)S(1)}, u32[]{:S(2)}, u32[]{:S(2)}) async-start(f32[32,1,2048]{2,1,0:T(1,128)} %copy.29), calls=%async_computation.4 | async-start | bytes 524288 | tf_op jit(solution)/shard_map/all_to_all | solution.py:351
  427.9 1.0 copy.30
  428.9 16.8 %all-to-all-done.4 = f32[32,1,2048]{2,1,0:T(1,128)S(1)} async-done(((f32[32,1,2048]{2,1,0:T(1,128)}), f32[32,1,2048]{2,1,0:T(1,128)S(1)}, u32[]{:S(2)}, u32[]{:S(2)}) %all-to-all-start.4) | async-done | bytes 262176 | tf_op jit(solution)/shard_map/all_to_all | solution.py:351
  445.7 9.2 %all-to-all-start.5 = ((f32[32,1,2048]{2,1,0:T(1,128)}), f32[32,1,2048]{2,1,0:T(1,128)S(1)}, u32[]{:S(2)}, u32[]{:S(2)}) async-start(f32[32,1,2048]{2,1,0:T(1,128)} %copy.30), calls=%async_computation.5 | async-start | bytes 524288 | tf_op jit(solution)/shard_map/all_to_all | solution.py:352
  454.9 0.6 reduce.1
  455.6 0.2 stack.35
  455.7 0.1 copy.31
  455.8 17.4 %all-to-all-done.5 = f32[32,1,2048]{2,1,0:T(1,128)S(1)} async-done(((f32[32,1,2048]{2,1,0:T(1,128)}), f32[32,1,2048]{2,1,0:T(1,128)S(1)}, u32[]{:S(2)}, u32[]{:S(2)}) %all-to-all-start.5) | async-done | bytes 262176 | tf_op jit(solution)/shard_map/all_to_all | solution.py:352
  473.2 0.6 reduce.2
  473.8 0.2 stack.36
  474.0 0.1 copy.32
  474.2 21.8 %all_to_all.81 = f32[4,2,32,512]{3,2,1,0:T(8,128)S(1)} all-to-all(f32[4,2,32,512]{3,2,1,0:T(8,128)S(1)} %maximum_bitcast_fusion), channel_id=1, replica_groups={{0,32,64,96},{128,160,192,224},{256,288,320,352},{384,416,448,480},{1,3..., dimensions={0} | all-to-all | bytes 1048576 | tf_op jit(solution)/shard_map/all_to_all | solution.py:357
  495.9 0.1 broadcast_in_dim.45
  496.1 17.3 %all_to_all.82 = f32[4,128,512]{2,1,0:T(8,128)S(1)} all-to-all(f32[4,128,512]{2,1,0:T(8,128)S(1)} %broadcast_in_dim.45), channel_id=1, replica_groups={{0,128,256,384},{32,160,288,416},{64,192,320,448},{96,224,352,480},{1,1..., dimensions={0} | all-to-all | bytes 2097152 | tf_op jit(solution)/shard_map/all_to_all | solution.py:48
  513.4 1.2 fusion
  514.6 9.5 %all_to_all.83 = f32[4,32,512]{2,1,0:T(8,128)S(1)} all-to-all(f32[4,32,512]{2,1,0:T(8,128)S(1)} %fusion), channel_id=1, replica_groups={{0,32,64,96},{128,160,192,224},{256,288,320,352},{384,416,448,480},{1,3..., dimensions={0} | all-to-all | bytes 524288 | tf_op jit(solution)/shard_map/all_to_all | solution.py:363
  524.2 21.5 %all_to_all.84 = f32[32,1,512]{2,1,0:T(1,128)S(1)} all-to-all(f32[32,1,512]{2,1,0:T(1,128)S(1)} %all_to_all.65), channel_id=1, replica_groups=mesh['band'=16,'mesh'=32] {'mesh'}, dimensions={0} | all-to-all | bytes 131072 | tf_op jit(solution)/shard_map/all_to_all | solution.py:364
  545.7 0.7 broadcast_in_dim.46
  546.4 3.9 all-to-all-start.10
  550.3 0.8 copy.44
  551.1 14.2 %all-to-all-done.10 = f32[32,1,512]{2,1,0:T(1,128)S(1)} async-done(((f32[32,1,512]{2,1,0:T(1,128)}), f32[32,1,512]{2,1,0:T(1,128)S(1)}, u32[]{:S(2)}, u32[]{:S(2)}) %all-to-all-start.10) | async-done | bytes 65568 | tf_op jit(solution)/shard_map/all_to_all | solution.py:366
  565.3 0.6 copy.46
  (22 shorter events, 0.5 us)
Async XLA Ops:
  14.4 29.3 %all-to-all-start = ((f32[4,117,128]{2,1,0:T(8,128)}), f32[4,117,128]{2,1,0:T(8,128)S(1)}, u32[]{:S(2)}, u32[]{:S(2)}) async-start(f32[4,117,128]{2,1,0:T(8,128)} %broadcast_in_dim.20), calls=%async_computation | async-start | bytes 491520 | tf_op jit(solution)/shard_map/all_to_all | solution.py:48
  31.9 50.5 %copy-start.1 = (f32[3]{0:T(128)S(1)}, f32[3]{0:T(128)}, u32[]{:S(2)}) copy-start(f32[3]{0:T(128)} %param.15) | copy-start | bytes 40
  31.9 54.7 %copy-start = (f32[343,343]{1,0:T(8,128)S(1)}, f32[343,343]{1,0:T(8,128)}, u32[]{:S(2)}) copy-start(f32[343,343]{1,0:T(8,128)} %param.11) | copy-start | bytes 1411792
  43.7 34.2 %all-to-all-start.3 = ((f32[32,1,2048]{2,1,0:T(1,128)}), f32[32,1,2048]{2,1,0:T(1,128)S(1)}, u32[]{:S(2)}, u32[]{:S(2)}) async-start(f32[32,1,2048]{2,1,0:T(1,128)} %all_to_all.54), calls=%async_computation.3 | async-start | bytes 524288 | tf_op jit(solution)/shard_map/all_to_all | solution.py:349
  78.9 17.9 %all-to-all-start.1 = ((f32[4,4,117,128]{3,1,2,0:T(4,128)}), f32[4,4,117,128]{3,1,2,0:T(4,128)S(1)}, u32[]{:S(2)}, u32[]{:S(2)}) async-start(f32[4,4,117,128]{3,1,2,0:T(4,128)} %broadcast_in_dim.21), calls=%async_computation.1 | async-start | bytes 1916928 | tf_op jit(solution)/shard_map/all_to_all | solution.py:48
  421.4 24.3 %all-to-all-start.4 = ((f32[32,1,2048]{2,1,0:T(1,128)}), f32[32,1,2048]{2,1,0:T(1,128)S(1)}, u32[]{:S(2)}, u32[]{:S(2)}) async-start(f32[32,1,2048]{2,1,0:T(1,128)} %copy.29), calls=%async_computation.4 | async-start | bytes 524288 | tf_op jit(solution)/shard_map/all_to_all | solution.py:351
  445.7 27.5 %all-to-all-start.5 = ((f32[32,1,2048]{2,1,0:T(1,128)}), f32[32,1,2048]{2,1,0:T(1,128)S(1)}, u32[]{:S(2)}, u32[]{:S(2)}) async-start(f32[32,1,2048]{2,1,0:T(1,128)} %copy.30), calls=%async_computation.5 | async-start | bytes 524288 | tf_op jit(solution)/shard_map/all_to_all | solution.py:352
  546.4 18.9 %all-to-all-start.10 = ((f32[32,1,512]{2,1,0:T(1,128)}), f32[32,1,512]{2,1,0:T(1,128)S(1)}, u32[]{:S(2)}, u32[]{:S(2)}) async-start(f32[32,1,512]{2,1,0:T(1,128)} %broadcast_in_dim.46), calls=%async_computation.10 | async-start | bytes 131072 | tf_op jit(solution)/shard_map/all_to_all | solution.py:366

commit v2 on v1

v2 whole, which is shorter than its diff:
```python
import functools

import jax
import jax.numpy as jnp
from jax import lax
from jax.experimental import pallas as pl
from jax.experimental.pallas import tpu as pltpu
from jax.sharding import PartitionSpec as P

DEGREE = 3
OFFSETS = (-2, -1, 1, 2)
HIGHEST = lax.Precision.HIGHEST

PARTS = 32
GROUPS = PARTS // 8
NODES = 2048
SLOTS = 128
GHOSTS = 4 * SLOTS
EXT = GHOSTS + NODES
CELLS = 8
NPC = 343
NPC_PAD = 384
CELL_CHUNKS = NPC_PAD // 128
ENTRIES = CELLS * NPC + GHOSTS
ENTRY_CHUNKS = 26
ENTRY_PAD = ENTRY_CHUNKS * 128
FEW = 5
SKIP = 2
SHORT_RUN = 16

IDX_AT = 0
POS_AT = IDX_AT + CELLS * CELL_CHUNKS
PLACE_AT = POS_AT + ENTRY_CHUNKS
END_AT = PLACE_AT + ENTRY_CHUNKS
SEND_AT = END_AT + EXT // 128
POT_AT = SEND_AT + GHOSTS // 128
MISC_AT = POT_AT + NODES // 128
TABLE_CHUNKS = MISC_AT + 1


def groups_of(size, bits):
    mask = sum(bits)
    members = {}
    for i in range(size):
        members.setdefault(i & ~mask, []).append(i)
    return list(members.values())


def spread(block, axis, size, bits):
    members = groups_of(size, bits)
    copies = jnp.broadcast_to(block[None], (len(members[0]),) + block.shape)
    return lax.all_to_all(copies, axis, 0, 0, axis_index_groups=members)


def partition_table(cell_nodes, send_list, potential, cell_scale, node_count):
    shifted = jnp.where(cell_nodes >= NODES, cell_nodes - NODES, cell_nodes + GHOSTS)
    slots = jnp.pad(shifted, ((0, 0), (0, NPC_PAD - NPC))).reshape(-1)
    send = send_list.reshape(-1)
    keys = jnp.concatenate([shifted.reshape(-1), send + GHOSTS])
    tagged = keys * 4096 + lax.iota(jnp.int32, ENTRIES)
    ordered = lax.sort(tagged)
    entry = ordered & 4095
    sorted_key = ordered >> 12
    from_slot = (entry // NPC) * NPC_PAD + entry % NPC
    position = jnp.where(entry < CELLS * NPC, from_slot, entry + (CELLS * NPC_PAD - CELLS * NPC))
    nodes = lax.iota(jnp.int32, EXT)
    up_to = jnp.sum((keys[None, :] <= nodes[:, None]).astype(jnp.int32), axis=1)
    before = jnp.concatenate([jnp.zeros((1,), jnp.int32), up_to[:-1]])
    end = jnp.where(up_to > before, up_to - 1, -1)
    first = jnp.sum((keys[None, :] < sorted_key[:, None]).astype(jnp.int32), axis=1)
    place = lax.iota(jnp.int32, ENTRIES) - first
    longest = jnp.max(place) + 1
    ghost_entries = up_to[GHOSTS - 1]
    place = jnp.pad(place, (0, ENTRY_PAD - ENTRIES))
    position = jnp.pad(position, (0, ENTRY_PAD - ENTRIES))
    misc = jnp.concatenate([
        cell_scale,
        jnp.stack([node_count[0], ghost_entries, longest]).astype(jnp.float32),
        jnp.zeros((117,), jnp.float32),
    ])
    ints = jnp.concatenate([slots, position, place, end, send]).astype(jnp.float32)
    return jnp.concatenate([ints, potential, misc]).reshape(TABLE_CHUNKS, 128)


def chunk(c):
    return pl.ds(c * 128, 128)


def rows(g):
    return pl.ds(pl.multiple_of(g * 8, 8), 8)


def picked(sources, index):
    low = index & 127
    high = index >> 7
    total = jnp.zeros((8, 128), jnp.float32)
    for j, source in sources:
        total = jnp.where(high == j, jnp.take_along_axis(source, low, axis=1), total)
    return total


def filter_kernel(
    step_count, last, coef, table, start, matrix, out,
    mat_hi, mat_lo, idx, pos, place, end, send, scale, cur, prev, ext, vals, prod, arrived, w, halo, sums,
):
    lane = lax.broadcasted_iota(jnp.int32, (8, 128), 1)
    last_lane = jnp.full((8, 128), 127, jnp.int32)

    for k in range(CELL_CHUNKS):
        whole = matrix[k * 128 : (k + 1) * 128, :]
        high_part = whole.astype(jnp.bfloat16)
        low_part = (whole - high_part.astype(jnp.float32)).astype(jnp.bfloat16)
        mat_hi[k * 128 : (k + 1) * 128, :] = high_part
        mat_lo[k * 128 : (k + 1) * 128, :] = low_part

    def to_int(dest, first, count):
        for c in range(count):
            dest[:, chunk(c)] = table[:, chunk(first + c)].astype(jnp.int32)

    to_int(idx, IDX_AT, CELLS * CELL_CHUNKS)
    to_int(pos, POS_AT, ENTRY_CHUNKS)
    to_int(place, PLACE_AT, ENTRY_CHUNKS)
    to_int(end, END_AT, EXT // 128)
    to_int(send, SEND_AT, GHOSTS // 128)
    for c in range(CELLS):
        column = table[:, MISC_AT * 128 + c : MISC_AT * 128 + c + 1]
        scale[c * 32 : (c + 1) * 32, :] = jnp.broadcast_to(column, (PARTS, 128))

    def misc(c):
        return table[:, MISC_AT * 128 + CELLS + c : MISC_AT * 128 + CELLS + c + 1]

    few = (jnp.max(misc(1)).astype(jnp.int32) <= FEW * 128) & (jnp.min(misc(1)).astype(jnp.int32) >= SKIP * 128)
    long_runs = jnp.max(misc(2)).astype(jnp.int32) > SHORT_RUN

    if last:
        cur[...] = start[...]
    else:
        live = misc(0).astype(jnp.int32)
        node = lax.broadcasted_iota(jnp.int32, (PARTS, NODES), 1)
        cur[...] = jnp.where(node < live, start[...], 0.0)
        prev[...] = jnp.zeros((PARTS, NODES), jnp.float32)

    def over_groups(body):
        def at(g, _):
            body(g, rows(g))
            return 0

        lax.fori_loop(0, GROUPS, at, 0)

    def wrap(values, k):
        c = chunk(k)
        halo[2:34, c] = values
        halo[0:2, c] = values[30:32]
        halo[34:36, c] = values[0:2]

    def products_of(g):
        return [
            (c * CELL_CHUNKS + k, prod[pl.ds(pl.multiple_of(c * 32 + g * 8, 8), 8), chunk(k)])
            for c in range(CELLS)
            for k in range(CELL_CHUNKS)
        ]

    def pick_into_w(r, sources, first, stop):
        for q in range(first, stop):
            w[r, chunk(q)] = picked(sources, pos[r, chunk(q)])

    def doubling(r, stop, distances):
        for d in distances:
            back = (lane - d) & 127
            for q in range(stop):
                x = w[r, chunk(q)]
                near = jnp.minimum(place[r, chunk(q)], lane) >= d
                w[r, chunk(q)] = x + jnp.where(near, jnp.take_along_axis(x, back, axis=1), 0.0)

    def run_sums(r, stop):
        xs = [w[r, chunk(q)] for q in range(stop)]
        at = [jnp.minimum(place[r, chunk(q)], lane) for q in range(stop)]
        d = 1
        while d < SHORT_RUN:
            back = (lane - d) & 127
            moved = [jnp.take_along_axis(x, back, axis=1) for x in xs]
            xs = [x + jnp.where(a >= d, m, 0.0) for x, a, m in zip(xs, at, moved)]
            d *= 2
        for q in range(stop):
            w[r, chunk(q)] = xs[q]

        @pl.when(long_runs)
        def _():
            doubling(r, stop, (16, 32, 64))

        carry = jnp.zeros((8, 128), jnp.float32)
        for q in range(stop):
            x = w[r, chunk(q)]
            total = jnp.take_along_axis(x, last_lane, axis=1)
            goes_on = place[r, chunk(q)] > lane
            through = jnp.take_along_axis(jnp.where(goes_on, 1.0, 0.0), last_lane, axis=1)
            w[r, chunk(q)] = x + jnp.where(goes_on, carry, 0.0)
            carry = total + through * carry

    def run_ends(r, first, stop, node_first, node_count, dest):
        sources = [(q, w[r, chunk(q)]) for q in range(first, stop)]
        for n in range(node_count):
            dest[r, chunk(n)] = picked(sources, end[r, chunk(node_first + n)])

    def ghost_sums(stop):
        def picks(g, r):
            pick_into_w(r, products_of(g), 0, stop)
            run_sums(r, stop)
            run_ends(r, 0, stop, 0, 4, sums)

        over_groups(picks)

    def own_sums(first):
        def picks(g, r):
            sources = products_of(g)
            base = CELLS * CELL_CHUNKS
            sources += [(base + k, arrived[r, chunk(k)]) for k in range(4)]
            pick_into_w(r, sources, first, ENTRY_CHUNKS)

        over_groups(picks)
        over_groups(lambda g, r: run_sums(r, ENTRY_CHUNKS))
        over_groups(lambda g, r: run_ends(r, first, ENTRY_CHUNKS, 4, 16, sums))

    def apply():
        def outgoing(g, r):
            sources = [(j, cur[r, chunk(j)]) for j in range(NODES // 128)]
            for k in range(4):
                sums[r, chunk(k)] = picked(sources, send[r, chunk(k)])

        over_groups(outgoing)
        for k in range(4):
            wrap(sums[:, k * 128 : (k + 1) * 128], k)
        for k, o in enumerate(OFFSETS):
            ext[:, k * 128 : (k + 1) * 128] = halo[2 + o : 34 + o, k * 128 : (k + 1) * 128]
        ext[:, GHOSTS:] = cur[...]

        def gather(g, r):
            sources = [(j, ext[r, chunk(j)]) for j in range(EXT // 128)]

            def some_cells(b, _):
                for u in range(4):
                    c = b * 4 + u
                    for k in range(CELL_CHUNKS):
                        here = pl.ds(pl.multiple_of(c * NPC_PAD + k * 128, 128), 128)
                        there = pl.ds(pl.multiple_of(c * 32 + g * 8, 8), 8)
                        vals[there, chunk(k)] = picked(sources, idx[r, here])
                return 0

            lax.fori_loop(0, 2, some_cells, 0)

        over_groups(gather)

        x = vals[...]
        high = x.astype(jnp.bfloat16)
        low = (x - high.astype(jnp.float32)).astype(jnp.bfloat16)

        def dot(a, b):
            return jnp.dot(a, b, preferred_element_type=jnp.float32)

        y = dot(high, mat_hi[...]) + (dot(low, mat_hi[...]) + dot(high, mat_lo[...]))
        for k in range(CELL_CHUNKS):
            prod[:, k * 128 : (k + 1) * 128] = y[:, k * 128 : (k + 1) * 128] * scale[...]

        pl.when(few)(lambda: ghost_sums(FEW))
        pl.when(~few)(lambda: ghost_sums(ENTRY_CHUNKS))
        for k in range(4):
            wrap(sums[:, k * 128 : (k + 1) * 128], k)
        for k, o in enumerate(OFFSETS):
            arrived[:, k * 128 : (k + 1) * 128] = halo[2 - o : 34 - o, k * 128 : (k + 1) * 128]

        pl.when(few)(lambda: own_sums(SKIP))
        pl.when(~few)(lambda: own_sums(0))

    def step(i, _):
        apply()
        degree = lax.rem(i, DEGREE)
        gain = coef[degree]
        back = coef[DEGREE + degree]
        centre = coef[2 * DEGREE]
        for c in range(NODES // 128):
            here = chunk(c)
            v = cur[:, here]
            hv = sums[:, here] + table[:, chunk(POT_AT + c)] * v
            following = gain * (hv - centre * v)
            following = jnp.where(degree == 0, following, following - back * prev[:, here])
            prev[:, here] = v
            cur[:, here] = following
        return 0

    if last:
        apply()
        for c in range(NODES // 128):
            out[:, chunk(c)] = sums[:, chunk(c)] + table[:, chunk(POT_AT + c)] * cur[:, chunk(c)]
    else:
        lax.fori_loop(0, step_count, step, 0)
        out[...] = cur[...]


def run_filter(coef, table, start, cell_matrix, step_count, last):
    padded = jnp.pad(cell_matrix, ((0, NPC_PAD - NPC), (0, NPC_PAD - NPC)))
    vmem = pl.BlockSpec(memory_space=pltpu.VMEM)
    f32, i32 = jnp.float32, jnp.int32
    cells = CELLS * PARTS
    return pl.pallas_call(
        functools.partial(filter_kernel, step_count, last),
        out_shape=jax.ShapeDtypeStruct((PARTS, NODES), f32),
        in_specs=[pl.BlockSpec(memory_space=pltpu.SMEM)] + [vmem] * 3,
        out_specs=vmem,
        scratch_shapes=[
            pltpu.VMEM((NPC_PAD, NPC_PAD), jnp.bfloat16),
            pltpu.VMEM((NPC_PAD, NPC_PAD), jnp.bfloat16),
            pltpu.VMEM((PARTS, CELLS * NPC_PAD), i32),
            pltpu.VMEM((PARTS, ENTRY_PAD), i32),
            pltpu.VMEM((PARTS, ENTRY_PAD), i32),
            pltpu.VMEM((PARTS, EXT), i32),
            pltpu.VMEM((PARTS, GHOSTS), i32),
            pltpu.VMEM((cells, 128), f32),
            pltpu.VMEM((PARTS, NODES), f32),
            pltpu.VMEM((PARTS, NODES), f32),
            pltpu.VMEM((PARTS, EXT), f32),
            pltpu.VMEM((cells, NPC_PAD), f32),
            pltpu.VMEM((cells, NPC_PAD), f32),
            pltpu.VMEM((PARTS, GHOSTS), f32),
            pltpu.VMEM((PARTS, ENTRY_PAD), f32),
            pltpu.VMEM((40, GHOSTS), f32),
            pltpu.VMEM((PARTS, NODES), f32),
        ],
        compiler_params=pltpu.CompilerParams(vmem_limit_bytes=48 * 1024 * 1024),
    )(coef, table, start, padded)


def coefficients(filter_bounds):
    lowest, wanted_top, upper = filter_bounds[0], filter_bounds[1], filter_bounds[2]
    half_width = (upper - wanted_top) / 2.0
    centre = (upper + wanted_top) / 2.0
    sigma = half_width / (lowest - centre)
    ratio = 2.0 / sigma
    gains, backs = [sigma / half_width], [jnp.zeros_like(sigma)]
    for _ in range(DEGREE - 1):
        following = 1.0 / (ratio - sigma)
        gains.append(2.0 * following / half_width)
        backs.append(sigma * following)
        sigma = following
    return jnp.stack(gains + backs + [centre, centre])


def body(vectors, potential, cell_scale, cell_matrix, cell_nodes, send_list, node_count, filter_bounds):
    own_table = partition_table(cell_nodes, send_list[0], potential, cell_scale, node_count)
    table = spread(own_table, "mesh", PARTS, (8, 16))
    table = spread(table, "mesh", PARTS, (2, 4))
    table = spread(table, "mesh", PARTS, (1,))
    table = table.transpose(2, 1, 0, 3, 4).reshape(PARTS, TABLE_CHUNKS * 128)

    start = lax.all_to_all(vectors, "mesh", 0, 0, tiled=True)
    coef = coefficients(filter_bounds)
    f = run_filter(coef, table, start, cell_matrix, 2 * DEGREE, False)
    g = run_filter(coef, table, f, cell_matrix, 1, True)
    filtered = lax.all_to_all(f, "mesh", 0, 0, tiled=True)
    applied = lax.all_to_all(g, "mesh", 0, 0, tiled=True)

    band_rows = filtered.shape[0]
    z_lo = groups_of(16, (1, 2))
    both = jnp.stack([filtered, applied]).reshape(2, band_rows, 4, NODES // 4)
    both = lax.all_to_all(both.transpose(2, 0, 1, 3), "band", 0, 0, axis_index_groups=z_lo)
    right = both[:, 0].reshape(4 * band_rows, NODES // 4)
    left = both[:, 1].reshape(4 * band_rows, NODES // 4)
    right = spread(right, "band", 16, (4, 8)).reshape(16 * band_rows, NODES // 4)
    partial = lax.dot_general(left, right, (((1,), (1,)), ((), ())), precision=HIGHEST)
    partial = partial.reshape(4, band_rows, 16 * band_rows)
    partial = lax.all_to_all(partial, "band", 0, 0, axis_index_groups=z_lo).sum(0)
    row = lax.all_to_all(partial, "mesh", 0, 0, tiled=True).sum(0, keepdims=True)
    row = row / (NODES * PARTS)
    hproj = lax.all_to_all(jnp.broadcast_to(row, partial.shape), "mesh", 0, 0, tiled=True)
    return filtered, hproj


def solution(mesh):
    placed = (
        P("band", "mesh"),
        P("mesh"),
        P("mesh"),
        P(),
        P("mesh", None),
        P("mesh", None, None),
        P("mesh"),
        P(),
    )
    return jax.shard_map(
        body,
        mesh=mesh,
        in_specs=placed,
        out_specs=(P("band", "mesh"), P("band", None)),
        check_vma=False,
    )
```

time: 567 us -> 360 us (0.63)
  Pallas kernels: 317 us -> 103 us
  other arithmetic: 12.1 us -> 17.9 us
    pallas_call x1 -> x2, Pallas kernels: 317 us -> 103 us  [run_filter(): pl.pallas_call(functools.partial(filter_kernel, step_count, last), out_sh...]
where the time goes in v2:
time: 360 us; the launch traced here: 359 us
  Pallas kernels  103 us (29%)
  waiting for transfers between devices  90.7 us (25%)
  blocking collectives  75.7 us (21%)
  starting transfers between devices  52.3 us (15%)
  other arithmetic  17.9 us (5%)
  local copies, waits for them, and re-layouts  12.1 us (3%)
  between operations  5.66 us (2%)
    pallas_call x2, Pallas kernels, run_filter(): pl.pallas_call(functools.partial(filter_kernel, step_count, last), out_sh...  103 us
    all_to_all x2, blocking collectives, spread(): return lax.all_to_all(copies, axis, 0, 0, axis_index_groups=members)  22.9 us
    all_to_all x2, waiting for transfers between devices, spread(): return lax.all_to_all(copies, axis, 0, 0, axis_index_groups=members)  21.8 us
    all_to_all x1, blocking collectives, body(): lax.all_to_all(both.transpose(2, 0, 1, 3), 'band', 0, 0, axis_index_group...  21.8 us
    all_to_all x1, blocking collectives, body(): lax.all_to_all(partial, 'mesh', 0, 0, tiled=True).sum(0, keepdims=True)  21.5 us
    all_to_all x1, waiting for transfers between devices, body(): start = lax.all_to_all(vectors, 'mesh', 0, 0, tiled=True)  20.5 us
    all_to_all x2, starting transfers between devices, spread(): return lax.all_to_all(copies, axis, 0, 0, axis_index_groups=members)  19.1 us
    all_to_all x1, waiting for transfers between devices, body(): filtered = lax.all_to_all(f, 'mesh', 0, 0, tiled=True)  17.4 us
  transfers between devices with their start and end apart: 6, of which 6 were waited for; matrix products, arithmetic and copies ran while one was open for 1% of the time, Pallas kernels for 0%

profile of v2, /device:TPU:1, one launch (start us, length us, event | category | flops | bytes accessed | tf_op | source)
XLA Modules:
  0.0 358.5 jit_solution(1938490418709656619)
XLA Ops:
  0.6 0.7 add_select_fusion.2
  1.4 0.7 bitcast_add_fusion
  2.2 5.9 %sort.14 = (s32[3256]{0:T(1024)S(1)}, s32[3256]{0:T(1024)}) sort(s32[3256]{0:T(1024)S(1)} %get-tuple-element.10, s32[3256]{0:T(1024)S(1)} %iota.14), dimensions={0}, to_apply=%region_0.1 | sort | flops 39072 | bytes 52096 | tf_op jit(solution)/shard_map/sort | solution.py:61
  8.1 3.3 convert_reduce_fusion.1
  11.4 4.4 %convert_reduce_fusion = s32[3256]{0:T(1024)S(1)} fusion(s32[3256]{0:T(1024)S(1)} %get-tuple-element.9, s32[3256]{0:T(1024)S(1)} %get-tuple-element.7), kind=kLoop, calls=%fused_computation | loop fusion | flops 31801352 | bytes 39072 | tf_op jit(solution)/shard_map/reduce_sum | solution.py:70
  15.8 0.6 fusion.5
  16.5 0.6 slice.29
  17.2 0.7 constant_dynamic-update-slice_fusion
  19.2 0.7 add_convert_fusion
  19.9 0.8 concatenate.16
  20.7 0.7 broadcast_in_dim.20
  21.4 15.6 %all-to-all-start = ((f32[4,117,128]{2,1,0:T(8,128)}), f32[4,117,128]{2,1,0:T(8,128)S(1)}, u32[]{:S(2)}, u32[]{:S(2)}) async-start(f32[4,117,128]{2,1,0:T(8,128)} %broadcast_in_dim.20), calls=%async_computation | async-start | bytes 491520 | tf_op jit(solution)/shard_map/all_to_all | solution.py:52
  37.0 1.8 all_to_all.54
  38.8 11.8 %all-to-all-done = f32[4,117,128]{2,1,0:T(8,128)S(1)} async-done(((f32[4,117,128]{2,1,0:T(8,128)}), f32[4,117,128]{2,1,0:T(8,128)S(1)}, u32[]{:S(2)}, u32[]{:S(2)}) %all-to-all-start) | async-done | bytes 239648 | tf_op jit(solution)/shard_map/all_to_all | solution.py:52
  50.6 13.6 %all-to-all-start.3 = ((f32[32,1,2048]{2,1,0:T(1,128)}), f32[32,1,2048]{2,1,0:T(1,128)S(1)}, u32[]{:S(2)}, u32[]{:S(2)}) async-start(f32[32,1,2048]{2,1,0:T(1,128)} %all_to_all.54), calls=%async_computation.3 | async-start | bytes 524288 | tf_op jit(solution)/shard_map/all_to_all | solution.py:354
  64.3 20.5 %all-to-all-done.3 = f32[32,1,2048]{2,1,0:T(1,128)S(1)} async-done(((f32[32,1,2048]{2,1,0:T(1,128)}), f32[32,1,2048]{2,1,0:T(1,128)S(1)}, u32[]{:S(2)}, u32[]{:S(2)}) %all-to-all-start.3) | async-done | bytes 262176 | tf_op jit(solution)/shard_map/all_to_all | solution.py:354
  84.8 1.1 broadcast_in_dim.21
  85.9 3.5 all-to-all-start.1
  89.4 0.6 fusion.6
  93.6 0.1 stack.40.coef
  93.8 10.0 %all-to-all-done.1 = f32[4,4,117,128]{3,1,2,0:T(4,128)S(1)} async-done(((f32[4,4,117,128]{3,1,2,0:T(4,128)}), f32[4,4,117,128]{3,1,2,0:T(4,128)S(1)}, u32[]{:S(2)}, u32[]{:S(2)}) %all-to-all-start.1) | async-done | bytes 958496 | tf_op jit(solution)/shard_map/all_to_all | solution.py:52
  103.7 0.2 broadcast_in_dim.22
  104.0 5.6 %all_to_all.80 = f32[2,4,4,117,128]{4,2,3,1,0:T(4,128)S(1)} all-to-all(f32[2,4,4,117,128]{4,2,3,1,0:T(4,128)S(1)} %broadcast_in_dim.22), channel_id=1, replica_groups={{0,1},{2,3},{4,5},{6,7},{8,9},{10,11},{12,13},{14,15},{16,17},{18,19},{..., dimensions={0} | all-to-all | bytes 3833856 | tf_op jit(solution)/shard_map/all_to_all | solution.py:52
  109.6 0.2 copy.28
  109.8 0.3 copy.43
  110.1 87.6 %shard_map.95.start = f32[32,2048]{1,0:T(8,128)S(1)} custom-call(f32[8]{0:T(128)S(1)} %stack.40.coef, f32[32,14976]{1,0:T(8,128)S(1)} %bitcast.42, f32[32,2048]{1,0:T(8,128)S(1)} %bitcast.45, f32[384,384]{1,0:T(8,128)S(1)} %pad.19.matrix), custom_call_target="tpu_custom_call" | custom-call | tf_op jit(solution)/shard_map/pallas_call | solution.py:304
  197.8 15.3 %shard_map.96 = f32[32,2048]{1,0:T(8,128)S(1)} custom-call(f32[8]{0:T(128)S(1)} %stack.40.coef, f32[32,14976]{1,0:T(8,128)S(1)} %bitcast.43, f32[32,2048]{1,0:T(8,128)S(1)} %shard_map.95.start, f32[384,384]{1,0:T(8,128)S(1)} %pad.19.matrix), custom_call_target="tpu_custom_call" | custom-call | tf_op jit(solution)/shard_map/pallas_call | solution.py:304
  213.0 1.0 copy.30
  214.0 6.5 %all-to-all-start.5 = ((f32[32,1,2048]{2,1,0:T(1,128)}), f32[32,1,2048]{2,1,0:T(1,128)S(1)}, u32[]{:S(2)}, u32[]{:S(2)}) async-start(f32[32,1,2048]{2,1,0:T(1,128)} %copy.30), calls=%async_computation.5 | async-start | bytes 524288 | tf_op jit(solution)/shard_map/all_to_all | solution.py:359
  220.5 1.0 copy.29
  221.5 16.8 %all-to-all-done.5 = f32[32,1,2048]{2,1,0:T(1,128)S(1)} async-done(((f32[32,1,2048]{2,1,0:T(1,128)}), f32[32,1,2048]{2,1,0:T(1,128)S(1)}, u32[]{:S(2)}, u32[]{:S(2)}) %all-to-all-start.5) | async-done | bytes 262176 | tf_op jit(solution)/shard_map/all_to_all | solution.py:359
  238.3 9.2 %all-to-all-start.4 = ((f32[32,1,2048]{2,1,0:T(1,128)}), f32[32,1,2048]{2,1,0:T(1,128)S(1)}, u32[]{:S(2)}, u32[]{:S(2)}) async-start(f32[32,1,2048]{2,1,0:T(1,128)} %copy.29), calls=%async_computation.4 | async-start | bytes 524288 | tf_op jit(solution)/shard_map/all_to_all | solution.py:358
  247.5 0.6 reduce.2
  248.1 0.2 stack.44
  248.4 17.4 %all-to-all-done.4 = f32[32,1,2048]{2,1,0:T(1,128)S(1)} async-done(((f32[32,1,2048]{2,1,0:T(1,128)}), f32[32,1,2048]{2,1,0:T(1,128)S(1)}, u32[]{:S(2)}, u32[]{:S(2)}) %all-to-all-start.4) | async-done | bytes 262176 | tf_op jit(solution)/shard_map/all_to_all | solution.py:358
  265.8 0.6 reduce.1
  266.4 0.2 stack.43
  266.7 21.8 %all_to_all.81 = f32[4,2,32,512]{3,2,1,0:T(8,128)S(1)} all-to-all(f32[4,2,32,512]{3,2,1,0:T(8,128)S(1)} %maximum_bitcast_fusion), channel_id=1, replica_groups={{0,32,64,96},{128,160,192,224},{256,288,320,352},{384,416,448,480},{1,3..., dimensions={0} | all-to-all | bytes 1048576 | tf_op jit(solution)/shard_map/all_to_all | solution.py:364
  288.5 0.1 broadcast_in_dim.24
  288.6 17.3 %all_to_all.82 = f32[4,128,512]{2,1,0:T(8,128)S(1)} all-to-all(f32[4,128,512]{2,1,0:T(8,128)S(1)} %broadcast_in_dim.24), channel_id=1, replica_groups={{0,128,256,384},{32,160,288,416},{64,192,320,448},{96,224,352,480},{1,1..., dimensions={0} | all-to-all | bytes 2097152 | tf_op jit(solution)/shard_map/all_to_all | solution.py:52
  305.9 1.2 fusion
  307.1 9.5 %all_to_all.83 = f32[4,32,512]{2,1,0:T(8,128)S(1)} all-to-all(f32[4,32,512]{2,1,0:T(8,128)S(1)} %fusion), channel_id=1, replica_groups={{0,32,64,96},{128,160,192,224},{256,288,320,352},{384,416,448,480},{1,3..., dimensions={0} | all-to-all | bytes 524288 | tf_op jit(solution)/shard_map/all_to_all | solution.py:370
  316.7 21.5 %all_to_all.84 = f32[32,1,512]{2,1,0:T(1,128)S(1)} all-to-all(f32[32,1,512]{2,1,0:T(1,128)S(1)} %all_to_all.65), channel_id=1, replica_groups=mesh['band'=16,'mesh'=32] {'mesh'}, dimensions={0} | all-to-all | bytes 131072 | tf_op jit(solution)/shard_map/all_to_all | solution.py:371
  338.3 0.7 broadcast_in_dim.48
  339.0 3.9 %all-to-all-start.10 = ((f32[32,1,512]{2,1,0:T(1,128)}), f32[32,1,512]{2,1,0:T(1,128)S(1)}, u32[]{:S(2)}, u32[]{:S(2)}) async-start(f32[32,1,512]{2,1,0:T(1,128)} %broadcast_in_dim.48), calls=%async_computation.10 | async-start | bytes 131072 | tf_op jit(solution)/shard_map/all_to_all | solution.py:373
  342.9 0.8 copy.44
  343.7 14.2 %all-to-all-done.10 = f32[32,1,512]{2,1,0:T(1,128)S(1)} async-done(((f32[32,1,512]{2,1,0:T(1,128)}), f32[32,1,512]{2,1,0:T(1,128)S(1)}, u32[]{:S(2)}, u32[]{:S(2)}) %all-to-all-start.10) | async-done | bytes 65568 | tf_op jit(solution)/shard_map/all_to_all | solution.py:373
  357.9 0.6 copy.46
  (27 shorter events, 0.9 us)
Async XLA Ops:
  21.4 29.3 %all-to-all-start = ((f32[4,117,128]{2,1,0:T(8,128)}), f32[4,117,128]{2,1,0:T(8,128)S(1)}, u32[]{:S(2)}, u32[]{:S(2)}) async-start(f32[4,117,128]{2,1,0:T(8,128)} %broadcast_in_dim.20), calls=%async_computation | async-start | bytes 491520 | tf_op jit(solution)/shard_map/all_to_all | solution.py:52
  38.8 50.5 %copy-start.1 = (f32[3]{0:T(128)S(1)}, f32[3]{0:T(128)}, u32[]{:S(2)}) copy-start(f32[3]{0:T(128)} %param.15) | copy-start | bytes 40
  38.8 54.7 %copy-start = (f32[343,343]{1,0:T(8,128)S(1)}, f32[343,343]{1,0:T(8,128)}, u32[]{:S(2)}) copy-start(f32[343,343]{1,0:T(8,128)} %param.11) | copy-start | bytes 1411792
  50.6 34.2 %all-to-all-start.3 = ((f32[32,1,2048]{2,1,0:T(1,128)}), f32[32,1,2048]{2,1,0:T(1,128)S(1)}, u32[]{:S(2)}, u32[]{:S(2)}) async-start(f32[32,1,2048]{2,1,0:T(1,128)} %all_to_all.54), calls=%async_computation.3 | async-start | bytes 524288 | tf_op jit(solution)/shard_map/all_to_all | solution.py:354
  85.9 17.9 %all-to-all-start.1 = ((f32[4,4,117,128]{3,1,2,0:T(4,128)}), f32[4,4,117,128]{3,1,2,0:T(4,128)S(1)}, u32[]{:S(2)}, u32[]{:S(2)}) async-start(f32[4,4,117,128]{3,1,2,0:T(4,128)} %broadcast_in_dim.21), calls=%async_computation.1 | async-start | bytes 1916928 | tf_op jit(solution)/shard_map/all_to_all | solution.py:52
  214.0 24.3 %all-to-all-start.5 = ((f32[32,1,2048]{2,1,0:T(1,128)}), f32[32,1,2048]{2,1,0:T(1,128)S(1)}, u32[]{:S(2)}, u32[]{:S(2)}) async-start(f32[32,1,2048]{2,1,0:T(1,128)} %copy.30), calls=%async_computation.5 | async-start | bytes 524288 | tf_op jit(solution)/shard_map/all_to_all | solution.py:359
  238.3 27.5 %all-to-all-start.4 = ((f32[32,1,2048]{2,1,0:T(1,128)}), f32[32,1,2048]{2,1,0:T(1,128)S(1)}, u32[]{:S(2)}, u32[]{:S(2)}) async-start(f32[32,1,2048]{2,1,0:T(1,128)} %copy.29), calls=%async_computation.4 | async-start | bytes 524288 | tf_op jit(solution)/shard_map/all_to_all | solution.py:358
  339.0 18.9 %all-to-all-start.10 = ((f32[32,1,512]{2,1,0:T(1,128)}), f32[32,1,512]{2,1,0:T(1,128)S(1)}, u32[]{:S(2)}, u32[]{:S(2)}) async-start(f32[32,1,512]{2,1,0:T(1,128)} %broadcast_in_dim.48), calls=%async_computation.10 | async-start | bytes 131072 | tf_op jit(solution)/shard_map/all_to_all | solution.py:373

commit v3 on v2

--- a/solution.py
+++ b/solution.py
@@ -25,7 +25,7 @@
 ENTRY_CHUNKS = 26
 ENTRY_PAD = ENTRY_CHUNKS * 128
 FEW = 5
-SKIP = 2
+SKIP = 3
 SHORT_RUN = 16
 
 IDX_AT = 0
@@ -50,6 +50,26 @@
     members = groups_of(size, bits)
     copies = jnp.broadcast_to(block[None], (len(members[0]),) + block.shape)
     return lax.all_to_all(copies, axis, 0, 0, axis_index_groups=members)
+
+
+def swapped(block, axis, size, distance):
+    return lax.ppermute(block, axis, [(i ^ distance, i) for i in range(size)])
+
+
+def in_place(own, received, mine):
+    blocks = [own, *received]
+    return jnp.stack([lax.select_n(mine, *[blocks[j ^ m] for m in range(4)]) for j in range(4)])
+
+
+def exchange(pieces, axis, size, unit):
+    mine = (lax.axis_index(axis) // unit) % 4
+    kept, *sent = [lax.dynamic_index_in_dim(pieces, mine ^ d, 0, keepdims=False) for d in range(4)]
+    return in_place(kept, [swapped(p, axis, size, (d + 1) * unit) for d, p in enumerate(sent)], mine)
+
+
+def collected(block, axis, size, unit):
+    mine = (lax.axis_index(axis) // unit) % 4
+    return in_place(block, [swapped(block, axis, size, d * unit) for d in (1, 2, 3)], mine)
 
 
 def partition_table(cell_nodes, send_list, potential, cell_scale, node_count):
@@ -129,11 +149,14 @@
     def misc(c):
         return table[:, MISC_AT * 128 + CELLS + c : MISC_AT * 128 + CELLS + c + 1]
 
-    few = (jnp.max(misc(1)).astype(jnp.int32) <= FEW * 128) & (jnp.min(misc(1)).astype(jnp.int32) >= SKIP * 128)
-    long_runs = jnp.max(misc(2)).astype(jnp.int32) > SHORT_RUN
-
+    short = jnp.max(misc(1)).astype(jnp.int32) <= FEW * 128
+    short &= jnp.min(misc(1)).astype(jnp.int32) >= SKIP * 128
+    short &= jnp.max(misc(2)).astype(jnp.int32) <= SHORT_RUN
+
+    quarter = NODES // 4
     if last:
-        cur[...] = start[...]
+        for q in range(4):
+            cur[:, q * quarter : (q + 1) * quarter] = start[q * 32 : (q + 1) * 32, :]
     else:
         live = misc(0).astype(jnp.int32)
         node = lax.broadcasted_iota(jnp.int32, (PARTS, NODES), 1)
@@ -160,66 +183,77 @@
             for k in range(CELL_CHUNKS)
         ]
 
-    def pick_into_w(r, sources, first, stop):
+    def into_order(r, sources, first, stop):
         for q in range(first, stop):
             w[r, chunk(q)] = picked(sources, pos[r, chunk(q)])
 
-    def doubling(r, stop, distances):
-        for d in distances:
-            back = (lane - d) & 127
-            for q in range(stop):
-                x = w[r, chunk(q)]
-                near = jnp.minimum(place[r, chunk(q)], lane) >= d
-                w[r, chunk(q)] = x + jnp.where(near, jnp.take_along_axis(x, back, axis=1), 0.0)
-
-    def run_sums(r, stop):
-        xs = [w[r, chunk(q)] for q in range(stop)]
-        at = [jnp.minimum(place[r, chunk(q)], lane) for q in range(stop)]
-        d = 1
-        while d < SHORT_RUN:
+    def partial_runs(places, longest):
+        xs = [w[r, chunk(q)] for r, q in places]
+        near = [jnp.minimum(place[r, chunk(q)], lane) for r, q in places]
+        for d in [1 << k for k in range(7) if (1 << k) < longest]:
             back = (lane - d) & 127
             moved = [jnp.take_along_axis(x, back, axis=1) for x in xs]
-            xs = [x + jnp.where(a >= d, m, 0.0) for x, a, m in zip(xs, at, moved)]
-            d *= 2
-        for q in range(stop):
-            w[r, chunk(q)] = xs[q]
-
-        @pl.when(long_runs)
-        def _():
-            doubling(r, stop, (16, 32, 64))
-
+            xs = [x + jnp.where(a >= d, m, 0.0) for x, a, m in zip(xs, near, moved)]
+        for (r, q), x in zip(places, xs):
+            w[r, chunk(q)] = x
+
+    def joined_runs(r, first, stop):
+        xs = [w[r, chunk(q)] for q in range(first, stop)]
+        done = [(first, xs[0])]
+        for q, x, before in zip(range(first + 1, stop), xs[1:], xs):
+            carry = jnp.take_along_axis(before, last_lane, axis=1)
+            done.append((q, x + jnp.where(place[r, chunk(q)] > lane, carry, 0.0)))
+        return done
+
+    def chained_runs(r):
         carry = jnp.zeros((8, 128), jnp.float32)
-        for q in range(stop):
+        done = []
+        for q in range(ENTRY_CHUNKS):
             x = w[r, chunk(q)]
             total = jnp.take_along_axis(x, last_lane, axis=1)
             goes_on = place[r, chunk(q)] > lane
             through = jnp.take_along_axis(jnp.where(goes_on, 1.0, 0.0), last_lane, axis=1)
-            w[r, chunk(q)] = x + jnp.where(goes_on, carry, 0.0)
+            done.append((q, x + jnp.where(goes_on, carry, 0.0)))
             carry = total + through * carry
-
-    def run_ends(r, first, stop, node_first, node_count, dest):
-        sources = [(q, w[r, chunk(q)]) for q in range(first, stop)]
+        return done
+
+    def run_ends(r, sources, node_first, node_count):
         for n in range(node_count):
-            dest[r, chunk(n)] = picked(sources, end[r, chunk(node_first + n)])
-
-    def ghost_sums(stop):
-        def picks(g, r):
-            pick_into_w(r, products_of(g), 0, stop)
-            run_sums(r, stop)
-            run_ends(r, 0, stop, 0, 4, sums)
-
-        over_groups(picks)
-
-    def own_sums(first):
-        def picks(g, r):
-            sources = products_of(g)
-            base = CELLS * CELL_CHUNKS
-            sources += [(base + k, arrived[r, chunk(k)]) for k in range(4)]
-            pick_into_w(r, sources, first, ENTRY_CHUNKS)
-
-        over_groups(picks)
-        over_groups(lambda g, r: run_sums(r, ENTRY_CHUNKS))
-        over_groups(lambda g, r: run_ends(r, first, ENTRY_CHUNKS, 4, 16, sums))
+            sums[r, chunk(n)] = picked(sources, end[r, chunk(node_first + n)])
+
+    def with_arrivals(g, r):
+        base = CELLS * CELL_CHUNKS
+        return products_of(g) + [(base + k, arrived[r, chunk(k)]) for k in range(4)]
+
+    fixed = [pl.ds(g * 8, 8) for g in range(GROUPS)]
+
+    def in_order_and_summed(sources_of):
+        def at(g, r):
+            into_order(r, sources_of(g, r), 0, ENTRY_CHUNKS)
+            partial_runs([(r, q) for q in range(ENTRY_CHUNKS)], 128)
+
+        over_groups(at)
+
+    def ghost_sums():
+        for g, r in enumerate(fixed):
+            into_order(r, products_of(g), 0, FEW)
+        partial_runs([(r, q) for r in fixed for q in range(FEW)], SHORT_RUN)
+        for r in fixed:
+            run_ends(r, joined_runs(r, 0, FEW), 0, 4)
+
+    def ghost_sums_any():
+        in_order_and_summed(lambda g, r: products_of(g))
+        over_groups(lambda g, r: run_ends(r, chained_runs(r), 0, 4))
+
+    def own_sums():
+        over_groups(lambda g, r: into_order(r, with_arrivals(g, r), SKIP, ENTRY_CHUNKS))
+        for r in fixed:
+            partial_runs([(r, q) for q in range(SKIP, ENTRY_CHUNKS)], SHORT_RUN)
+        over_groups(lambda g, r: run_ends(r, joined_runs(r, SKIP, ENTRY_CHUNKS), 4, 16))
+
+    def own_sums_any():
+        in_order_and_summed(with_arrivals)
+        over_groups(lambda g, r: run_ends(r, chained_runs(r), 4, 16))
 
     def apply():
         def outgoing(g, r):
@@ -227,7 +261,8 @@
             for k in range(4):
                 sums[r, chunk(k)] = picked(sources, send[r, chunk(k)])
 
-        over_groups(outgoing)
+        for g in range(GROUPS):
+            outgoing(g, pl.ds(g * 8, 8))
         for k in range(4):
             wrap(sums[:, k * 128 : (k + 1) * 128], k)
         for k, o in enumerate(OFFSETS):
@@ -237,16 +272,10 @@
         def gather(g, r):
             sources = [(j, ext[r, chunk(j)]) for j in range(EXT // 128)]
 
-            def some_cells(b, _):
-                for u in range(4):
-                    c = b * 4 + u
-                    for k in range(CELL_CHUNKS):
-                        here = pl.ds(pl.multiple_of(c * NPC_PAD + k * 128, 128), 128)
-                        there = pl.ds(pl.multiple_of(c * 32 + g * 8, 8), 8)
-                        vals[there, chunk(k)] = picked(sources, idx[r, here])
-                return 0
-
-            lax.fori_loop(0, 2, some_cells, 0)
+            for c in range(CELLS):
+                there = pl.ds(pl.multiple_of(c * 32 + g * 8, 8), 8)
+                for k in range(CELL_CHUNKS):
+                    vals[there, chunk(k)] = picked(sources, idx[r, chunk(c * CELL_CHUNKS + k)])
 
         over_groups(gather)
 
@@ -261,15 +290,15 @@
         for k in range(CELL_CHUNKS):
             prod[:, k * 128 : (k + 1) * 128] = y[:, k * 128 : (k + 1) * 128] * scale[...]
 
-        pl.when(few)(lambda: ghost_sums(FEW))
-        pl.when(~few)(lambda: ghost_sums(ENTRY_CHUNKS))
+        pl.when(short)(ghost_sums)
+        pl.when(~short)(ghost_sums_any)
         for k in range(4):
             wrap(sums[:, k * 128 : (k + 1) * 128], k)
         for k, o in enumerate(OFFSETS):
             arrived[:, k * 128 : (k + 1) * 128] = halo[2 - o : 34 - o, k * 128 : (k + 1) * 128]
 
-        pl.when(few)(lambda: own_sums(SKIP))
-        pl.when(~few)(lambda: own_sums(0))
+        pl.when(short)(own_sums)
+        pl.when(~short)(own_sums_any)
 
     def step(i, _):
         apply()
@@ -290,10 +319,11 @@
     if last:
         apply()
         for c in range(NODES // 128):
-            out[:, chunk(c)] = sums[:, chunk(c)] + table[:, chunk(POT_AT + c)] * cur[:, chunk(c)]
+            cur[:, chunk(c)] = sums[:, chunk(c)] + table[:, chunk(POT_AT + c)] * cur[:, chunk(c)]
     else:
         lax.fori_loop(0, step_count, step, 0)
-        out[...] = cur[...]
+    for q in range(4):
+        out[q * 32 : (q + 1) * 32, :] = cur[:, q * quarter : (q + 1) * quarter]
 
 
 def run_filter(coef, table, start, cell_matrix, step_count, last):
@@ -303,7 +333,7 @@
     cells = CELLS * PARTS
     return pl.pallas_call(
         functools.partial(filter_kernel, step_count, last),
-        out_shape=jax.ShapeDtypeStruct((PARTS, NODES), f32),
+        out_shape=jax.ShapeDtypeStruct((4 * PARTS, NODES // 4), f32),
         in_specs=[pl.BlockSpec(memory_space=pltpu.SMEM)] + [vmem] * 3,
         out_specs=vmem,
         scratch_shapes=[
@@ -326,6 +356,9 @@
             pltpu.VMEM((PARTS, NODES), f32),
         ],
         compiler_params=pltpu.CompilerParams(vmem_limit_bytes=48 * 1024 * 1024),
+        cost_estimate=pl.CostEstimate(
+            flops=step_count * 15_000_000_000, bytes_accessed=step_count * 50_000_000, transcendentals=0
+        ),
     )(coef, table, start, padded)
 
 
@@ -345,32 +378,42 @@
 
 
 def body(vectors, potential, cell_scale, cell_matrix, cell_nodes, send_list, node_count, filter_bounds):
+    start = lax.all_to_all(vectors, "mesh", 0, 0, tiled=True)
     own_table = partition_table(cell_nodes, send_list[0], potential, cell_scale, node_count)
-    table = spread(own_table, "mesh", PARTS, (8, 16))
+    own_table, start = lax.optimization_barrier((own_table, start))
+    table = collected(own_table, "mesh", PARTS, 8)
     table = spread(table, "mesh", PARTS, (2, 4))
     table = spread(table, "mesh", PARTS, (1,))
     table = table.transpose(2, 1, 0, 3, 4).reshape(PARTS, TABLE_CHUNKS * 128)
 
-    start = lax.all_to_all(vectors, "mesh", 0, 0, tiled=True)
     coef = coefficients(filter_bounds)
+    quarters = groups_of(16 * PARTS, (1, 2, 4, 8, 16, PARTS, 2 * PARTS))
+
+    def to_quarters(field):
+        pieces = field.reshape(4 * PARTS, NODES // 512, 128)
+        pieces = lax.all_to_all(pieces, ("band", "mesh"), 0, 0, axis_index_groups=quarters)
+        return pieces.reshape(4 * PARTS, NODES // 4)
+
     f = run_filter(coef, table, start, cell_matrix, 2 * DEGREE, False)
+    f_quarter = to_quarters(f)
     g = run_filter(coef, table, f, cell_matrix, 1, True)
-    filtered = lax.all_to_all(f, "mesh", 0, 0, tiled=True)
-    applied = lax.all_to_all(g, "mesh", 0, 0, tiled=True)
-
-    band_rows = filtered.shape[0]
-    z_lo = groups_of(16, (1, 2))
-    both = jnp.stack([filtered, applied]).reshape(2, band_rows, 4, NODES // 4)
-    both = lax.all_to_all(both.transpose(2, 0, 1, 3), "band", 0, 0, axis_index_groups=z_lo)
-    right = both[:, 0].reshape(4 * band_rows, NODES // 4)
-    left = both[:, 1].reshape(4 * band_rows, NODES // 4)
-    right = spread(right, "band", 16, (4, 8)).reshape(16 * band_rows, NODES // 4)
+    left = to_quarters(g)
+    band_rows = vectors.shape[0]
+    filtered = exchange(f_quarter.reshape(4, band_rows, NODES // 4), "band", 16, 1)
+    filtered = filtered.transpose(1, 0, 2).reshape(band_rows, NODES)
+
+    right = collected(f_quarter, "band", 16, 4).reshape(16 * band_rows, NODES // 4)
     partial = lax.dot_general(left, right, (((1,), (1,)), ((), ())), precision=HIGHEST)
-    partial = partial.reshape(4, band_rows, 16 * band_rows)
-    partial = lax.all_to_all(partial, "band", 0, 0, axis_index_groups=z_lo).sum(0)
-    row = lax.all_to_all(partial, "mesh", 0, 0, tiled=True).sum(0, keepdims=True)
-    row = row / (NODES * PARTS)
-    hproj = lax.all_to_all(jnp.broadcast_to(row, partial.shape), "mesh", 0, 0, tiled=True)
+
+    plane = groups_of(PARTS, (1, 2, 4))
+    partial = partial.reshape(4, 8, band_rows // 8, 16 * band_rows).transpose(1, 0, 2, 3)
+    partial = lax.all_to_all(partial, "mesh", 0, 0, axis_index_groups=plane).sum(0)
+    along_z = groups_of(16 * PARTS, (8, 16, PARTS, 2 * PARTS))
+    partial = jnp.broadcast_to(partial[:, None], (4, 4) + partial.shape[1:])
+    partial = partial.reshape((16,) + partial.shape[2:])
+    block = lax.all_to_all(partial, ("band", "mesh"), 0, 0, axis_index_groups=along_z).sum(0)
+    block = block / (NODES * PARTS)
+    hproj = spread(block, "mesh", PARTS, (1, 2, 4)).reshape(band_rows, 16 * band_rows)
     return filtered, hproj
 
 

time: 360 us -> 282 us (0.78)
  blocking collectives: 75.7 us -> 18.6 us
  starting transfers between devices: 52.3 us -> 100 us
  waiting for transfers between devices: 90.7 us -> 45.2 us
  Pallas kernels: 103 us -> 80.8 us
    all_to_all x3 -> x1, blocking collectives: 52.8 us -> 11.8 us  [body(): lax.all_to_all(partial, 'mesh', 0, 0, axis_index_groups=plane).sum(0)]
    ppermute x0 -> x9, starting transfers between devices: none -> 35 us  [swapped(): return lax.ppermute(block, axis, [(i ^ distance, i) for i in range(size)])]
    all_to_all x3, waiting for transfers between devices: 48.5 us -> 17.1 us  [the longest x2 17.1 us: to_quarters(): lax.all_to_all(pieces, ('band', 'mesh'), 0, 0, axis_index_groups=quarters)]
    pallas_call x2, Pallas kernels: 103 us -> 80.8 us  [run_filter(): pl.pallas_call(functools.partial(filter_kernel, step_count, last), out_sh...]
    all_to_all x1, waiting for transfers between devices: 20.5 us -> 0.47 us  [body(): start = lax.all_to_all(vectors, 'mesh', 0, 0, tiled=True)]
    all_to_all x2 -> x1, blocking collectives: 22.9 us -> 6.79 us  [spread(): return lax.all_to_all(copies, axis, 0, 0, axis_index_groups=members)]
    ppermute x0 -> x9, waiting for transfers between devices: none -> 14.8 us  [swapped(): return lax.ppermute(block, axis, [(i ^ distance, i) for i in range(size)])]
    all_to_all x3, starting transfers between devices: 19.6 us -> 33.5 us  [the longest x2 22.2 us: to_quarters(): lax.all_to_all(pieces, ('band', 'mesh'), 0, 0, axis_index_groups=quarters)]
  transfers between devices with their start and end apart: 6 -> 15, of which waited for: 6 -> 10; matrix products, arithmetic and copies ran while one was open for 1% -> 8% of each run, Pallas kernels for 0% -> 4%
where the time goes in v3:
time: 282 us; the launch traced here: 281 us
  starting transfers between devices  100 us (35%)
  Pallas kernels  80.8 us (29%)
  waiting for transfers between devices  45.2 us (16%)
  blocking collectives  18.6 us (7%)
  other arithmetic  17.5 us (6%)
  local copies, waits for them, and re-layouts  12 us (4%)
  between operations  5.84 us (2%)
    pallas_call x2, Pallas kernels, run_filter(): pl.pallas_call(functools.partial(filter_kernel, step_count, last), out_sh...  80.8 us
    ppermute x9, starting transfers between devices, swapped(): return lax.ppermute(block, axis, [(i ^ distance, i) for i in range(size)])  35 us
    all_to_all x2, starting transfers between devices, to_quarters(): lax.all_to_all(pieces, ('band', 'mesh'), 0, 0, axis_index_groups=quarters)  22.2 us
    all_to_all x1, starting transfers between devices, body(): start = lax.all_to_all(vectors, 'mesh', 0, 0, tiled=True)  19.4 us
    all_to_all x2, waiting for transfers between devices, to_quarters(): lax.all_to_all(pieces, ('band', 'mesh'), 0, 0, axis_index_groups=quarters)  17.1 us
    ppermute x9, waiting for transfers between devices, swapped(): return lax.ppermute(block, axis, [(i ^ distance, i) for i in range(size)])  14.8 us
    all_to_all x2, waiting for transfers between devices, spread(): return lax.all_to_all(copies, axis, 0, 0, axis_index_groups=members)  12.9 us
    all_to_all x2, starting transfers between devices, spread(): return lax.all_to_all(copies, axis, 0, 0, axis_index_groups=members)  12.4 us
  transfers between devices with their start and end apart: 15, of which 10 were waited for; matrix products, arithmetic and copies ran while one was open for 8% of the time, Pallas kernels for 4%

profile of v3, /device:TPU:1, one launch (start us, length us, event | category | flops | bytes accessed | tf_op | source)
XLA Modules:
  0.0 281.4 jit_solution(7761394190596270173)
XLA Ops:
  0.6 1.8 all_to_all.29
  2.5 19.4 %all-to-all-start = ((f32[32,1,2048]{2,1,0:T(1,128)}), f32[32,1,2048]{2,1,0:T(1,128)S(1)}, u32[]{:S(2)}, u32[]{:S(2)}) async-start(f32[32,1,2048]{2,1,0:T(1,128)} %all_to_all.29), calls=%async_computation | async-start | bytes 524288 | tf_op jit(solution)/shard_map/all_to_all | solution.py:381
  21.8 0.7 add_select_fusion.2
  22.6 0.7 bitcast_add_fusion
  23.4 5.9 %sort.14 = (s32[3256]{0:T(1024)S(1)}, s32[3256]{0:T(1024)}) sort(s32[3256]{0:T(1024)S(1)} %get-tuple-element.29, s32[3256]{0:T(1024)S(1)} %iota.14), dimensions={0}, to_apply=%region_0.1 | sort | flops 39072 | bytes 52096 | tf_op jit(solution)/shard_map/sort | solution.py:81
  29.3 3.3 %convert_reduce_fusion.1 = s32[2560]{0:T(1024)S(1)} fusion(s32[3256]{0:T(1024)S(1)} %get-tuple-element.28), kind=kLoop, calls=%fused_computation.1 | loop fusion | flops 25003520 | bytes 23264 | tf_op jit(solution)/shard_map/reduce_sum | solution.py:87
  32.6 4.4 %convert_reduce_fusion = s32[3256]{0:T(1024)S(1)} fusion(s32[3256]{0:T(1024)S(1)} %get-tuple-element.28, s32[3256]{0:T(1024)S(1)} %get-tuple-element.26), kind=kLoop, calls=%fused_computation | loop fusion | flops 31801352 | bytes 39072 | tf_op jit(solution)/shard_map/reduce_sum | solution.py:90
  37.1 0.7 slice.21
  37.8 0.6 fusion.12
  38.5 0.7 constant_dynamic-update-slice_fusion
  40.5 0.8 add_convert_fusion
  41.2 0.8 concatenate.15
  42.6 6.7 %collective-permute-start = (f32[117,128]{1,0:T(8,128)S(1)}, f32[117,128]{1,0:T(8,128)S(1)}, u32[]{:S(2)}, u32[]{:S(2)}) collective-permute-start(f32[117,128]{1,0:T(8,128)S(1)} %bitcast.104), channel_id=1, source_target_pairs={{8,0},{9,1},{10,2},{11,3},{12,4},{13,5},{14,6},{15,7},{0,8},{1,9},... | collective-permute-start | bytes 179720 | tf_op jit(solution)/shard_map/ppermute | solution.py:56
  49.3 7.0 %collective-permute-start.1 = (f32[117,128]{1,0:T(8,128)S(1)}, f32[117,128]{1,0:T(8,128)S(1)}, u32[]{:S(2)}, u32[]{:S(2)}) collective-permute-start(f32[117,128]{1,0:T(8,128)S(1)} %bitcast.105), channel_id=1, source_target_pairs={{16,0},{17,1},{18,2},{19,3},{20,4},{21,5},{22,6},{23,7},{24,8},{25... | collective-permute-start | bytes 179720 | tf_op jit(solution)/shard_map/ppermute | solution.py:56
  56.4 2.4 collective-permute-start.2
  58.8 4.2 %collective-permute-done.1 = f32[117,128]{1,0:T(8,128)S(1)} collective-permute-done((f32[117,128]{1,0:T(8,128)S(1)}, f32[117,128]{1,0:T(8,128)S(1)}, u32[]{:S(2)}, u32[]{:S(2)}) %collective-permute-start.1) | collective-permute-done | bytes 59936 | tf_op jit(solution)/shard_map/ppermute | solution.py:56
  63.0 2.3 collective-permute-done.2
  65.9 1.1 broadcast_in_dim.13
  67.0 6.4 %all-to-all-start.1 = ((f32[4,4,117,128]{3,1,2,0:T(4,128)}), f32[4,4,117,128]{3,1,2,0:T(4,128)S(1)}, u32[]{:S(2)}, u32[]{:S(2)}) async-start(f32[4,4,117,128]{3,1,2,0:T(4,128)} %broadcast_in_dim.13), calls=%async_computation.1 | async-start | bytes 1916928 | tf_op jit(solution)/shard_map/all_to_all | solution.py:52
  73.4 0.6 fusion.13
  77.5 9.1 %all-to-all-done.1 = f32[4,4,117,128]{3,1,2,0:T(4,128)S(1)} async-done(((f32[4,4,117,128]{3,1,2,0:T(4,128)}), f32[4,4,117,128]{3,1,2,0:T(4,128)S(1)}, u32[]{:S(2)}, u32[]{:S(2)}) %all-to-all-start.1) | async-done | bytes 958496 | tf_op jit(solution)/shard_map/all_to_all | solution.py:52
  86.8 6.8 %all_to_all.47 = f32[2,4,4,117,128]{4,2,3,1,0:T(4,128)S(1)} all-to-all(f32[2,4,4,117,128]{4,2,3,1,0:T(4,128)S(1)} %broadcast_in_dim.14), channel_id=1, replica_groups={{0,1},{2,3},{4,5},{6,7},{8,9},{10,11},{12,13},{14,15},{16,17},{18,19},{..., dimensions={0} | all-to-all | bytes 3833856 | tf_op jit(solution)/shard_map/all_to_all | solution.py:52
  94.1 68.5 %shard_map.95.start = f32[128,512]{1,0:T(8,128)S(1)} custom-call(f32[8]{0:T(128)S(1)} %stack.76.coef, f32[32,14976]{1,0:T(8,128)S(1)} %bitcast.91, f32[32,2048]{1,0:T(8,128)S(1)} %bitcast.93, f32[384,384]{1,0:T(8,128)S(1)} %pad.19.matrix), custom_call_target="tpu_custom_call" | custom-call | flops 89999998976 | bytes 300000000 | tf_op jit(solution)/shard_map/pallas_call | solution.py:334
  162.7 0.8 reshape.63
  163.4 13.3 %all-to-all-start.3 = ((f32[128,4,128]{2,1,0:T(4,128)}), f32[128,4,128]{2,1,0:T(4,128)S(1)}, u32[]{:S(2)}, u32[]{:S(2)}) async-start(f32[128,4,128]{2,1,0:T(4,128)} %reshape.63), calls=%async_computation.3 | async-start | bytes 524288 | tf_op jit(solution)/shard_map/all_to_all | solution.py:394
  176.8 12.2 %shard_map.96 = f32[128,512]{1,0:T(8,128)S(1)} custom-call(f32[8]{0:T(128)S(1)} %stack.76.coef, f32[32,14976]{1,0:T(8,128)S(1)} %bitcast.92, f32[128,512]{1,0:T(8,128)S(1)} %shard_map.95.start, f32[384,384]{1,0:T(8,128)S(1)} %pad.19.matrix), custom_call_target="tpu_custom_call" | custom-call | flops 15000000512 | bytes 50000000 | tf_op jit(solution)/shard_map/pallas_call | solution.py:334
  189.0 0.8 reshape.65
  189.8 6.9 %all-to-all-done.3 = f32[128,4,128]{2,1,0:T(4,128)S(1)} async-done(((f32[128,4,128]{2,1,0:T(4,128)}), f32[128,4,128]{2,1,0:T(4,128)S(1)}, u32[]{:S(2)}, u32[]{:S(2)}) %all-to-all-start.3) | async-done | bytes 262176 | tf_op jit(solution)/shard_map/all_to_all | solution.py:394
  196.7 8.9 %all-to-all-start.4 = ((f32[128,4,128]{2,1,0:T(4,128)}), f32[128,4,128]{2,1,0:T(4,128)S(1)}, u32[]{:S(2)}, u32[]{:S(2)}) async-start(f32[128,4,128]{2,1,0:T(4,128)} %reshape.65), calls=%async_computation.4 | async-start | bytes 524288 | tf_op jit(solution)/shard_map/all_to_all | solution.py:394
  205.6 3.1 %collective-permute-start.6 = (f32[128,512]{1,0:T(8,128)S(1)}, f32[128,512]{1,0:T(8,128)S(1)}, u32[]{:S(2)}, u32[]{:S(2)}) collective-permute-start(f32[128,512]{1,0:T(8,128)S(1)} %bitcast.100), channel_id=1, source_target_pairs={{128,0},{160,32},{192,64},{224,96},{0,128},{32,160},{64,192},{96,2... | collective-permute-start | bytes 786440 | tf_op jit(solution)/shard_map/ppermute | solution.py:56
  208.7 4.4 %collective-permute-start.7 = (f32[128,512]{1,0:T(8,128)S(1)}, f32[128,512]{1,0:T(8,128)S(1)}, u32[]{:S(2)}, u32[]{:S(2)}) collective-permute-start(f32[128,512]{1,0:T(8,128)S(1)} %bitcast.101), channel_id=1, source_target_pairs={{256,0},{288,32},{320,64},{352,96},{384,128},{416,160},{448,192},{... | collective-permute-start | bytes 786440 | tf_op jit(solution)/shard_map/ppermute | solution.py:56
  213.1 2.1 collective-permute-start.8
  215.3 10.2 %all-to-all-done.4 = f32[128,4,128]{2,1,0:T(4,128)S(1)} async-done(((f32[128,4,128]{2,1,0:T(4,128)}), f32[128,4,128]{2,1,0:T(4,128)S(1)}, u32[]{:S(2)}, u32[]{:S(2)}) %all-to-all-start.4) | async-done | bytes 262176 | tf_op jit(solution)/shard_map/all_to_all | solution.py:394
  225.6 2.9 %collective-permute-done.8 = f32[128,512]{1,0:T(8,128)S(1)} collective-permute-done((f32[128,512]{1,0:T(8,128)S(1)}, f32[128,512]{1,0:T(8,128)S(1)}, u32[]{:S(2)}, u32[]{:S(2)}) %collective-permute-start.8) | collective-permute-done | bytes 262176 | tf_op jit(solution)/shard_map/ppermute | solution.py:56
  228.8 1.2 convolution_bitcast_fusion
  230.2 11.8 %all_to_all.48 = f32[8,4,4,512]{3,2,1,0:T(4,128)S(1)} all-to-all(f32[8,4,4,512]{3,2,1,0:T(4,128)S(1)} %copy.43), channel_id=1, replica_groups={{0,1,2,3,4,5,6,7},{8,9,10,11,12,13,14,15},{16,17,18,19,20,21,22,23},{24..., dimensions={0} | all-to-all | bytes 524288 | tf_op jit(solution)/shard_map/all_to_all | solution.py:410
  242.1 0.7 broadcast_in_dim.15
  242.7 11.3 %all-to-all-start.6 = ((f32[16,4,512]{2,1,0:T(4,128)}), f32[16,4,512]{2,1,0:T(4,128)S(1)}, u32[]{:S(2)}, u32[]{:S(2)}) async-start(f32[16,4,512]{2,1,0:T(4,128)} %bitcast.30), calls=%async_computation.6 | async-start | bytes 262144 | tf_op jit(solution)/shard_map/all_to_all | solution.py:414
  254.2 3.2 %collective-permute-start.3 = (f32[32,512]{1,0:T(8,128)S(1)}, f32[32,512]{1,0:T(8,128)S(1)}, u32[]{:S(2)}, u32[]{:S(2)}) collective-permute-start(f32[32,512]{1,0:T(8,128)S(1)} %get-tuple-element.19), channel_id=1, source_target_pairs={{32,0},{0,32},{96,64},{64,96},{160,128},{128,160},{224,192},{192,2... | collective-permute-start | bytes 196616 | tf_op jit(solution)/shard_map/ppermute | solution.py:56
  257.4 4.0 %collective-permute-start.4 = (f32[32,512]{1,0:T(8,128)S(1)}, f32[32,512]{1,0:T(8,128)S(1)}, u32[]{:S(2)}, u32[]{:S(2)}) collective-permute-start(f32[32,512]{1,0:T(8,128)S(1)} %get-tuple-element.17), channel_id=1, source_target_pairs={{64,0},{96,32},{0,64},{32,96},{192,128},{224,160},{128,192},{160,2... | collective-permute-start | bytes 196616 | tf_op jit(solution)/shard_map/ppermute | solution.py:56
  261.4 2.0 collective-permute-start.5
  263.5 1.0 collective-permute-done.4
  264.5 4.3 %collective-permute-done.5 = f32[32,512]{1,0:T(8,128)S(1)} collective-permute-done((f32[32,512]{1,0:T(8,128)S(1)}, f32[32,512]{1,0:T(8,128)S(1)}, u32[]{:S(2)}, u32[]{:S(2)}) %collective-permute-start.5) | collective-permute-done | bytes 65568 | tf_op jit(solution)/shard_map/ppermute | solution.py:56
  269.2 0.6 broadcast_in_dim.16
  269.8 6.0 %all-to-all-start.7 = ((f32[8,4,512]{2,1,0:T(4,128)}), f32[8,4,512]{2,1,0:T(4,128)S(1)}, u32[]{:S(2)}, u32[]{:S(2)}) async-start(f32[8,4,512]{2,1,0:T(4,128)} %broadcast_in_dim.16), calls=%async_computation.7 | async-start | bytes 131072 | tf_op jit(solution)/shard_map/all_to_all | solution.py:52
  276.1 0.8 copy.49
  276.9 3.8 %all-to-all-done.7 = f32[8,4,512]{2,1,0:T(4,128)S(1)} async-done(((f32[8,4,512]{2,1,0:T(4,128)}), f32[8,4,512]{2,1,0:T(4,128)S(1)}, u32[]{:S(2)}, u32[]{:S(2)}) %all-to-all-start.7) | async-done | bytes 65568 | tf_op jit(solution)/shard_map/all_to_all | solution.py:52
  280.7 0.7 reshape.69
  (50 shorter events, 3.6 us)
Async XLA Ops:
  2.5 40.0 %all-to-all-start = ((f32[32,1,2048]{2,1,0:T(1,128)}), f32[32,1,2048]{2,1,0:T(1,128)S(1)}, u32[]{:S(2)}, u32[]{:S(2)}) async-start(f32[32,1,2048]{2,1,0:T(1,128)} %all_to_all.29), calls=%async_computation | async-start | bytes 524288 | tf_op jit(solution)/shard_map/all_to_all | solution.py:381
  42.6 16.2 %collective-permute-start = (f32[117,128]{1,0:T(8,128)S(1)}, f32[117,128]{1,0:T(8,128)S(1)}, u32[]{:S(2)}, u32[]{:S(2)}) collective-permute-start(f32[117,128]{1,0:T(8,128)S(1)} %bitcast.104), channel_id=1, source_target_pairs={{8,0},{9,1},{10,2},{11,3},{12,4},{13,5},{14,6},{15,7},{0,8},{1,9},... | collective-permute-start | bytes 179720 | tf_op jit(solution)/shard_map/ppermute | solution.py:56
  49.3 13.7 %collective-permute-start.1 = (f32[117,128]{1,0:T(8,128)S(1)}, f32[117,128]{1,0:T(8,128)S(1)}, u32[]{:S(2)}, u32[]{:S(2)}) collective-permute-start(f32[117,128]{1,0:T(8,128)S(1)} %bitcast.105), channel_id=1, source_target_pairs={{16,0},{17,1},{18,2},{19,3},{20,4},{21,5},{22,6},{23,7},{24,8},{25... | collective-permute-start | bytes 179720 | tf_op jit(solution)/shard_map/ppermute | solution.py:56
  56.4 9.0 %collective-permute-start.2 = (f32[117,128]{1,0:T(8,128)S(1)}, f32[117,128]{1,0:T(8,128)S(1)}, u32[]{:S(2)}, u32[]{:S(2)}) collective-permute-start(f32[117,128]{1,0:T(8,128)S(1)} %bitcast.106), channel_id=1, source_target_pairs={{24,0},{25,1},{26,2},{27,3},{28,4},{29,5},{30,6},{31,7},{16,8},{17... | collective-permute-start | bytes 179720 | tf_op jit(solution)/shard_map/ppermute | solution.py:56
  65.4 8.0 %copy-start.1 = (f32[3]{0:T(128)S(1)}, f32[3]{0:T(128)}, u32[]{:S(2)}) copy-start(f32[3]{0:T(128)} %param.15) | copy-start | bytes 40
  65.5 11.8 %copy-start = (f32[343,343]{1,0:T(8,128)S(1)}, f32[343,343]{1,0:T(8,128)}, u32[]{:S(2)}) copy-start(f32[343,343]{1,0:T(8,128)} %param.11) | copy-start | bytes 1411792
  67.0 19.6 %all-to-all-start.1 = ((f32[4,4,117,128]{3,1,2,0:T(4,128)}), f32[4,4,117,128]{3,1,2,0:T(4,128)S(1)}, u32[]{:S(2)}, u32[]{:S(2)}) async-start(f32[4,4,117,128]{3,1,2,0:T(4,128)} %broadcast_in_dim.13), calls=%async_computation.1 | async-start | bytes 1916928 | tf_op jit(solution)/shard_map/all_to_all | solution.py:52
  163.4 33.2 %all-to-all-start.3 = ((f32[128,4,128]{2,1,0:T(4,128)}), f32[128,4,128]{2,1,0:T(4,128)S(1)}, u32[]{:S(2)}, u32[]{:S(2)}) async-start(f32[128,4,128]{2,1,0:T(4,128)} %reshape.63), calls=%async_computation.3 | async-start | bytes 524288 | tf_op jit(solution)/shard_map/all_to_all | solution.py:394
  196.7 28.8 %all-to-all-start.4 = ((f32[128,4,128]{2,1,0:T(4,128)}), f32[128,4,128]{2,1,0:T(4,128)S(1)}, u32[]{:S(2)}, u32[]{:S(2)}) async-start(f32[128,4,128]{2,1,0:T(4,128)} %reshape.65), calls=%async_computation.4 | async-start | bytes 524288 | tf_op jit(solution)/shard_map/all_to_all | solution.py:394
  205.6 20.0 %collective-permute-start.6 = (f32[128,512]{1,0:T(8,128)S(1)}, f32[128,512]{1,0:T(8,128)S(1)}, u32[]{:S(2)}, u32[]{:S(2)}) collective-permute-start(f32[128,512]{1,0:T(8,128)S(1)} %bitcast.100), channel_id=1, source_target_pairs={{128,0},{160,32},{192,64},{224,96},{0,128},{32,160},{64,192},{96,2... | collective-permute-start | bytes 786440 | tf_op jit(solution)/shard_map/ppermute | solution.py:56
  208.7 16.9 %collective-permute-start.7 = (f32[128,512]{1,0:T(8,128)S(1)}, f32[128,512]{1,0:T(8,128)S(1)}, u32[]{:S(2)}, u32[]{:S(2)}) collective-permute-start(f32[128,512]{1,0:T(8,128)S(1)} %bitcast.101), channel_id=1, source_target_pairs={{256,0},{288,32},{320,64},{352,96},{384,128},{416,160},{448,192},{... | collective-permute-start | bytes 786440 | tf_op jit(solution)/shard_map/ppermute | solution.py:56
  213.1 15.5 %collective-permute-start.8 = (f32[128,512]{1,0:T(8,128)S(1)}, f32[128,512]{1,0:T(8,128)S(1)}, u32[]{:S(2)}, u32[]{:S(2)}) collective-permute-start(f32[128,512]{1,0:T(8,128)S(1)} %bitcast.102), channel_id=1, source_target_pairs={{384,0},{416,32},{448,64},{480,96},{256,128},{288,160},{320,192},{... | collective-permute-start | bytes 786440 | tf_op jit(solution)/shard_map/ppermute | solution.py:56
  242.7 26.4 %all-to-all-start.6 = ((f32[16,4,512]{2,1,0:T(4,128)}), f32[16,4,512]{2,1,0:T(4,128)S(1)}, u32[]{:S(2)}, u32[]{:S(2)}) async-start(f32[16,4,512]{2,1,0:T(4,128)} %bitcast.30), calls=%async_computation.6 | async-start | bytes 262144 | tf_op jit(solution)/shard_map/all_to_all | solution.py:414
  254.2 9.3 %collective-permute-start.3 = (f32[32,512]{1,0:T(8,128)S(1)}, f32[32,512]{1,0:T(8,128)S(1)}, u32[]{:S(2)}, u32[]{:S(2)}) collective-permute-start(f32[32,512]{1,0:T(8,128)S(1)} %get-tuple-element.19), channel_id=1, source_target_pairs={{32,0},{0,32},{96,64},{64,96},{160,128},{128,160},{224,192},{192,2... | collective-permute-start | bytes 196616 | tf_op jit(solution)/shard_map/ppermute | solution.py:56
  257.4 7.1 %collective-permute-start.4 = (f32[32,512]{1,0:T(8,128)S(1)}, f32[32,512]{1,0:T(8,128)S(1)}, u32[]{:S(2)}, u32[]{:S(2)}) collective-permute-start(f32[32,512]{1,0:T(8,128)S(1)} %get-tuple-element.17), channel_id=1, source_target_pairs={{64,0},{96,32},{0,64},{32,96},{192,128},{224,160},{128,192},{160,2... | collective-permute-start | bytes 196616 | tf_op jit(solution)/shard_map/ppermute | solution.py:56
  261.4 7.4 %collective-permute-start.5 = (f32[32,512]{1,0:T(8,128)S(1)}, f32[32,512]{1,0:T(8,128)S(1)}, u32[]{:S(2)}, u32[]{:S(2)}) collective-permute-start(f32[32,512]{1,0:T(8,128)S(1)} %get-tuple-element.18), channel_id=1, source_target_pairs={{96,0},{64,32},{32,64},{0,96},{224,128},{192,160},{160,192},{128,2... | collective-permute-start | bytes 196616 | tf_op jit(solution)/shard_map/ppermute | solution.py:56
  269.8 10.9 %all-to-all-start.7 = ((f32[8,4,512]{2,1,0:T(4,128)}), f32[8,4,512]{2,1,0:T(4,128)S(1)}, u32[]{:S(2)}, u32[]{:S(2)}) async-start(f32[8,4,512]{2,1,0:T(4,128)} %broadcast_in_dim.16), calls=%async_computation.7 | async-start | bytes 131072 | tf_op jit(solution)/shard_map/all_to_all | solution.py:52

commit v4 on v3

--- a/solution.py
+++ b/solution.py
@@ -24,9 +24,15 @@
 ENTRIES = CELLS * NPC + GHOSTS
 ENTRY_CHUNKS = 26
 ENTRY_PAD = ENTRY_CHUNKS * 128
+PAD_NODE = 4095
+CELL_MULTIPLIER, CELL_SHIFT = 6115, 21
 FEW = 5
 SKIP = 3
 SHORT_RUN = 16
+WINDOWS = (
+    (3, 8), (4, 11), (6, 13), (7, 16), (8, 19), (10, 21), (11, 24), (12, 26),
+    (13, 26), (15, 26), (16, 26), (18, 26), (19, 26), (20, 26), (22, 26), (23, 26),
+)
 
 IDX_AT = 0
 POS_AT = IDX_AT + CELLS * CELL_CHUNKS
@@ -35,7 +41,8 @@
 SEND_AT = END_AT + EXT // 128
 POT_AT = SEND_AT + GHOSTS // 128
 MISC_AT = POT_AT + NODES // 128
-TABLE_CHUNKS = MISC_AT + 1
+START_AT = MISC_AT + 4
+TABLE_CHUNKS = START_AT + NODES // 128
 
 
 def groups_of(size, bits):
@@ -56,50 +63,115 @@
     return lax.ppermute(block, axis, [(i ^ distance, i) for i in range(size)])
 
 
-def in_place(own, received, mine):
-    blocks = [own, *received]
+def in_place(blocks, mine):
     return jnp.stack([lax.select_n(mine, *[blocks[j ^ m] for m in range(4)]) for j in range(4)])
 
 
 def exchange(pieces, axis, size, unit):
     mine = (lax.axis_index(axis) // unit) % 4
     kept, *sent = [lax.dynamic_index_in_dim(pieces, mine ^ d, 0, keepdims=False) for d in range(4)]
-    return in_place(kept, [swapped(p, axis, size, (d + 1) * unit) for d, p in enumerate(sent)], mine)
+    return [kept] + [swapped(p, axis, size, (d + 1) * unit) for d, p in enumerate(sent)], mine
 
 
 def collected(block, axis, size, unit):
     mine = (lax.axis_index(axis) // unit) % 4
-    return in_place(block, [swapped(block, axis, size, d * unit) for d in (1, 2, 3)], mine)
+    received = [swapped(block, axis, size, d * unit) for d in (1, 2, 3)]
+    return in_place([block] + received, mine), received
+
+
+def table_kernel(ordered, slots, send, pot, cell_scale, node_count, out, hot_high, hot_low):
+    shape = (32, 128)
+    row = lax.broadcasted_iota(jnp.int32, shape, 0)
+    lane = lax.broadcasted_iota(jnp.int32, shape, 1)
+    order = row * 128 + lane
+    valid = order < ENTRIES
+    entry = ordered[...] & 4095
+    node = ordered[...] >> 12
+
+    def along_rows(x, combine):
+        for d in (1, 2, 4, 8, 16, 32, 64):
+            x = jnp.where(lane >= d, combine(x, pltpu.roll(x, d, 1)), x)
+        ends = jnp.broadcast_to(x[:, 127:128], shape)
+        before = jnp.where(row >= 1, pltpu.roll(ends, 1, 0), 0.0)
+        for d in (1, 2, 4, 8, 16):
+            before = jnp.where(row >= d, combine(before, pltpu.roll(before, d, 0)), before)
+        return combine(x, before)
+
+    key = node.astype(jnp.float32)
+    shifted = pltpu.roll(key, 1, 1)
+    previous = jnp.where(lane == 0, pltpu.roll(shifted, 1, 0), shifted)
+    head = (previous != key) | (order == 0)
+    at = order.astype(jnp.float32)
+    first = along_rows(jnp.where(head, at, 0.0), jnp.maximum)
+    place = jnp.where(valid, at - first, 0.0)
+
+    cell = (entry * CELL_MULTIPLIER) >> CELL_SHIFT
+    position = entry + jnp.where(entry < CELLS * NPC, cell, CELLS) * (NPC_PAD - NPC)
+    position = jnp.where(valid, position, 0).astype(jnp.float32)
+
+    high_row = lax.broadcasted_iota(jnp.int32, (32, 128), 0)
+    low_row = lax.broadcasted_iota(jnp.int32, (128, 128), 0)
+    for q in range(ENTRY_CHUNKS):
+        some = node[q : q + 1, :]
+        hot_high[:, chunk(q)] = jnp.where(high_row == (some >> 7), 1.0, 0.0).astype(jnp.bfloat16)
+        hot_low[:, chunk(q)] = jnp.where(low_row == (some & 127), 1.0, 0.0).astype(jnp.bfloat16)
+    count = lax.dot_general(
+        hot_high[...], hot_low[...], (((1,), (1,)), ((), ())), preferred_element_type=jnp.float32
+    )
+    up_to = along_rows(count, jnp.add)
+    end = jnp.where(count > 0.0, up_to - 1.0, -1.0)
+
+    nodes = slots[...]
+    nodes = jnp.where(nodes >= NODES, nodes - NODES, nodes + GHOSTS)
+    out[IDX_AT:POS_AT, :] = nodes.astype(jnp.float32)
+    out[POS_AT:PLACE_AT, :] = position[:ENTRY_CHUNKS]
+    out[PLACE_AT:END_AT, :] = place[:ENTRY_CHUNKS]
+    out[END_AT:SEND_AT, :] = end[: EXT // 128]
+    out[SEND_AT:POT_AT, :] = send[...].astype(jnp.float32)
+    out[POT_AT:MISC_AT, :] = pot[...]
+    ghost_entries = jnp.broadcast_to(up_to[GHOSTS // 128 - 1 : GHOSTS // 128, 127:128], (1, 128))
+    longest = jnp.max(place) + 1.0
+    one_lane = lane[:1]
+    misc = jnp.where(one_lane == CELLS, node_count[0].astype(jnp.float32), 0.0)
+    misc = jnp.where(one_lane == CELLS + 1, ghost_entries, misc)
+    misc = jnp.where(one_lane == CELLS + 2, longest, misc)
+    out[MISC_AT : MISC_AT + 1, :] = misc
+    out[MISC_AT : MISC_AT + 1, 0:CELLS] = cell_scale[...]
+    out[MISC_AT + 1 :, :] = jnp.zeros((START_AT - MISC_AT - 1, 128), jnp.float32)
 
 
 def partition_table(cell_nodes, send_list, potential, cell_scale, node_count):
     shifted = jnp.where(cell_nodes >= NODES, cell_nodes - NODES, cell_nodes + GHOSTS)
-    slots = jnp.pad(shifted, ((0, 0), (0, NPC_PAD - NPC))).reshape(-1)
-    send = send_list.reshape(-1)
-    keys = jnp.concatenate([shifted.reshape(-1), send + GHOSTS])
-    tagged = keys * 4096 + lax.iota(jnp.int32, ENTRIES)
-    ordered = lax.sort(tagged)
-    entry = ordered & 4095
-    sorted_key = ordered >> 12
-    from_slot = (entry // NPC) * NPC_PAD + entry % NPC
-    position = jnp.where(entry < CELLS * NPC, from_slot, entry + (CELLS * NPC_PAD - CELLS * NPC))
-    nodes = lax.iota(jnp.int32, EXT)
-    up_to = jnp.sum((keys[None, :] <= nodes[:, None]).astype(jnp.int32), axis=1)
-    before = jnp.concatenate([jnp.zeros((1,), jnp.int32), up_to[:-1]])
-    end = jnp.where(up_to > before, up_to - 1, -1)
-    first = jnp.sum((keys[None, :] < sorted_key[:, None]).astype(jnp.int32), axis=1)
-    place = lax.iota(jnp.int32, ENTRIES) - first
-    longest = jnp.max(place) + 1
-    ghost_entries = up_to[GHOSTS - 1]
-    place = jnp.pad(place, (0, ENTRY_PAD - ENTRIES))
-    position = jnp.pad(position, (0, ENTRY_PAD - ENTRIES))
-    misc = jnp.concatenate([
-        cell_scale,
-        jnp.stack([node_count[0], ghost_entries, longest]).astype(jnp.float32),
-        jnp.zeros((117,), jnp.float32),
-    ])
-    ints = jnp.concatenate([slots, position, place, end, send]).astype(jnp.float32)
-    return jnp.concatenate([ints, potential, misc]).reshape(TABLE_CHUNKS, 128)
+    keys = jnp.concatenate([shifted.reshape(-1), send_list.reshape(-1) + GHOSTS])
+    ordered = lax.sort(keys * 4096 + lax.iota(jnp.int32, ENTRIES))
+    ordered = jnp.pad(ordered, (0, 4096 - ENTRIES), constant_values=PAD_NODE * 4096).reshape(32, 128)
+    slots = jnp.pad(cell_nodes, ((0, 0), (0, NPC_PAD - NPC))).reshape(CELLS * CELL_CHUNKS, 128)
+    vmem = pl.BlockSpec(memory_space=pltpu.VMEM)
+    return pl.pallas_call(
+        table_kernel,
+        out_shape=jax.ShapeDtypeStruct((START_AT, 128), jnp.float32),
+        in_specs=[vmem] * 5 + [pl.BlockSpec(memory_space=pltpu.SMEM)],
+        out_specs=vmem,
+        scratch_shapes=[
+            pltpu.VMEM((32, ENTRY_PAD), jnp.bfloat16),
+            pltpu.VMEM((128, ENTRY_PAD), jnp.bfloat16),
+        ],
+        compiler_params=pltpu.CompilerParams(vmem_limit_bytes=16 * 1024 * 1024),
+    )(ordered, slots, send_list, potential.reshape(NODES // 128, 128), cell_scale.reshape(1, CELLS), node_count)
+
+
+def gathered_tables(own_table, vectors):
+    def next_step(both, members, receivers):
+        tables, values = both[..., :START_AT, :], both[..., START_AT:, :]
+        values = jnp.split(values, receivers, axis=-2)
+        operand = jnp.stack([jnp.concatenate([tables, v], axis=-2) for v in values])
+        return lax.all_to_all(operand, "mesh", 0, 0, axis_index_groups=groups_of(PARTS, members))
+
+    values = vectors.reshape(PARTS * (NODES // 128), 128)
+    both = next_step(jnp.concatenate([own_table, values]), (8, 16), 4)
+    both = next_step(both, (2, 4), 4)
+    both = next_step(both, (1,), 2)
+    return both.transpose(2, 1, 0, 3, 4).reshape(PARTS, TABLE_CHUNKS * 128)
 
 
 def chunk(c):
@@ -120,7 +192,7 @@
 
 
 def filter_kernel(
-    step_count, last, coef, table, start, matrix, out,
+    step_count, last, coef, table, field, matrix, out,
     mat_hi, mat_lo, idx, pos, place, end, send, scale, cur, prev, ext, vals, prod, arrived, w, halo, sums,
 ):
     lane = lax.broadcasted_iota(jnp.int32, (8, 128), 1)
@@ -152,15 +224,22 @@
     short = jnp.max(misc(1)).astype(jnp.int32) <= FEW * 128
     short &= jnp.min(misc(1)).astype(jnp.int32) >= SKIP * 128
     short &= jnp.max(misc(2)).astype(jnp.int32) <= SHORT_RUN
+    outside = jnp.zeros((PARTS, 128), jnp.float32)
+    for n, (first, stop) in enumerate(WINDOWS):
+        ends = table[:, chunk(END_AT + GHOSTS // 128 + n)]
+        missed = (ends >= 0.0) & ((ends < first * 128.0) | (ends >= stop * 128.0))
+        outside = jnp.maximum(outside, jnp.where(missed, 1.0, 0.0))
+    short &= jnp.max(outside).astype(jnp.int32) == 0
 
     quarter = NODES // 4
     if last:
         for q in range(4):
-            cur[:, q * quarter : (q + 1) * quarter] = start[q * 32 : (q + 1) * 32, :]
+            cur[:, q * quarter : (q + 1) * quarter] = field[q * 32 : (q + 1) * 32, :]
     else:
         live = misc(0).astype(jnp.int32)
         node = lax.broadcasted_iota(jnp.int32, (PARTS, NODES), 1)
-        cur[...] = jnp.where(node < live, start[...], 0.0)
+        start = table[:, START_AT * 128 : TABLE_CHUNKS * 128]
+        cur[...] = jnp.where(node < live, start, 0.0)
         prev[...] = jnp.zeros((PARTS, NODES), jnp.float32)
 
     def over_groups(body):
@@ -217,9 +296,12 @@
             carry = total + through * carry
         return done
 
-    def run_ends(r, sources, node_first, node_count):
-        for n in range(node_count):
-            sums[r, chunk(n)] = picked(sources, end[r, chunk(node_first + n)])
+    def run_ends(r, sources, node_first, windows):
+        for n, (first, stop) in enumerate(windows):
+            inside = [(q, source) for q, source in sources if first <= q < stop]
+            sums[r, chunk(n)] = picked(inside, end[r, chunk(node_first + n)])
+
+    anywhere = ((0, ENTRY_CHUNKS),)
 
     def with_arrivals(g, r):
         base = CELLS * CELL_CHUNKS
@@ -239,21 +321,21 @@
             into_order(r, products_of(g), 0, FEW)
         partial_runs([(r, q) for r in fixed for q in range(FEW)], SHORT_RUN)
         for r in fixed:
-            run_ends(r, joined_runs(r, 0, FEW), 0, 4)
+            run_ends(r, joined_runs(r, 0, FEW), 0, ((0, FEW),) * 4)
 
     def ghost_sums_any():
         in_order_and_summed(lambda g, r: products_of(g))
-        over_groups(lambda g, r: run_ends(r, chained_runs(r), 0, 4))
+        over_groups(lambda g, r: run_ends(r, chained_runs(r), 0, anywhere * 4))
 
     def own_sums():
         over_groups(lambda g, r: into_order(r, with_arrivals(g, r), SKIP, ENTRY_CHUNKS))
         for r in fixed:
             partial_runs([(r, q) for q in range(SKIP, ENTRY_CHUNKS)], SHORT_RUN)
-        over_groups(lambda g, r: run_ends(r, joined_runs(r, SKIP, ENTRY_CHUNKS), 4, 16))
+        over_groups(lambda g, r: run_ends(r, joined_runs(r, SKIP, ENTRY_CHUNKS), 4, WINDOWS))
 
     def own_sums_any():
         in_order_and_summed(with_arrivals)
-        over_groups(lambda g, r: run_ends(r, chained_runs(r), 4, 16))
+        over_groups(lambda g, r: run_ends(r, chained_runs(r), 4, anywhere * 16))
 
     def apply():
         def outgoing(g, r):
@@ -326,7 +408,7 @@
         out[q * 32 : (q + 1) * 32, :] = cur[:, q * quarter : (q + 1) * quarter]
 
 
-def run_filter(coef, table, start, cell_matrix, step_count, last):
+def run_filter(coef, table, field, cell_matrix, step_count, last):
     padded = jnp.pad(cell_matrix, ((0, NPC_PAD - NPC), (0, NPC_PAD - NPC)))
     vmem = pl.BlockSpec(memory_space=pltpu.VMEM)
     f32, i32 = jnp.float32, jnp.int32
@@ -359,7 +441,7 @@
         cost_estimate=pl.CostEstimate(
             flops=step_count * 15_000_000_000, bytes_accessed=step_count * 50_000_000, transcendentals=0
         ),
-    )(coef, table, start, padded)
+    )(coef, table, field, padded)
 
 
 def coefficients(filter_bounds):
@@ -378,13 +460,8 @@
 
 
 def body(vectors, potential, cell_scale, cell_matrix, cell_nodes, send_list, node_count, filter_bounds):
-    start = lax.all_to_all(vectors, "mesh", 0, 0, tiled=True)
     own_table = partition_table(cell_nodes, send_list[0], potential, cell_scale, node_count)
-    own_table, start = lax.optimization_barrier((own_table, start))
-    table = collected(own_table, "mesh", PARTS, 8)
-    table = spread(table, "mesh", PARTS, (2, 4))
-    table = spread(table, "mesh", PARTS, (1,))
-    table = table.transpose(2, 1, 0, 3, 4).reshape(PARTS, TABLE_CHUNKS * 128)
+    table = gathered_tables(own_table, vectors)
 
     coef = coefficients(filter_bounds)
     quarters = groups_of(16 * PARTS, (1, 2, 4, 8, 16, PARTS, 2 * PARTS))
@@ -394,15 +471,13 @@
         pieces = lax.all_to_all(pieces, ("band", "mesh"), 0, 0, axis_index_groups=quarters)
         return pieces.reshape(4 * PARTS, NODES // 4)
 
-    f = run_filter(coef, table, start, cell_matrix, 2 * DEGREE, False)
+    f = run_filter(coef, table, jnp.zeros((8, 128), jnp.float32), cell_matrix, 2 * DEGREE, False)
     f_quarter = to_quarters(f)
     g = run_filter(coef, table, f, cell_matrix, 1, True)
     left = to_quarters(g)
     band_rows = vectors.shape[0]
-    filtered = exchange(f_quarter.reshape(4, band_rows, NODES // 4), "band", 16, 1)
-    filtered = filtered.transpose(1, 0, 2).reshape(band_rows, NODES)
-
-    right = collected(f_quarter, "band", 16, 4).reshape(16 * band_rows, NODES // 4)
+    right, received = collected(f_quarter, "band", 16, 4)
+    right = right.reshape(16 * band_rows, NODES // 4)
     partial = lax.dot_general(left, right, (((1,), (1,)), ((), ())), precision=HIGHEST)
 
     plane = groups_of(PARTS, (1, 2, 4))
@@ -413,7 +488,12 @@
     partial = partial.reshape((16,) + partial.shape[2:])
     block = lax.all_to_all(partial, ("band", "mesh"), 0, 0, axis_index_groups=along_z).sum(0)
     block = block / (NODES * PARTS)
-    hproj = spread(block, "mesh", PARTS, (1, 2, 4)).reshape(band_rows, 16 * band_rows)
+    hproj = spread(block, "mesh", PARTS, (1, 2, 4))
+    f_quarter, _ = lax.optimization_barrier((f_quarter, received[0]))
+    quarter_rows, mine = exchange(f_quarter.reshape(4, band_rows, NODES // 4), "band", 16, 1)
+    quarter_rows, hproj = lax.optimization_barrier((quarter_rows, hproj))
+    filtered = in_place(quarter_rows, mine).transpose(1, 0, 2).reshape(band_rows, NODES)
+    hproj = hproj.reshape(band_rows, 16 * band_rows)
     return filtered, hproj
 
 

time: 282 us -> 266 us (0.943)
  blocking collectives: 18.6 us -> 60.8 us
  starting transfers between devices: 100 us -> 62.3 us
  other arithmetic: 17.5 us -> 10.5 us
  Pallas kernels: 80.8 us -> 75.5 us
  waiting for transfers between devices: 45.2 us -> 40.1 us
    all_to_all x1 -> x2, blocking collectives: 6.79 us -> 48.9 us  [next_step(): lax.all_to_all(operand, 'mesh', 0, 0, axis_index_groups=groups_of(PARTS,...]
    ppermute x9 -> x6, starting transfers between devices: 35 us -> 18.9 us  [swapped(): return lax.ppermute(block, axis, [(i ^ distance, i) for i in range(size)])]
    all_to_all x1, starting transfers between devices: 19.4 us -> 4.31 us  [next_step(): lax.all_to_all(operand, 'mesh', 0, 0, axis_index_groups=groups_of(PARTS,...]
    all_to_all x1, waiting for transfers between devices: 0.47 us -> 11.4 us  [next_step(): lax.all_to_all(operand, 'mesh', 0, 0, axis_index_groups=groups_of(PARTS,...]
    ppermute x9 -> x6, waiting for transfers between devices: 14.8 us -> 3.9 us  [swapped(): return lax.ppermute(block, axis, [(i ^ distance, i) for i in range(size)])]
    all_to_all x2 -> x1, waiting for transfers between devices: 12.9 us -> 4.85 us  [spread(): return lax.all_to_all(copies, axis, 0, 0, axis_index_groups=members)]
    reduce_sum x2 -> x0, other arithmetic: 7.71 us -> none  [the longest x1 4.41 us: partition_table(): jnp.sum((keys[None, :] < sorted_key[:, None]).astype(jnp.int32), axis=1)]
    pallas_call x2, Pallas kernels: 80.8 us -> 74.4 us  [run_filter(): pl.pallas_call(functools.partial(filter_kernel, step_count, last), out_sh...]
  transfers between devices with their start and end apart: 15 -> 11, of which waited for: 10 -> 6; matrix products, arithmetic and copies ran while one was open for 8% -> 1% of each run, Pallas kernels for 4% -> 4%
where the time goes in v4:
time: 266 us; the launch traced here: 265 us
  Pallas kernels  75.5 us (28%)
  starting transfers between devices  62.3 us (23%)
  blocking collectives  60.8 us (23%)
  waiting for transfers between devices  40.1 us (15%)
  other arithmetic  10.5 us (4%)
  local copies, waits for them, and re-layouts  9.48 us (4%)
  between operations  5.25 us (2%)
    pallas_call x2, Pallas kernels, run_filter(): pl.pallas_call(functools.partial(filter_kernel, step_count, last), out_sh...  74.4 us
    all_to_all x2, blocking collectives, next_step(): lax.all_to_all(operand, 'mesh', 0, 0, axis_index_groups=groups_of(PARTS,...  48.9 us
    all_to_all x2, starting transfers between devices, to_quarters(): lax.all_to_all(pieces, ('band', 'mesh'), 0, 0, axis_index_groups=quarters)  20.6 us
    ppermute x6, starting transfers between devices, swapped(): return lax.ppermute(block, axis, [(i ^ distance, i) for i in range(size)])  18.9 us
    all_to_all x2, waiting for transfers between devices, to_quarters(): lax.all_to_all(pieces, ('band', 'mesh'), 0, 0, axis_index_groups=quarters)  16.9 us
    all_to_all x1, blocking collectives, body(): lax.all_to_all(partial, 'mesh', 0, 0, axis_index_groups=plane).sum(0)  11.8 us
    all_to_all x1, waiting for transfers between devices, next_step(): lax.all_to_all(operand, 'mesh', 0, 0, axis_index_groups=groups_of(PARTS,...  11.4 us
    all_to_all x1, starting transfers between devices, body(): lax.all_to_all(partial, ('band', 'mesh'), 0, 0, axis_index_groups=along_z)  11.3 us
  transfers between devices with their start and end apart: 11, of which 6 were waited for; matrix products, arithmetic and copies ran while one was open for 1% of the time, Pallas kernels for 4%

profile of v4, /device:TPU:1, one launch (start us, length us, event | category | flops | bytes accessed | tf_op | source)
XLA Modules:
  0.0 265.0 jit_solution(16510370066418021459)
XLA Ops:
  0.7 1.0 fusion.10
  1.7 0.7 add_select_fusion
  2.5 0.7 add_bitcast_fusion
  3.3 5.9 %sort.14 = (s32[3256]{0:T(1024)S(1)}, s32[3256]{0:T(1024)}) sort(s32[3256]{0:T(1024)S(1)} %fusion.8, s32[3256]{0:T(1024)S(1)} %iota.7), dimensions={0}, to_apply=%region_0.1 | sort | flops 39072 | bytes 52096 | tf_op jit(solution)/shard_map/sort | solution.py:146
  9.2 0.7 pad.14
  10.6 1.1 shard_map.95
  11.8 41.3 %all_to_all.40 = f32[4,248,128]{2,1,0:T(8,128)S(1)} all-to-all(f32[4,248,128]{2,1,0:T(8,128)S(1)} %pad_maximum_fusion.3), channel_id=1, replica_groups={{0,8,16,24},{1,9,17,25},{2,10,18,26},{3,11,19,27},{4,12,20,28},{5,13,21..., dimensions={0} | all-to-all | bytes 1015808 | tf_op jit(solution)/shard_map/all_to_all | solution.py:168
  53.2 0.1 fusion
  53.3 1.2 pad_maximum_fusion.1
  54.4 4.3 %all-to-all-start.1 = ((f32[4,4,152,128]{3,2,1,0:T(8,128)}), f32[4,4,152,128]{3,2,1,0:T(8,128)S(1)}, u32[]{:S(2)}, u32[]{:S(2)}) async-start(f32[4,4,152,128]{3,2,1,0:T(8,128)} %pad_maximum_fusion.1), calls=%async_computation.1 | async-start | bytes 2490368 | tf_op jit(solution)/shard_map/all_to_all | solution.py:168
  58.8 0.6 fusion.11
  62.9 0.1 stack.94.coef
  63.0 11.4 %all-to-all-done.1 = f32[4,4,152,128]{3,2,1,0:T(8,128)S(1)} async-done(((f32[4,4,152,128]{3,2,1,0:T(8,128)}), f32[4,4,152,128]{3,2,1,0:T(8,128)S(1)}, u32[]{:S(2)}, u32[]{:S(2)}) %all-to-all-start.1) | async-done | bytes 1245216 | tf_op jit(solution)/shard_map/all_to_all | solution.py:168
  74.7 0.1 pad_maximum_fusion
  74.9 0.2 copy.39
  75.1 7.6 %all_to_all.41 = f32[2,4,4,136,128]{4,3,1,2,0:T(8,128)S(1)} all-to-all(f32[2,4,4,136,128]{4,3,1,2,0:T(8,128)S(1)} %copy.39), channel_id=1, replica_groups={{0,1},{2,3},{4,5},{6,7},{8,9},{10,11},{12,13},{14,15},{16,17},{18,19},{..., dimensions={0} | all-to-all | bytes 4456448 | tf_op jit(solution)/shard_map/all_to_all | solution.py:168
  82.6 0.2 copy.40
  82.8 0.4 copy.64
  83.2 63.2 %shard_map.96.field = f32[128,512]{1,0:T(8,128)S(1)} custom-call(f32[8]{0:T(128)S(1)} %stack.94.coef, f32[32,17408]{1,0:T(8,128)S(1)} %bitcast.87, f32[8,128]{1,0:T(8,128)S(1)} %broadcast_in_dim.6.field, f32[384,384]{1,0:T(8,128)S(1)} %pad.15.matrix), custom_call_target="tpu_custom_call" | custom-call | flops 89999998976 | bytes 300000000 | tf_op jit(solution)/shard_map/pallas_call | solution.py:416
  146.5 0.8 reshape.75
  147.3 11.8 %all-to-all-start.3 = ((f32[128,4,128]{2,1,0:T(4,128)}), f32[128,4,128]{2,1,0:T(4,128)}, u32[]{:S(2)}, u32[]{:S(2)}) async-start(f32[128,4,128]{2,1,0:T(4,128)} %reshape.75), calls=%async_computation.3 | async-start | bytes 524288 | tf_op jit(solution)/shard_map/all_to_all | solution.py:471
  159.1 11.2 %shard_map.97 = f32[128,512]{1,0:T(8,128)S(1)} custom-call(f32[8]{0:T(128)S(1)} %stack.94.coef, f32[32,17408]{1,0:T(8,128)S(1)} %bitcast.88, f32[128,512]{1,0:T(8,128)S(1)} %shard_map.96.field, f32[384,384]{1,0:T(8,128)S(1)} %pad.15.matrix), custom_call_target="tpu_custom_call" | custom-call | flops 15000000512 | bytes 50000000 | tf_op jit(solution)/shard_map/pallas_call | solution.py:416
  170.2 0.8 reshape.78
  171.0 7.6 %all-to-all-done.3 = f32[128,4,128]{2,1,0:T(4,128)} async-done(((f32[128,4,128]{2,1,0:T(4,128)}), f32[128,4,128]{2,1,0:T(4,128)}, u32[]{:S(2)}, u32[]{:S(2)}) %all-to-all-start.3) | async-done | bytes 262176 | tf_op jit(solution)/shard_map/all_to_all | solution.py:471
  178.6 8.9 %all-to-all-start.4 = ((f32[128,4,128]{2,1,0:T(4,128)}), f32[128,4,128]{2,1,0:T(4,128)S(1)}, u32[]{:S(2)}, u32[]{:S(2)}) async-start(f32[128,4,128]{2,1,0:T(4,128)} %reshape.78), calls=%async_computation.4 | async-start | bytes 524288 | tf_op jit(solution)/shard_map/all_to_all | solution.py:471
  187.5 1.0 copy.65
  188.5 3.1 %collective-permute-start = (f32[128,512]{1,0:T(8,128)S(1)}, f32[128,512]{1,0:T(8,128)S(1)}, u32[]{:S(2)}, u32[]{:S(2)}) collective-permute-start(f32[128,512]{1,0:T(8,128)S(1)} %bitcast.95), channel_id=1, source_target_pairs={{128,0},{160,32},{192,64},{224,96},{0,128},{32,160},{64,192},{96,2... | collective-permute-start | bytes 786440 | tf_op jit(solution)/shard_map/ppermute | solution.py:63
  191.6 4.4 %collective-permute-start.4 = (f32[128,512]{1,0:T(8,128)S(1)}, f32[128,512]{1,0:T(8,128)S(1)}, u32[]{:S(2)}, u32[]{:S(2)}) collective-permute-start(f32[128,512]{1,0:T(8,128)S(1)} %bitcast.96), channel_id=1, source_target_pairs={{256,0},{288,32},{320,64},{352,96},{384,128},{416,160},{448,192},{... | collective-permute-start | bytes 786440 | tf_op jit(solution)/shard_map/ppermute | solution.py:63
  196.0 2.1 collective-permute-start.5
  198.1 9.3 %all-to-all-done.4 = f32[128,4,128]{2,1,0:T(4,128)S(1)} async-done(((f32[128,4,128]{2,1,0:T(4,128)}), f32[128,4,128]{2,1,0:T(4,128)S(1)}, u32[]{:S(2)}, u32[]{:S(2)}) %all-to-all-start.4) | async-done | bytes 262176 | tf_op jit(solution)/shard_map/all_to_all | solution.py:471
  207.4 0.2 dot_general.5
  207.5 3.9 %collective-permute-done.5 = f32[128,512]{1,0:T(8,128)S(1)} collective-permute-done((f32[128,512]{1,0:T(8,128)S(1)}, f32[128,512]{1,0:T(8,128)S(1)}, u32[]{:S(2)}, u32[]{:S(2)}) %collective-permute-start.5) | collective-permute-done | bytes 262176 | tf_op jit(solution)/shard_map/ppermute | solution.py:63
  211.4 1.1 select_bitcast_fusion.3
  212.6 1.2 convolution_bitcast_fusion
  213.8 0.2 copy.42
  214.0 11.8 %all_to_all.42 = f32[8,4,4,512]{3,2,1,0:T(4,128)S(1)} all-to-all(f32[8,4,4,512]{3,2,1,0:T(4,128)S(1)} %copy.42), channel_id=1, replica_groups={{0,1,2,3,4,5,6,7},{8,9,10,11,12,13,14,15},{16,17,18,19,20,21,22,23},{24..., dimensions={0} | all-to-all | bytes 524288 | tf_op jit(solution)/shard_map/all_to_all | solution.py:485
  225.9 0.7 broadcast_in_dim.7
  226.5 11.3 %all-to-all-start.6 = ((f32[16,4,512]{2,1,0:T(4,128)}), f32[16,4,512]{2,1,0:T(4,128)S(1)}, u32[]{:S(2)}, u32[]{:S(2)}) async-start(f32[16,4,512]{2,1,0:T(4,128)} %bitcast.36), calls=%async_computation.6 | async-start | bytes 262144 | tf_op jit(solution)/shard_map/all_to_all | solution.py:489
  237.9 3.2 %collective-permute-start.1 = (f32[32,512]{1,0:T(8,128)S(1)}, f32[32,512]{1,0:T(8,128)S(1)}, u32[]{:S(2)}, u32[]{:S(2)}) collective-permute-start(f32[32,512]{1,0:T(8,128)S(1)} %get-tuple-element.30), channel_id=1, source_target_pairs={{32,0},{0,32},{96,64},{64,96},{160,128},{128,160},{224,192},{192,2... | collective-permute-start | bytes 196616 | tf_op jit(solution)/shard_map/ppermute | solution.py:63
  241.1 4.0 %collective-permute-start.2 = (f32[32,512]{1,0:T(8,128)S(1)}, f32[32,512]{1,0:T(8,128)S(1)}, u32[]{:S(2)}, u32[]{:S(2)}) collective-permute-start(f32[32,512]{1,0:T(8,128)S(1)} %get-tuple-element.29), channel_id=1, source_target_pairs={{64,0},{96,32},{0,64},{32,96},{192,128},{224,160},{128,192},{160,2... | collective-permute-start | bytes 196616 | tf_op jit(solution)/shard_map/ppermute | solution.py:63
  245.1 2.0 collective-permute-start.3
  247.2 3.0 %all-to-all-done.6 = f32[16,4,512]{2,1,0:T(4,128)S(1)} async-done(((f32[16,4,512]{2,1,0:T(4,128)}), f32[16,4,512]{2,1,0:T(4,128)S(1)}, u32[]{:S(2)}, u32[]{:S(2)}) %all-to-all-start.6) | async-done | bytes 131104 | tf_op jit(solution)/shard_map/all_to_all | solution.py:489
  250.3 0.6 broadcast_in_dim.8
  250.9 7.2 %all-to-all-start.7 = ((f32[8,4,512]{2,1,0:T(4,128)}), f32[8,4,512]{2,1,0:T(4,128)S(1)}, u32[]{:S(2)}, u32[]{:S(2)}) async-start(f32[8,4,512]{2,1,0:T(4,128)} %broadcast_in_dim.8), calls=%async_computation.7 | async-start | bytes 131072 | tf_op jit(solution)/shard_map/all_to_all | solution.py:59
  258.1 4.8 %all-to-all-done.7 = f32[8,4,512]{2,1,0:T(4,128)S(1)} async-done(((f32[8,4,512]{2,1,0:T(4,128)}), f32[8,4,512]{2,1,0:T(4,128)S(1)}, u32[]{:S(2)}, u32[]{:S(2)}) %all-to-all-start.7) | async-done | bytes 65568 | tf_op jit(solution)/shard_map/all_to_all | solution.py:59
  263.3 0.3 pad_maximum_fusion.7
  263.6 0.8 copy.51
  264.4 0.7 reshape.82
  (44 shorter events, 1.1 us)
Async XLA Ops:
  0.6 9.9 %copy-start.1 = (s32[1,4,128]{2,1,0:T(4,128)S(1)}, s32[1,4,128]{2,1,0:T(4,128)}, u32[]{:S(2)}) copy-start(s32[1,4,128]{2,1,0:T(4,128)} %param.13) | copy-start | bytes 6148
  0.6 9.9 %copy-start = (f32[2048]{0:T(1024)S(1)}, f32[2048]{0:T(1024)}, u32[]{:S(2)}) copy-start(f32[2048]{0:T(1024)} %param.9) | copy-start | bytes 24580
  0.7 9.9 %copy-start.2 = (f32[8]{0:T(128)S(1)}, f32[8]{0:T(128)}, u32[]{:S(2)}) copy-start(f32[8]{0:T(128)} %param.10) | copy-start | bytes 100
  54.4 4.3 %copy-start.4 = (f32[3]{0:T(128)S(1)}, f32[3]{0:T(128)}, u32[]{:S(2)}) copy-start(f32[3]{0:T(128)} %param.15) | copy-start | bytes 40
  54.4 8.5 %copy-start.3 = (f32[343,343]{1,0:T(8,128)S(1)}, f32[343,343]{1,0:T(8,128)}, u32[]{:S(2)}) copy-start(f32[343,343]{1,0:T(8,128)} %param.11) | copy-start | bytes 1411792
  54.4 20.0 %all-to-all-start.1 = ((f32[4,4,152,128]{3,2,1,0:T(8,128)}), f32[4,4,152,128]{3,2,1,0:T(8,128)S(1)}, u32[]{:S(2)}, u32[]{:S(2)}) async-start(f32[4,4,152,128]{3,2,1,0:T(8,128)} %pad_maximum_fusion.1), calls=%async_computation.1 | async-start | bytes 2490368 | tf_op jit(solution)/shard_map/all_to_all | solution.py:168
  147.3 31.3 %all-to-all-start.3 = ((f32[128,4,128]{2,1,0:T(4,128)}), f32[128,4,128]{2,1,0:T(4,128)}, u32[]{:S(2)}, u32[]{:S(2)}) async-start(f32[128,4,128]{2,1,0:T(4,128)} %reshape.75), calls=%async_computation.3 | async-start | bytes 524288 | tf_op jit(solution)/shard_map/all_to_all | solution.py:471
  178.6 28.8 %all-to-all-start.4 = ((f32[128,4,128]{2,1,0:T(4,128)}), f32[128,4,128]{2,1,0:T(4,128)S(1)}, u32[]{:S(2)}, u32[]{:S(2)}) async-start(f32[128,4,128]{2,1,0:T(4,128)} %reshape.78), calls=%async_computation.4 | async-start | bytes 524288 | tf_op jit(solution)/shard_map/all_to_all | solution.py:471
  188.5 19.1 %collective-permute-start = (f32[128,512]{1,0:T(8,128)S(1)}, f32[128,512]{1,0:T(8,128)S(1)}, u32[]{:S(2)}, u32[]{:S(2)}) collective-permute-start(f32[128,512]{1,0:T(8,128)S(1)} %bitcast.95), channel_id=1, source_target_pairs={{128,0},{160,32},{192,64},{224,96},{0,128},{32,160},{64,192},{96,2... | collective-permute-start | bytes 786440 | tf_op jit(solution)/shard_map/ppermute | solution.py:63
  191.6 15.9 %collective-permute-start.4 = (f32[128,512]{1,0:T(8,128)S(1)}, f32[128,512]{1,0:T(8,128)S(1)}, u32[]{:S(2)}, u32[]{:S(2)}) collective-permute-start(f32[128,512]{1,0:T(8,128)S(1)} %bitcast.96), channel_id=1, source_target_pairs={{256,0},{288,32},{320,64},{352,96},{384,128},{416,160},{448,192},{... | collective-permute-start | bytes 786440 | tf_op jit(solution)/shard_map/ppermute | solution.py:63
  196.0 15.5 %collective-permute-start.5 = (f32[128,512]{1,0:T(8,128)S(1)}, f32[128,512]{1,0:T(8,128)S(1)}, u32[]{:S(2)}, u32[]{:S(2)}) collective-permute-start(f32[128,512]{1,0:T(8,128)S(1)} %bitcast.97), channel_id=1, source_target_pairs={{384,0},{416,32},{448,64},{480,96},{256,128},{288,160},{320,192},{... | collective-permute-start | bytes 786440 | tf_op jit(solution)/shard_map/ppermute | solution.py:63
  226.5 23.7 %all-to-all-start.6 = ((f32[16,4,512]{2,1,0:T(4,128)}), f32[16,4,512]{2,1,0:T(4,128)S(1)}, u32[]{:S(2)}, u32[]{:S(2)}) async-start(f32[16,4,512]{2,1,0:T(4,128)} %bitcast.36), calls=%async_computation.6 | async-start | bytes 262144 | tf_op jit(solution)/shard_map/all_to_all | solution.py:489
  237.9 20.2 %collective-permute-start.1 = (f32[32,512]{1,0:T(8,128)S(1)}, f32[32,512]{1,0:T(8,128)S(1)}, u32[]{:S(2)}, u32[]{:S(2)}) collective-permute-start(f32[32,512]{1,0:T(8,128)S(1)} %get-tuple-element.30), channel_id=1, source_target_pairs={{32,0},{0,32},{96,64},{64,96},{160,128},{128,160},{224,192},{192,2... | collective-permute-start | bytes 196616 | tf_op jit(solution)/shard_map/ppermute | solution.py:63
  241.1 17.0 %collective-permute-start.2 = (f32[32,512]{1,0:T(8,128)S(1)}, f32[32,512]{1,0:T(8,128)S(1)}, u32[]{:S(2)}, u32[]{:S(2)}) collective-permute-start(f32[32,512]{1,0:T(8,128)S(1)} %get-tuple-element.29), channel_id=1, source_target_pairs={{64,0},{96,32},{0,64},{32,96},{192,128},{224,160},{128,192},{160,2... | collective-permute-start | bytes 196616 | tf_op jit(solution)/shard_map/ppermute | solution.py:63
  245.1 13.0 %collective-permute-start.3 = (f32[32,512]{1,0:T(8,128)S(1)}, f32[32,512]{1,0:T(8,128)S(1)}, u32[]{:S(2)}, u32[]{:S(2)}) collective-permute-start(f32[32,512]{1,0:T(8,128)S(1)} %get-tuple-element.28), channel_id=1, source_target_pairs={{96,0},{64,32},{32,64},{0,96},{224,128},{192,160},{160,192},{128,2... | collective-permute-start | bytes 196616 | tf_op jit(solution)/shard_map/ppermute | solution.py:63
  250.9 12.1 %all-to-all-start.7 = ((f32[8,4,512]{2,1,0:T(4,128)}), f32[8,4,512]{2,1,0:T(4,128)S(1)}, u32[]{:S(2)}, u32[]{:S(2)}) async-start(f32[8,4,512]{2,1,0:T(4,128)} %broadcast_in_dim.8), calls=%async_computation.7 | async-start | bytes 131072 | tf_op jit(solution)/shard_map/all_to_all | solution.py:59

commit v5 on v4

--- a/solution.py
+++ b/solution.py
@@ -73,13 +73,14 @@
     return [kept] + [swapped(p, axis, size, (d + 1) * unit) for d, p in enumerate(sent)], mine
 
 
-def collected(block, axis, size, unit):
-    mine = (lax.axis_index(axis) // unit) % 4
-    received = [swapped(block, axis, size, d * unit) for d in (1, 2, 3)]
-    return in_place([block] + received, mine), received
-
-
-def table_kernel(ordered, slots, send, pot, cell_scale, node_count, out, hot_high, hot_low):
+def table_kernel(
+    ordered, slots_in, send_in, pot_in, cell_scale_in, node_count, out,
+    hot_high, hot_low, slots, send, pot, cell_scale, arrival,
+):
+    fetched = ((slots_in, slots), (send_in, send), (pot_in, pot), (cell_scale_in, cell_scale))
+    fetches = [pltpu.make_async_copy(a, b, arrival.at[i]) for i, (a, b) in enumerate(fetched)]
+    for fetch in fetches:
+        fetch.start()
     shape = (32, 128)
     row = lax.broadcasted_iota(jnp.int32, shape, 0)
     lane = lax.broadcasted_iota(jnp.int32, shape, 1)
@@ -121,9 +122,15 @@
     up_to = along_rows(count, jnp.add)
     end = jnp.where(count > 0.0, up_to - 1.0, -1.0)
 
+    for fetch in fetches:
+        fetch.wait()
     nodes = slots[...]
-    nodes = jnp.where(nodes >= NODES, nodes - NODES, nodes + GHOSTS)
-    out[IDX_AT:POS_AT, :] = nodes.astype(jnp.float32)
+    nodes = jnp.where(nodes >= NODES, nodes - NODES, nodes + GHOSTS).astype(jnp.float32)
+    out[IDX_AT:POS_AT, :] = jnp.zeros((POS_AT - IDX_AT, 128), jnp.float32)
+    for c in range(CELLS):
+        for k in range(CELL_CHUNKS):
+            at, width = IDX_AT + c * CELL_CHUNKS + k, min(128, NPC - k * 128)
+            out[at : at + 1, 0:width] = nodes[c : c + 1, k * 128 : k * 128 + width]
     out[POS_AT:PLACE_AT, :] = position[:ENTRY_CHUNKS]
     out[PLACE_AT:END_AT, :] = place[:ENTRY_CHUNKS]
     out[END_AT:SEND_AT, :] = end[: EXT // 128]
@@ -145,19 +152,23 @@
     keys = jnp.concatenate([shifted.reshape(-1), send_list.reshape(-1) + GHOSTS])
     ordered = lax.sort(keys * 4096 + lax.iota(jnp.int32, ENTRIES))
     ordered = jnp.pad(ordered, (0, 4096 - ENTRIES), constant_values=PAD_NODE * 4096).reshape(32, 128)
-    slots = jnp.pad(cell_nodes, ((0, 0), (0, NPC_PAD - NPC))).reshape(CELLS * CELL_CHUNKS, 128)
     vmem = pl.BlockSpec(memory_space=pltpu.VMEM)
     return pl.pallas_call(
         table_kernel,
         out_shape=jax.ShapeDtypeStruct((START_AT, 128), jnp.float32),
-        in_specs=[vmem] * 5 + [pl.BlockSpec(memory_space=pltpu.SMEM)],
+        in_specs=[vmem] + [pl.BlockSpec(memory_space=pltpu.HBM)] * 4 + [pl.BlockSpec(memory_space=pltpu.SMEM)],
         out_specs=vmem,
         scratch_shapes=[
             pltpu.VMEM((32, ENTRY_PAD), jnp.bfloat16),
             pltpu.VMEM((128, ENTRY_PAD), jnp.bfloat16),
+            pltpu.VMEM((CELLS, NPC), jnp.int32),
+            pltpu.VMEM((4, SLOTS), jnp.int32),
+            pltpu.VMEM((NODES // 128, 128), jnp.float32),
+            pltpu.VMEM((1, CELLS), jnp.float32),
+            pltpu.SemaphoreType.DMA((4,)),
         ],
         compiler_params=pltpu.CompilerParams(vmem_limit_bytes=16 * 1024 * 1024),
-    )(ordered, slots, send_list, potential.reshape(NODES // 128, 128), cell_scale.reshape(1, CELLS), node_count)
+    )(ordered, cell_nodes, send_list, potential.reshape(NODES // 128, 128), cell_scale.reshape(1, CELLS), node_count)
 
 
 def gathered_tables(own_table, vectors):
@@ -242,12 +253,12 @@
         cur[...] = jnp.where(node < live, start, 0.0)
         prev[...] = jnp.zeros((PARTS, NODES), jnp.float32)
 
-    def over_groups(body):
+    def over_groups(body, unroll=1):
         def at(g, _):
             body(g, rows(g))
             return 0
 
-        lax.fori_loop(0, GROUPS, at, 0)
+        lax.fori_loop(0, GROUPS, at, 0, unroll=unroll)
 
     def wrap(values, k):
         c = chunk(k)
@@ -328,10 +339,10 @@
         over_groups(lambda g, r: run_ends(r, chained_runs(r), 0, anywhere * 4))
 
     def own_sums():
-        over_groups(lambda g, r: into_order(r, with_arrivals(g, r), SKIP, ENTRY_CHUNKS))
+        over_groups(lambda g, r: into_order(r, with_arrivals(g, r), SKIP, ENTRY_CHUNKS), 2)
         for r in fixed:
             partial_runs([(r, q) for q in range(SKIP, ENTRY_CHUNKS)], SHORT_RUN)
-        over_groups(lambda g, r: run_ends(r, joined_runs(r, SKIP, ENTRY_CHUNKS), 4, WINDOWS))
+        over_groups(lambda g, r: run_ends(r, joined_runs(r, SKIP, ENTRY_CHUNKS), 4, WINDOWS), 2)
 
     def own_sums_any():
         in_order_and_summed(with_arrivals)
@@ -359,7 +370,7 @@
                 for k in range(CELL_CHUNKS):
                     vals[there, chunk(k)] = picked(sources, idx[r, chunk(c * CELL_CHUNKS + k)])
 
-        over_groups(gather)
+        over_groups(gather, 2)
 
         x = vals[...]
         high = x.astype(jnp.bfloat16)
@@ -476,22 +487,26 @@
     g = run_filter(coef, table, f, cell_matrix, 1, True)
     left = to_quarters(g)
     band_rows = vectors.shape[0]
-    right, received = collected(f_quarter, "band", 16, 4)
-    right = right.reshape(16 * band_rows, NODES // 4)
-    partial = lax.dot_general(left, right, (((1,), (1,)), ((), ())), precision=HIGHEST)
+    received = [swapped(f_quarter, "band", 16, 4 * d) for d in (1, 2, 3)]
+    products = [
+        lax.dot_general(left, right, (((1,), (1,)), ((), ())), precision=HIGHEST)
+        for right in (f_quarter, *received)
+    ]
+    partial = in_place(products, lax.axis_index("band") // 4)
 
     plane = groups_of(PARTS, (1, 2, 4))
-    partial = partial.reshape(4, 8, band_rows // 8, 16 * band_rows).transpose(1, 0, 2, 3)
+    partial = partial.reshape(4, 4, 8, band_rows // 8, 4 * band_rows).transpose(2, 1, 3, 0, 4)
+    partial = partial.reshape(8, 4, band_rows // 8, 16 * band_rows)
     partial = lax.all_to_all(partial, "mesh", 0, 0, axis_index_groups=plane).sum(0)
     along_z = groups_of(16 * PARTS, (8, 16, PARTS, 2 * PARTS))
     partial = jnp.broadcast_to(partial[:, None], (4, 4) + partial.shape[1:])
     partial = partial.reshape((16,) + partial.shape[2:])
     block = lax.all_to_all(partial, ("band", "mesh"), 0, 0, axis_index_groups=along_z).sum(0)
     block = block / (NODES * PARTS)
-    hproj = spread(block, "mesh", PARTS, (1, 2, 4))
     f_quarter, _ = lax.optimization_barrier((f_quarter, received[0]))
     quarter_rows, mine = exchange(f_quarter.reshape(4, band_rows, NODES // 4), "band", 16, 1)
-    quarter_rows, hproj = lax.optimization_barrier((quarter_rows, hproj))
+    quarter_rows, block = lax.optimization_barrier((quarter_rows, block))
+    hproj = spread(block, "mesh", PARTS, (1, 2, 4))
     filtered = in_place(quarter_rows, mine).transpose(1, 0, 2).reshape(band_rows, NODES)
     hproj = hproj.reshape(band_rows, 16 * band_rows)
     return filtered, hproj

time: 266 us -> 262 us (0.985)
  Pallas kernels: 75.5 us -> 72.4 us
    pallas_call x2, Pallas kernels: 74.4 us -> 71.2 us  [run_filter(): pl.pallas_call(functools.partial(filter_kernel, step_count, last), out_sh...]
  transfers between devices with their start and end apart: 11 -> 11, of which waited for: 6 -> 6; matrix products, arithmetic and copies ran while one was open for 1% -> 2% of each run, Pallas kernels for 4% -> 4%
where the time goes in v5:
time: 262 us; the launch traced here: 260 us
  Pallas kernels  72.4 us (28%)
  blocking collectives  60.8 us (23%)
  starting transfers between devices  60.6 us (23%)
  waiting for transfers between devices  38 us (15%)
  local copies, waits for them, and re-layouts  11.7 us (4%)
  other arithmetic  9.31 us (4%)
  between operations  5.28 us (2%)
    pallas_call x2, Pallas kernels, run_filter(): pl.pallas_call(functools.partial(filter_kernel, step_count, last), out_sh...  71.2 us
    all_to_all x2, blocking collectives, next_step(): lax.all_to_all(operand, 'mesh', 0, 0, axis_index_groups=groups_of(PARTS,...  48.9 us
    all_to_all x2, starting transfers between devices, to_quarters(): lax.all_to_all(pieces, ('band', 'mesh'), 0, 0, axis_index_groups=quarters)  20.8 us
    ppermute x6, starting transfers between devices, swapped(): return lax.ppermute(block, axis, [(i ^ distance, i) for i in range(size)])  18.9 us
    all_to_all x2, waiting for transfers between devices, to_quarters(): lax.all_to_all(pieces, ('band', 'mesh'), 0, 0, axis_index_groups=quarters)  17.2 us
    all_to_all x1, blocking collectives, body(): lax.all_to_all(partial, 'mesh', 0, 0, axis_index_groups=plane).sum(0)  11.9 us
    all_to_all x1, waiting for transfers between devices, next_step(): lax.all_to_all(operand, 'mesh', 0, 0, axis_index_groups=groups_of(PARTS,...  11.4 us
    all_to_all x1, starting transfers between devices, body(): lax.all_to_all(partial, ('band', 'mesh'), 0, 0, axis_index_groups=along_z)  10.6 us
  transfers between devices with their start and end apart: 11, of which 6 were waited for; matrix products, arithmetic and copies ran while one was open for 2% of the time, Pallas kernels for 4%

profile of v5, /device:TPU:1, one launch (start us, length us, event | category | flops | bytes accessed | tf_op | source)
XLA Modules:
  0.0 260.5 jit_solution(3606905636719606298)
XLA Ops:
  0.6 1.0 fusion.9
  1.7 0.7 add_select_fusion
  2.5 0.7 add_bitcast_fusion
  3.3 5.9 %sort.14 = (s32[3256]{0:T(1024)S(1)}, s32[3256]{0:T(1024)}) sort(s32[3256]{0:T(1024)S(1)} %fusion.7, s32[3256]{0:T(1024)S(1)} %iota.7), dimensions={0}, to_apply=%region_0.1 | sort | flops 39072 | bytes 52096 | tf_op jit(solution)/shard_map/sort | solution.py:153
  9.8 0.7 copy-done
  10.5 0.7 copy-done.1
  11.2 0.7 copy-done.2
  11.9 0.7 copy-done.3
  12.6 1.2 shard_map.95
  13.8 41.3 %all_to_all.40 = f32[4,248,128]{2,1,0:T(8,128)S(1)} all-to-all(f32[4,248,128]{2,1,0:T(8,128)S(1)} %pad_maximum_fusion.2), channel_id=1, replica_groups={{0,8,16,24},{1,9,17,25},{2,10,18,26},{3,11,19,27},{4,12,20,28},{5,13,21..., dimensions={0} | all-to-all | bytes 1015808 | tf_op jit(solution)/shard_map/all_to_all | solution.py:179
  55.3 1.1 pad_maximum_fusion.1
  56.5 4.3 %all-to-all-start.1 = ((f32[4,4,152,128]{3,2,1,0:T(8,128)}), f32[4,4,152,128]{3,2,1,0:T(8,128)S(1)}, u32[]{:S(2)}, u32[]{:S(2)}) async-start(f32[4,4,152,128]{3,2,1,0:T(8,128)} %pad_maximum_fusion.1), calls=%async_computation.1 | async-start | bytes 2490368 | tf_op jit(solution)/shard_map/all_to_all | solution.py:179
  60.8 0.6 fusion.10
  65.1 11.4 %all-to-all-done.1 = f32[4,4,152,128]{3,2,1,0:T(8,128)S(1)} async-done(((f32[4,4,152,128]{3,2,1,0:T(8,128)}), f32[4,4,152,128]{3,2,1,0:T(8,128)S(1)}, u32[]{:S(2)}, u32[]{:S(2)}) %all-to-all-start.1) | async-done | bytes 1245216 | tf_op jit(solution)/shard_map/all_to_all | solution.py:179
  76.9 0.2 copy.87
  77.1 7.6 %all_to_all.41 = f32[2,4,4,136,128]{4,3,1,2,0:T(8,128)S(1)} all-to-all(f32[2,4,4,136,128]{4,3,1,2,0:T(8,128)S(1)} %copy.87), channel_id=1, replica_groups={{0,1},{2,3},{4,5},{6,7},{8,9},{10,11},{12,13},{14,15},{16,17},{18,19},{..., dimensions={0} | all-to-all | bytes 4456448 | tf_op jit(solution)/shard_map/all_to_all | solution.py:179
  84.9 0.4 copy.105
  85.3 60.5 %shard_map.96.field = f32[128,512]{1,0:T(8,128)S(1)} custom-call(f32[8]{0:T(128)S(1)} %stack.94.coef, f32[32,17408]{1,0:T(8,128)S(1)} %bitcast.82, f32[8,128]{1,0:T(8,128)S(1)} %broadcast_in_dim.6.field, f32[384,384]{1,0:T(8,128)S(1)} %pad.10.matrix), custom_call_target="tpu_custom_call" | custom-call | flops 89999998976 | bytes 300000000 | tf_op jit(solution)/shard_map/pallas_call | solution.py:427
  145.8 0.8 reshape.77
  146.6 12.0 %all-to-all-start.3 = ((f32[128,4,128]{2,1,0:T(4,128)}), f32[128,4,128]{2,1,0:T(4,128)}, u32[]{:S(2)}, u32[]{:S(2)}) async-start(f32[128,4,128]{2,1,0:T(4,128)} %reshape.77), calls=%async_computation.3 | async-start | bytes 524288 | tf_op jit(solution)/shard_map/all_to_all | solution.py:482
  158.6 10.7 %shard_map.97 = f32[128,512]{1,0:T(8,128)S(1)} custom-call(f32[8]{0:T(128)S(1)} %stack.94.coef, f32[32,17408]{1,0:T(8,128)S(1)} %bitcast.83, f32[128,512]{1,0:T(8,128)S(1)} %shard_map.96.field, f32[384,384]{1,0:T(8,128)S(1)} %pad.10.matrix), custom_call_target="tpu_custom_call" | custom-call | flops 15000000512 | bytes 50000000 | tf_op jit(solution)/shard_map/pallas_call | solution.py:427
  169.3 0.8 reshape.80
  170.1 8.1 %all-to-all-done.3 = f32[128,4,128]{2,1,0:T(4,128)} async-done(((f32[128,4,128]{2,1,0:T(4,128)}), f32[128,4,128]{2,1,0:T(4,128)}, u32[]{:S(2)}, u32[]{:S(2)}) %all-to-all-start.3) | async-done | bytes 262176 | tf_op jit(solution)/shard_map/all_to_all | solution.py:482
  178.1 8.9 %all-to-all-start.4 = ((f32[128,4,128]{2,1,0:T(4,128)}), f32[128,4,128]{2,1,0:T(4,128)S(1)}, u32[]{:S(2)}, u32[]{:S(2)}) async-start(f32[128,4,128]{2,1,0:T(4,128)} %reshape.80), calls=%async_computation.4 | async-start | bytes 524288 | tf_op jit(solution)/shard_map/all_to_all | solution.py:482
  187.0 1.1 copy.89
  188.1 3.1 %collective-permute-start = (f32[128,512]{0,1:T(8,128)S(1)}, f32[128,512]{0,1:T(8,128)S(1)}, u32[]{:S(2)}, u32[]{:S(2)}) collective-permute-start(f32[128,512]{0,1:T(8,128)S(1)} %bitcast.92), channel_id=1, source_target_pairs={{128,0},{160,32},{192,64},{224,96},{0,128},{32,160},{64,192},{96,2... | collective-permute-start | bytes 786440 | tf_op jit(solution)/shard_map/ppermute | solution.py:63
  191.2 3.7 %collective-permute-start.5 = (f32[128,512]{0,1:T(8,128)S(1)}, f32[128,512]{0,1:T(8,128)S(1)}, u32[]{:S(2)}, u32[]{:S(2)}) collective-permute-start(f32[128,512]{0,1:T(8,128)S(1)} %bitcast.93), channel_id=1, source_target_pairs={{384,0},{416,32},{448,64},{480,96},{256,128},{288,160},{320,192},{... | collective-permute-start | bytes 786440 | tf_op jit(solution)/shard_map/ppermute | solution.py:63
  195.0 2.8 %collective-permute-start.4 = (f32[128,512]{0,1:T(8,128)S(1)}, f32[128,512]{0,1:T(8,128)S(1)}, u32[]{:S(2)}, u32[]{:S(2)}) collective-permute-start(f32[128,512]{0,1:T(8,128)S(1)} %bitcast.94), channel_id=1, source_target_pairs={{256,0},{288,32},{320,64},{352,96},{384,128},{416,160},{448,192},{... | collective-permute-start | bytes 786440 | tf_op jit(solution)/shard_map/ppermute | solution.py:63
  197.7 9.1 %all-to-all-done.4 = f32[128,4,128]{2,1,0:T(4,128)S(1)} async-done(((f32[128,4,128]{2,1,0:T(4,128)}), f32[128,4,128]{2,1,0:T(4,128)S(1)}, u32[]{:S(2)}, u32[]{:S(2)}) %all-to-all-start.4) | async-done | bytes 262176 | tf_op jit(solution)/shard_map/all_to_all | solution.py:482
  207.0 0.6 convolution_bitcast_fusion
  207.6 0.6 fusion.11
  208.2 0.6 fusion.12
  208.8 0.6 select_select_fusion.3
  209.8 0.2 maximum_bitcast_fusion.1
  210.1 0.2 copy.98
  210.3 11.9 %all_to_all.42 = f32[8,4,4,512]{3,2,1,0:T(4,128)S(1)} all-to-all(f32[8,4,4,512]{3,2,1,0:T(4,128)S(1)} %copy.98), channel_id=1, replica_groups={{0,1,2,3,4,5,6,7},{8,9,10,11,12,13,14,15},{16,17,18,19,20,21,22,23},{24..., dimensions={0} | all-to-all | bytes 524288 | tf_op jit(solution)/shard_map/all_to_all | solution.py:500
  222.2 0.7 broadcast_in_dim.7
  222.9 10.6 %all-to-all-start.6 = ((f32[16,4,512]{2,1,0:T(4,128)}), f32[16,4,512]{2,1,0:T(4,128)S(1)}, u32[]{:S(2)}, u32[]{:S(2)}) async-start(f32[16,4,512]{2,1,0:T(4,128)} %bitcast.36), calls=%async_computation.6 | async-start | bytes 262144 | tf_op jit(solution)/shard_map/all_to_all | solution.py:504
  233.7 3.2 %collective-permute-start.1 = (f32[32,512]{1,0:T(8,128)S(1)}, f32[32,512]{1,0:T(8,128)S(1)}, u32[]{:S(2)}, u32[]{:S(2)}) collective-permute-start(f32[32,512]{1,0:T(8,128)S(1)} %get-tuple-element.30), channel_id=1, source_target_pairs={{32,0},{0,32},{96,64},{64,96},{160,128},{128,160},{224,192},{192,2... | collective-permute-start | bytes 196616 | tf_op jit(solution)/shard_map/ppermute | solution.py:63
  237.0 4.0 %collective-permute-start.2 = (f32[32,512]{1,0:T(8,128)S(1)}, f32[32,512]{1,0:T(8,128)S(1)}, u32[]{:S(2)}, u32[]{:S(2)}) collective-permute-start(f32[32,512]{1,0:T(8,128)S(1)} %get-tuple-element.29), channel_id=1, source_target_pairs={{64,0},{96,32},{0,64},{32,96},{192,128},{224,160},{128,192},{160,2... | collective-permute-start | bytes 196616 | tf_op jit(solution)/shard_map/ppermute | solution.py:63
  241.0 2.0 collective-permute-start.3
  243.0 2.9 %all-to-all-done.6 = f32[16,4,512]{2,1,0:T(4,128)S(1)} async-done(((f32[16,4,512]{2,1,0:T(4,128)}), f32[16,4,512]{2,1,0:T(4,128)S(1)}, u32[]{:S(2)}, u32[]{:S(2)}) %all-to-all-start.6) | async-done | bytes 131104 | tf_op jit(solution)/shard_map/all_to_all | solution.py:504
  246.0 2.4 collective-permute-done.3
  248.3 0.6 broadcast_in_dim.8
  249.0 6.0 %all-to-all-start.7 = ((f32[8,4,512]{2,1,0:T(4,128)}), f32[8,4,512]{2,1,0:T(4,128)S(1)}, u32[]{:S(2)}, u32[]{:S(2)}) async-start(f32[8,4,512]{2,1,0:T(4,128)} %broadcast_in_dim.8), calls=%async_computation.7 | async-start | bytes 131072 | tf_op jit(solution)/shard_map/all_to_all | solution.py:59
  255.0 0.7 copy.102
  255.8 4.1 %all-to-all-done.7 = f32[8,4,512]{2,1,0:T(4,128)S(1)} async-done(((f32[8,4,512]{2,1,0:T(4,128)}), f32[8,4,512]{2,1,0:T(4,128)S(1)}, u32[]{:S(2)}, u32[]{:S(2)}) %all-to-all-start.7) | async-done | bytes 65568 | tf_op jit(solution)/shard_map/all_to_all | solution.py:59
  259.8 0.7 reshape.85
  (48 shorter events, 2.0 us)
Async XLA Ops:
  9.8 0.7 copy-start
  10.5 0.7 copy-start.1
  11.2 0.7 copy-start.2
  11.9 0.7 copy-start.3
  56.5 4.3 %copy-start.5 = (f32[3]{0:T(128)S(1)}, f32[3]{0:T(128)}, u32[]{:S(2)}) copy-start(f32[3]{0:T(128)} %param.15) | copy-start | bytes 40
  56.5 8.5 %copy-start.4 = (f32[343,343]{1,0:T(8,128)S(1)}, f32[343,343]{1,0:T(8,128)}, u32[]{:S(2)}) copy-start(f32[343,343]{1,0:T(8,128)} %param.11) | copy-start | bytes 1411792
  56.5 20.0 %all-to-all-start.1 = ((f32[4,4,152,128]{3,2,1,0:T(8,128)}), f32[4,4,152,128]{3,2,1,0:T(8,128)S(1)}, u32[]{:S(2)}, u32[]{:S(2)}) async-start(f32[4,4,152,128]{3,2,1,0:T(8,128)} %pad_maximum_fusion.1), calls=%async_computation.1 | async-start | bytes 2490368 | tf_op jit(solution)/shard_map/all_to_all | solution.py:179
  146.6 31.5 %all-to-all-start.3 = ((f32[128,4,128]{2,1,0:T(4,128)}), f32[128,4,128]{2,1,0:T(4,128)}, u32[]{:S(2)}, u32[]{:S(2)}) async-start(f32[128,4,128]{2,1,0:T(4,128)} %reshape.77), calls=%async_computation.3 | async-start | bytes 524288 | tf_op jit(solution)/shard_map/all_to_all | solution.py:482
  178.1 28.8 %all-to-all-start.4 = ((f32[128,4,128]{2,1,0:T(4,128)}), f32[128,4,128]{2,1,0:T(4,128)S(1)}, u32[]{:S(2)}, u32[]{:S(2)}) async-start(f32[128,4,128]{2,1,0:T(4,128)} %reshape.80), calls=%async_computation.4 | async-start | bytes 524288 | tf_op jit(solution)/shard_map/all_to_all | solution.py:482
  188.1 19.5 %collective-permute-start = (f32[128,512]{0,1:T(8,128)S(1)}, f32[128,512]{0,1:T(8,128)S(1)}, u32[]{:S(2)}, u32[]{:S(2)}) collective-permute-start(f32[128,512]{0,1:T(8,128)S(1)} %bitcast.92), channel_id=1, source_target_pairs={{128,0},{160,32},{192,64},{224,96},{0,128},{32,160},{64,192},{96,2... | collective-permute-start | bytes 786440 | tf_op jit(solution)/shard_map/ppermute | solution.py:63
  191.2 17.0 %collective-permute-start.5 = (f32[128,512]{0,1:T(8,128)S(1)}, f32[128,512]{0,1:T(8,128)S(1)}, u32[]{:S(2)}, u32[]{:S(2)}) collective-permute-start(f32[128,512]{0,1:T(8,128)S(1)} %bitcast.93), channel_id=1, source_target_pairs={{384,0},{416,32},{448,64},{480,96},{256,128},{288,160},{320,192},{... | collective-permute-start | bytes 786440 | tf_op jit(solution)/shard_map/ppermute | solution.py:63
  195.0 13.9 %collective-permute-start.4 = (f32[128,512]{0,1:T(8,128)S(1)}, f32[128,512]{0,1:T(8,128)S(1)}, u32[]{:S(2)}, u32[]{:S(2)}) collective-permute-start(f32[128,512]{0,1:T(8,128)S(1)} %bitcast.94), channel_id=1, source_target_pairs={{256,0},{288,32},{320,64},{352,96},{384,128},{416,160},{448,192},{... | collective-permute-start | bytes 786440 | tf_op jit(solution)/shard_map/ppermute | solution.py:63
  222.9 23.0 %all-to-all-start.6 = ((f32[16,4,512]{2,1,0:T(4,128)}), f32[16,4,512]{2,1,0:T(4,128)S(1)}, u32[]{:S(2)}, u32[]{:S(2)}) async-start(f32[16,4,512]{2,1,0:T(4,128)} %bitcast.36), calls=%async_computation.6 | async-start | bytes 262144 | tf_op jit(solution)/shard_map/all_to_all | solution.py:504
  233.7 12.2 %collective-permute-start.1 = (f32[32,512]{1,0:T(8,128)S(1)}, f32[32,512]{1,0:T(8,128)S(1)}, u32[]{:S(2)}, u32[]{:S(2)}) collective-permute-start(f32[32,512]{1,0:T(8,128)S(1)} %get-tuple-element.30), channel_id=1, source_target_pairs={{32,0},{0,32},{96,64},{64,96},{160,128},{128,160},{224,192},{192,2... | collective-permute-start | bytes 196616 | tf_op jit(solution)/shard_map/ppermute | solution.py:63
  237.0 9.0 %collective-permute-start.2 = (f32[32,512]{1,0:T(8,128)S(1)}, f32[32,512]{1,0:T(8,128)S(1)}, u32[]{:S(2)}, u32[]{:S(2)}) collective-permute-start(f32[32,512]{1,0:T(8,128)S(1)} %get-tuple-element.29), channel_id=1, source_target_pairs={{64,0},{96,32},{0,64},{32,96},{192,128},{224,160},{128,192},{160,2... | collective-permute-start | bytes 196616 | tf_op jit(solution)/shard_map/ppermute | solution.py:63
  241.0 7.4 %collective-permute-start.3 = (f32[32,512]{1,0:T(8,128)S(1)}, f32[32,512]{1,0:T(8,128)S(1)}, u32[]{:S(2)}, u32[]{:S(2)}) collective-permute-start(f32[32,512]{1,0:T(8,128)S(1)} %get-tuple-element.28), channel_id=1, source_target_pairs={{96,0},{64,32},{32,64},{0,96},{224,128},{192,160},{160,192},{128,2... | collective-permute-start | bytes 196616 | tf_op jit(solution)/shard_map/ppermute | solution.py:63
  249.0 10.9 %all-to-all-start.7 = ((f32[8,4,512]{2,1,0:T(4,128)}), f32[8,4,512]{2,1,0:T(4,128)S(1)}, u32[]{:S(2)}, u32[]{:S(2)}) async-start(f32[8,4,512]{2,1,0:T(4,128)} %broadcast_in_dim.8), calls=%async_computation.7 | async-start | bytes 131072 | tf_op jit(solution)/shard_map/all_to_all | solution.py:59

commit v6 on v5

--- a/solution.py
+++ b/solution.py
@@ -73,14 +73,7 @@
     return [kept] + [swapped(p, axis, size, (d + 1) * unit) for d, p in enumerate(sent)], mine
 
 
-def table_kernel(
-    ordered, slots_in, send_in, pot_in, cell_scale_in, node_count, out,
-    hot_high, hot_low, slots, send, pot, cell_scale, arrival,
-):
-    fetched = ((slots_in, slots), (send_in, send), (pot_in, pot), (cell_scale_in, cell_scale))
-    fetches = [pltpu.make_async_copy(a, b, arrival.at[i]) for i, (a, b) in enumerate(fetched)]
-    for fetch in fetches:
-        fetch.start()
+def table_kernel(ordered, slots, send, pot, cell_scale, node_count, out, hot_high, hot_low):
     shape = (32, 128)
     row = lax.broadcasted_iota(jnp.int32, shape, 0)
     lane = lax.broadcasted_iota(jnp.int32, shape, 1)
@@ -122,15 +115,9 @@
     up_to = along_rows(count, jnp.add)
     end = jnp.where(count > 0.0, up_to - 1.0, -1.0)
 
-    for fetch in fetches:
-        fetch.wait()
     nodes = slots[...]
-    nodes = jnp.where(nodes >= NODES, nodes - NODES, nodes + GHOSTS).astype(jnp.float32)
-    out[IDX_AT:POS_AT, :] = jnp.zeros((POS_AT - IDX_AT, 128), jnp.float32)
-    for c in range(CELLS):
-        for k in range(CELL_CHUNKS):
-            at, width = IDX_AT + c * CELL_CHUNKS + k, min(128, NPC - k * 128)
-            out[at : at + 1, 0:width] = nodes[c : c + 1, k * 128 : k * 128 + width]
+    nodes = jnp.where(nodes >= NODES, nodes - NODES, nodes + GHOSTS)
+    out[IDX_AT:POS_AT, :] = nodes.astype(jnp.float32)
     out[POS_AT:PLACE_AT, :] = position[:ENTRY_CHUNKS]
     out[PLACE_AT:END_AT, :] = place[:ENTRY_CHUNKS]
     out[END_AT:SEND_AT, :] = end[: EXT // 128]
@@ -152,23 +139,19 @@
     keys = jnp.concatenate([shifted.reshape(-1), send_list.reshape(-1) + GHOSTS])
     ordered = lax.sort(keys * 4096 + lax.iota(jnp.int32, ENTRIES))
     ordered = jnp.pad(ordered, (0, 4096 - ENTRIES), constant_values=PAD_NODE * 4096).reshape(32, 128)
+    slots = jnp.pad(cell_nodes, ((0, 0), (0, NPC_PAD - NPC))).reshape(CELLS * CELL_CHUNKS, 128)
     vmem = pl.BlockSpec(memory_space=pltpu.VMEM)
     return pl.pallas_call(
         table_kernel,
         out_shape=jax.ShapeDtypeStruct((START_AT, 128), jnp.float32),
-        in_specs=[vmem] + [pl.BlockSpec(memory_space=pltpu.HBM)] * 4 + [pl.BlockSpec(memory_space=pltpu.SMEM)],
+        in_specs=[vmem] * 5 + [pl.BlockSpec(memory_space=pltpu.SMEM)],
         out_specs=vmem,
         scratch_shapes=[
             pltpu.VMEM((32, ENTRY_PAD), jnp.bfloat16),
             pltpu.VMEM((128, ENTRY_PAD), jnp.bfloat16),
-            pltpu.VMEM((CELLS, NPC), jnp.int32),
-            pltpu.VMEM((4, SLOTS), jnp.int32),
-            pltpu.VMEM((NODES // 128, 128), jnp.float32),
-            pltpu.VMEM((1, CELLS), jnp.float32),
-            pltpu.SemaphoreType.DMA((4,)),
         ],
         compiler_params=pltpu.CompilerParams(vmem_limit_bytes=16 * 1024 * 1024),
-    )(ordered, cell_nodes, send_list, potential.reshape(NODES // 128, 128), cell_scale.reshape(1, CELLS), node_count)
+    )(ordered, slots, send_list, potential.reshape(NODES // 128, 128), cell_scale.reshape(1, CELLS), node_count)
 
 
 def gathered_tables(own_table, vectors):
@@ -242,10 +225,9 @@
         outside = jnp.maximum(outside, jnp.where(missed, 1.0, 0.0))
     short &= jnp.max(outside).astype(jnp.int32) == 0
 
-    quarter = NODES // 4
     if last:
-        for q in range(4):
-            cur[:, q * quarter : (q + 1) * quarter] = field[q * 32 : (q + 1) * 32, :]
+        for c in range(NODES // 128):
+            cur[:, chunk(c)] = field[c // 4 * 32 : (c // 4 + 1) * 32, c % 4, :]
     else:
         live = misc(0).astype(jnp.int32)
         node = lax.broadcasted_iota(jnp.int32, (PARTS, NODES), 1)
@@ -415,8 +397,8 @@
             cur[:, chunk(c)] = sums[:, chunk(c)] + table[:, chunk(POT_AT + c)] * cur[:, chunk(c)]
     else:
         lax.fori_loop(0, step_count, step, 0)
-    for q in range(4):
-        out[q * 32 : (q + 1) * 32, :] = cur[:, q * quarter : (q + 1) * quarter]
+    for c in range(NODES // 128):
+        out[c // 4 * 32 : (c // 4 + 1) * 32, c % 4, :] = cur[:, chunk(c)]
 
 
 def run_filter(coef, table, field, cell_matrix, step_count, last):
@@ -426,7 +408,7 @@
     cells = CELLS * PARTS
     return pl.pallas_call(
         functools.partial(filter_kernel, step_count, last),
-        out_shape=jax.ShapeDtypeStruct((4 * PARTS, NODES // 4), f32),
+        out_shape=jax.ShapeDtypeStruct((4 * PARTS, NODES // 512, 128), f32),
         in_specs=[pl.BlockSpec(memory_space=pltpu.SMEM)] + [vmem] * 3,
         out_specs=vmem,
         scratch_shapes=[
@@ -478,8 +460,7 @@
     quarters = groups_of(16 * PARTS, (1, 2, 4, 8, 16, PARTS, 2 * PARTS))
 
     def to_quarters(field):
-        pieces = field.reshape(4 * PARTS, NODES // 512, 128)
-        pieces = lax.all_to_all(pieces, ("band", "mesh"), 0, 0, axis_index_groups=quarters)
+        pieces = lax.all_to_all(field, ("band", "mesh"), 0, 0, axis_index_groups=quarters)
         return pieces.reshape(4 * PARTS, NODES // 4)
 
     f = run_filter(coef, table, jnp.zeros((8, 128), jnp.float32), cell_matrix, 2 * DEGREE, False)

time: 262 us -> 258 us (0.985)
  local copies, waits for them, and re-layouts: 11.7 us -> 7.18 us
  transfers between devices with their start and end apart: 11 -> 11, of which waited for: 6 -> 6; matrix products, arithmetic and copies ran while one was open for 2% -> 1% of each run, Pallas kernels for 4% -> 5%
where the time goes in v6:
time: 258 us; the launch traced here: 257 us
  Pallas kernels  74.5 us (29%)
  blocking collectives  60.8 us (24%)
  starting transfers between devices  59.8 us (23%)
  waiting for transfers between devices  38.5 us (15%)
  other arithmetic  9.54 us (4%)
  local copies, waits for them, and re-layouts  7.18 us (3%)
  between operations  5.28 us (2%)
    pallas_call x2, Pallas kernels, run_filter(): pl.pallas_call(functools.partial(filter_kernel, step_count, last), out_sh...  73.4 us
    all_to_all x2, blocking collectives, next_step(): lax.all_to_all(operand, 'mesh', 0, 0, axis_index_groups=groups_of(PARTS,...  48.9 us
    all_to_all x2, starting transfers between devices, to_quarters(): lax.all_to_all(field, ('band', 'mesh'), 0, 0, axis_index_groups=quarters)  20.4 us
    ppermute x6, starting transfers between devices, swapped(): return lax.ppermute(block, axis, [(i ^ distance, i) for i in range(size)])  18.9 us
    all_to_all x2, waiting for transfers between devices, to_quarters(): lax.all_to_all(field, ('band', 'mesh'), 0, 0, axis_index_groups=quarters)  18 us
    all_to_all x1, blocking collectives, body(): lax.all_to_all(partial, 'mesh', 0, 0, axis_index_groups=plane).sum(0)  11.9 us
    all_to_all x1, waiting for transfers between devices, next_step(): lax.all_to_all(operand, 'mesh', 0, 0, axis_index_groups=groups_of(PARTS,...  11.4 us
    all_to_all x1, starting transfers between devices, body(): lax.all_to_all(partial, ('band', 'mesh'), 0, 0, axis_index_groups=along_z)  10.1 us
  transfers between devices with their start and end apart: 11, of which 6 were waited for; matrix products, arithmetic and copies ran while one was open for 1% of the time, Pallas kernels for 5%

profile of v6, /device:TPU:1, one launch (start us, length us, event | category | flops | bytes accessed | tf_op | source)
XLA Modules:
  0.0 257.1 jit_solution(2396159254957750635)
XLA Ops:
  0.7 1.0 fusion.20
  1.7 0.7 add_select_fusion
  2.5 0.7 add_bitcast_fusion
  3.3 5.9 %sort.14 = (s32[3256]{0:T(1024)S(1)}, s32[3256]{0:T(1024)}) sort(s32[3256]{0:T(1024)S(1)} %fusion.18, s32[3256]{0:T(1024)S(1)} %iota.7), dimensions={0}, to_apply=%region_0.1 | sort | flops 39072 | bytes 52096 | tf_op jit(solution)/shard_map/sort | solution.py:140
  9.2 0.7 pad.14
  10.6 1.1 shard_map.95
  11.8 41.3 %all_to_all.40 = f32[4,248,128]{2,1,0:T(8,128)S(1)} all-to-all(f32[4,248,128]{2,1,0:T(8,128)S(1)} %pad_maximum_fusion.2), channel_id=1, replica_groups={{0,8,16,24},{1,9,17,25},{2,10,18,26},{3,11,19,27},{4,12,20,28},{5,13,21..., dimensions={0} | all-to-all | bytes 1015808 | tf_op jit(solution)/shard_map/all_to_all | solution.py:162
  53.2 0.1 fusion
  53.3 1.2 pad_maximum_fusion.1
  54.4 4.3 %all-to-all-start.1 = ((f32[4,4,152,128]{3,2,1,0:T(8,128)}), f32[4,4,152,128]{3,2,1,0:T(8,128)S(1)}, u32[]{:S(2)}, u32[]{:S(2)}) async-start(f32[4,4,152,128]{3,2,1,0:T(8,128)} %pad_maximum_fusion.1), calls=%async_computation.1 | async-start | bytes 2490368 | tf_op jit(solution)/shard_map/all_to_all | solution.py:162
  58.8 0.6 fusion.21
  62.9 0.1 stack.94.coef
  63.0 11.4 %all-to-all-done.1 = f32[4,4,152,128]{3,2,1,0:T(8,128)S(1)} async-done(((f32[4,4,152,128]{3,2,1,0:T(8,128)}), f32[4,4,152,128]{3,2,1,0:T(8,128)S(1)}, u32[]{:S(2)}, u32[]{:S(2)}) %all-to-all-start.1) | async-done | bytes 1245216 | tf_op jit(solution)/shard_map/all_to_all | solution.py:162
  74.7 0.1 pad_maximum_fusion
  74.9 0.2 copy.56
  75.1 7.6 %all_to_all.41 = f32[2,4,4,136,128]{4,3,1,2,0:T(8,128)S(1)} all-to-all(f32[2,4,4,136,128]{4,3,1,2,0:T(8,128)S(1)} %copy.56), channel_id=1, replica_groups={{0,1},{2,3},{4,5},{6,7},{8,9},{10,11},{12,13},{14,15},{16,17},{18,19},{..., dimensions={0} | all-to-all | bytes 4456448 | tf_op jit(solution)/shard_map/all_to_all | solution.py:162
  82.6 0.2 copy.57
  82.8 0.4 copy.94
  83.2 61.4 %shard_map.96.field = f32[128,4,128]{2,1,0:T(4,128)} custom-call(f32[8]{0:T(128)S(1)} %stack.94.coef, f32[32,17408]{1,0:T(8,128)S(1)} %bitcast.86, f32[8,128]{1,0:T(8,128)S(1)} %broadcast_in_dim.6.field, f32[384,384]{1,0:T(8,128)S(1)} %pad.15.matrix), custom_call_target="tpu_custom_call" | custom-call | flops 89999998976 | bytes 300000000 | tf_op jit(solution)/shard_map/pallas_call | solution.py:409
  144.6 11.5 %all-to-all-start.3 = ((f32[128,4,128]{2,1,0:T(4,128)}), f32[128,4,128]{2,1,0:T(4,128)S(1)}, u32[]{:S(2)}, u32[]{:S(2)}) async-start(f32[128,4,128]{2,1,0:T(4,128)} %shard_map.96.field), calls=%async_computation.3 | async-start | bytes 524288 | tf_op jit(solution)/shard_map/all_to_all | solution.py:463
  156.1 12.0 %shard_map.97 = f32[128,4,128]{2,1,0:T(4,128)} custom-call(f32[8]{0:T(128)S(1)} %stack.94.coef, f32[32,17408]{1,0:T(8,128)S(1)} %bitcast.87, f32[128,4,128]{2,1,0:T(4,128)} %shard_map.96.field, f32[384,384]{1,0:T(8,128)S(1)} %pad.15.matrix), custom_call_target="tpu_custom_call" | custom-call | flops 15000000512 | bytes 50000000 | tf_op jit(solution)/shard_map/pallas_call | solution.py:409
  168.1 7.8 %all-to-all-done.3 = f32[128,4,128]{2,1,0:T(4,128)S(1)} async-done(((f32[128,4,128]{2,1,0:T(4,128)}), f32[128,4,128]{2,1,0:T(4,128)S(1)}, u32[]{:S(2)}, u32[]{:S(2)}) %all-to-all-start.3) | async-done | bytes 262176 | tf_op jit(solution)/shard_map/all_to_all | solution.py:463
  176.0 8.9 %all-to-all-start.4 = ((f32[128,4,128]{2,1,0:T(4,128)}), f32[128,4,128]{2,1,0:T(4,128)S(1)}, u32[]{:S(2)}, u32[]{:S(2)}) async-start(f32[128,4,128]{2,1,0:T(4,128)} %shard_map.97), calls=%async_computation.4 | async-start | bytes 524288 | tf_op jit(solution)/shard_map/all_to_all | solution.py:463
  184.9 3.1 %collective-permute-start = (f32[128,512]{1,0:T(8,128)S(1)}, f32[128,512]{1,0:T(8,128)S(1)}, u32[]{:S(2)}, u32[]{:S(2)}) collective-permute-start(f32[128,512]{1,0:T(8,128)S(1)} %bitcast.97), channel_id=1, source_target_pairs={{128,0},{160,32},{192,64},{224,96},{0,128},{32,160},{64,192},{96,2... | collective-permute-start | bytes 786440 | tf_op jit(solution)/shard_map/ppermute | solution.py:63
  188.1 3.7 %collective-permute-start.5 = (f32[128,512]{1,0:T(8,128)S(1)}, f32[128,512]{1,0:T(8,128)S(1)}, u32[]{:S(2)}, u32[]{:S(2)}) collective-permute-start(f32[128,512]{1,0:T(8,128)S(1)} %bitcast.98), channel_id=1, source_target_pairs={{384,0},{416,32},{448,64},{480,96},{256,128},{288,160},{320,192},{... | collective-permute-start | bytes 786440 | tf_op jit(solution)/shard_map/ppermute | solution.py:63
  191.8 2.8 %collective-permute-start.4 = (f32[128,512]{1,0:T(8,128)S(1)}, f32[128,512]{1,0:T(8,128)S(1)}, u32[]{:S(2)}, u32[]{:S(2)}) collective-permute-start(f32[128,512]{1,0:T(8,128)S(1)} %bitcast.99), channel_id=1, source_target_pairs={{256,0},{288,32},{320,64},{352,96},{384,128},{416,160},{448,192},{... | collective-permute-start | bytes 786440 | tf_op jit(solution)/shard_map/ppermute | solution.py:63
  194.6 10.2 %all-to-all-done.4 = f32[128,4,128]{2,1,0:T(4,128)S(1)} async-done(((f32[128,4,128]{2,1,0:T(4,128)}), f32[128,4,128]{2,1,0:T(4,128)S(1)}, u32[]{:S(2)}, u32[]{:S(2)}) %all-to-all-start.4) | async-done | bytes 262176 | tf_op jit(solution)/shard_map/all_to_all | solution.py:463
  204.8 0.4 convolution_bitcast_fusion
  205.2 0.4 fusion.7
  205.6 0.4 fusion.3
  206.0 0.4 select_select_fusion.4
  206.7 0.2 maximum_bitcast_fusion.1
  206.9 0.1 reshape.78
  207.0 0.2 copy.64
  207.2 11.9 %all_to_all.42 = f32[8,4,4,512]{3,2,1,0:T(4,128)S(1)} all-to-all(f32[8,4,4,512]{3,2,1,0:T(4,128)S(1)} %copy.64), channel_id=1, replica_groups={{0,1,2,3,4,5,6,7},{8,9,10,11,12,13,14,15},{16,17,18,19,20,21,22,23},{24..., dimensions={0} | all-to-all | bytes 524288 | tf_op jit(solution)/shard_map/all_to_all | solution.py:481
  219.1 0.7 broadcast_in_dim.7
  219.8 10.1 %all-to-all-start.6 = ((f32[16,4,512]{2,1,0:T(4,128)}), f32[16,4,512]{2,1,0:T(4,128)S(1)}, u32[]{:S(2)}, u32[]{:S(2)}) async-start(f32[16,4,512]{2,1,0:T(4,128)} %bitcast.34), calls=%async_computation.6 | async-start | bytes 262144 | tf_op jit(solution)/shard_map/all_to_all | solution.py:485
  230.0 3.2 %collective-permute-start.1 = (f32[32,512]{1,0:T(8,128)S(1)}, f32[32,512]{1,0:T(8,128)S(1)}, u32[]{:S(2)}, u32[]{:S(2)}) collective-permute-start(f32[32,512]{1,0:T(8,128)S(1)} %get-tuple-element.30), channel_id=1, source_target_pairs={{32,0},{0,32},{96,64},{64,96},{160,128},{128,160},{224,192},{192,2... | collective-permute-start | bytes 196616 | tf_op jit(solution)/shard_map/ppermute | solution.py:63
  233.2 4.0 %collective-permute-start.2 = (f32[32,512]{1,0:T(8,128)S(1)}, f32[32,512]{1,0:T(8,128)S(1)}, u32[]{:S(2)}, u32[]{:S(2)}) collective-permute-start(f32[32,512]{1,0:T(8,128)S(1)} %get-tuple-element.29), channel_id=1, source_target_pairs={{64,0},{96,32},{0,64},{32,96},{192,128},{224,160},{128,192},{160,2... | collective-permute-start | bytes 196616 | tf_op jit(solution)/shard_map/ppermute | solution.py:63
  237.2 2.1 collective-permute-start.3
  239.3 3.0 %all-to-all-done.6 = f32[16,4,512]{2,1,0:T(4,128)S(1)} async-done(((f32[16,4,512]{2,1,0:T(4,128)}), f32[16,4,512]{2,1,0:T(4,128)S(1)}, u32[]{:S(2)}, u32[]{:S(2)}) %all-to-all-start.6) | async-done | bytes 131104 | tf_op jit(solution)/shard_map/all_to_all | solution.py:485
  242.4 2.2 collective-permute-done.3
  244.9 0.6 broadcast_in_dim.8
  245.5 6.0 %all-to-all-start.7 = ((f32[8,4,512]{2,1,0:T(4,128)}), f32[8,4,512]{2,1,0:T(4,128)S(1)}, u32[]{:S(2)}, u32[]{:S(2)}) async-start(f32[8,4,512]{2,1,0:T(4,128)} %broadcast_in_dim.8), calls=%async_computation.7 | async-start | bytes 131072 | tf_op jit(solution)/shard_map/all_to_all | solution.py:59
  251.6 0.3 pad_maximum_fusion.6
  251.8 0.8 copy.73
  252.6 3.8 %all-to-all-done.7 = f32[8,4,512]{2,1,0:T(4,128)S(1)} async-done(((f32[8,4,512]{2,1,0:T(4,128)}), f32[8,4,512]{2,1,0:T(4,128)S(1)}, u32[]{:S(2)}, u32[]{:S(2)}) %all-to-all-start.7) | async-done | bytes 65568 | tf_op jit(solution)/shard_map/all_to_all | solution.py:59
  256.4 0.7 reshape.81
  (48 shorter events, 1.4 us)
Async XLA Ops:
  0.6 9.9 %copy-start.1 = (s32[1,4,128]{2,1,0:T(4,128)S(1)}, s32[1,4,128]{2,1,0:T(4,128)}, u32[]{:S(2)}) copy-start(s32[1,4,128]{2,1,0:T(4,128)} %param.13) | copy-start | bytes 6148
  0.6 9.9 %copy-start = (f32[2048]{0:T(1024)S(1)}, f32[2048]{0:T(1024)}, u32[]{:S(2)}) copy-start(f32[2048]{0:T(1024)} %param.9) | copy-start | bytes 24580
  0.7 9.9 %copy-start.2 = (f32[8]{0:T(128)S(1)}, f32[8]{0:T(128)}, u32[]{:S(2)}) copy-start(f32[8]{0:T(128)} %param.10) | copy-start | bytes 100
  54.4 4.3 %copy-start.4 = (f32[3]{0:T(128)S(1)}, f32[3]{0:T(128)}, u32[]{:S(2)}) copy-start(f32[3]{0:T(128)} %param.15) | copy-start | bytes 40
  54.4 8.5 %copy-start.3 = (f32[343,343]{1,0:T(8,128)S(1)}, f32[343,343]{1,0:T(8,128)}, u32[]{:S(2)}) copy-start(f32[343,343]{1,0:T(8,128)} %param.11) | copy-start | bytes 1411792
  54.4 20.0 %all-to-all-start.1 = ((f32[4,4,152,128]{3,2,1,0:T(8,128)}), f32[4,4,152,128]{3,2,1,0:T(8,128)S(1)}, u32[]{:S(2)}, u32[]{:S(2)}) async-start(f32[4,4,152,128]{3,2,1,0:T(8,128)} %pad_maximum_fusion.1), calls=%async_computation.1 | async-start | bytes 2490368 | tf_op jit(solution)/shard_map/all_to_all | solution.py:162
  144.6 31.4 %all-to-all-start.3 = ((f32[128,4,128]{2,1,0:T(4,128)}), f32[128,4,128]{2,1,0:T(4,128)S(1)}, u32[]{:S(2)}, u32[]{:S(2)}) async-start(f32[128,4,128]{2,1,0:T(4,128)} %shard_map.96.field), calls=%async_computation.3 | async-start | bytes 524288 | tf_op jit(solution)/shard_map/all_to_all | solution.py:463
  176.0 28.8 %all-to-all-start.4 = ((f32[128,4,128]{2,1,0:T(4,128)}), f32[128,4,128]{2,1,0:T(4,128)S(1)}, u32[]{:S(2)}, u32[]{:S(2)}) async-start(f32[128,4,128]{2,1,0:T(4,128)} %shard_map.97), calls=%async_computation.4 | async-start | bytes 524288 | tf_op jit(solution)/shard_map/all_to_all | solution.py:463
  184.9 20.2 %collective-permute-start = (f32[128,512]{1,0:T(8,128)S(1)}, f32[128,512]{1,0:T(8,128)S(1)}, u32[]{:S(2)}, u32[]{:S(2)}) collective-permute-start(f32[128,512]{1,0:T(8,128)S(1)} %bitcast.97), channel_id=1, source_target_pairs={{128,0},{160,32},{192,64},{224,96},{0,128},{32,160},{64,192},{96,2... | collective-permute-start | bytes 786440 | tf_op jit(solution)/shard_map/ppermute | solution.py:63
  188.1 17.5 %collective-permute-start.5 = (f32[128,512]{1,0:T(8,128)S(1)}, f32[128,512]{1,0:T(8,128)S(1)}, u32[]{:S(2)}, u32[]{:S(2)}) collective-permute-start(f32[128,512]{1,0:T(8,128)S(1)} %bitcast.98), channel_id=1, source_target_pairs={{384,0},{416,32},{448,64},{480,96},{256,128},{288,160},{320,192},{... | collective-permute-start | bytes 786440 | tf_op jit(solution)/shard_map/ppermute | solution.py:63
  191.8 14.2 %collective-permute-start.4 = (f32[128,512]{1,0:T(8,128)S(1)}, f32[128,512]{1,0:T(8,128)S(1)}, u32[]{:S(2)}, u32[]{:S(2)}) collective-permute-start(f32[128,512]{1,0:T(8,128)S(1)} %bitcast.99), channel_id=1, source_target_pairs={{256,0},{288,32},{320,64},{352,96},{384,128},{416,160},{448,192},{... | collective-permute-start | bytes 786440 | tf_op jit(solution)/shard_map/ppermute | solution.py:63
  219.8 22.5 %all-to-all-start.6 = ((f32[16,4,512]{2,1,0:T(4,128)}), f32[16,4,512]{2,1,0:T(4,128)S(1)}, u32[]{:S(2)}, u32[]{:S(2)}) async-start(f32[16,4,512]{2,1,0:T(4,128)} %bitcast.34), calls=%async_computation.6 | async-start | bytes 262144 | tf_op jit(solution)/shard_map/all_to_all | solution.py:485
  230.0 12.4 %collective-permute-start.1 = (f32[32,512]{1,0:T(8,128)S(1)}, f32[32,512]{1,0:T(8,128)S(1)}, u32[]{:S(2)}, u32[]{:S(2)}) collective-permute-start(f32[32,512]{1,0:T(8,128)S(1)} %get-tuple-element.30), channel_id=1, source_target_pairs={{32,0},{0,32},{96,64},{64,96},{160,128},{128,160},{224,192},{192,2... | collective-permute-start | bytes 196616 | tf_op jit(solution)/shard_map/ppermute | solution.py:63
  233.2 9.2 %collective-permute-start.2 = (f32[32,512]{1,0:T(8,128)S(1)}, f32[32,512]{1,0:T(8,128)S(1)}, u32[]{:S(2)}, u32[]{:S(2)}) collective-permute-start(f32[32,512]{1,0:T(8,128)S(1)} %get-tuple-element.29), channel_id=1, source_target_pairs={{64,0},{96,32},{0,64},{32,96},{192,128},{224,160},{128,192},{160,2... | collective-permute-start | bytes 196616 | tf_op jit(solution)/shard_map/ppermute | solution.py:63
  237.2 7.3 %collective-permute-start.3 = (f32[32,512]{1,0:T(8,128)S(1)}, f32[32,512]{1,0:T(8,128)S(1)}, u32[]{:S(2)}, u32[]{:S(2)}) collective-permute-start(f32[32,512]{1,0:T(8,128)S(1)} %get-tuple-element.28), channel_id=1, source_target_pairs={{96,0},{64,32},{32,64},{0,96},{224,128},{192,160},{160,192},{128,2... | collective-permute-start | bytes 196616 | tf_op jit(solution)/shard_map/ppermute | solution.py:63
  245.5 10.9 %all-to-all-start.7 = ((f32[8,4,512]{2,1,0:T(4,128)}), f32[8,4,512]{2,1,0:T(4,128)S(1)}, u32[]{:S(2)}, u32[]{:S(2)}) async-start(f32[8,4,512]{2,1,0:T(4,128)} %broadcast_in_dim.8), calls=%async_computation.7 | async-start | bytes 131072 | tf_op jit(solution)/shard_map/all_to_all | solution.py:59

commit v7 on v6

--- a/solution.py
+++ b/solution.py
@@ -115,13 +115,11 @@
     up_to = along_rows(count, jnp.add)
     end = jnp.where(count > 0.0, up_to - 1.0, -1.0)
 
-    nodes = slots[...]
-    nodes = jnp.where(nodes >= NODES, nodes - NODES, nodes + GHOSTS)
-    out[IDX_AT:POS_AT, :] = nodes.astype(jnp.float32)
+    out[IDX_AT:POS_AT, :] = slots[...].astype(jnp.float32)
     out[POS_AT:PLACE_AT, :] = position[:ENTRY_CHUNKS]
     out[PLACE_AT:END_AT, :] = place[:ENTRY_CHUNKS]
     out[END_AT:SEND_AT, :] = end[: EXT // 128]
-    out[SEND_AT:POT_AT, :] = send[...].astype(jnp.float32)
+    out[SEND_AT:POT_AT, :] = (send[...] - GHOSTS).astype(jnp.float32)
     out[POT_AT:MISC_AT, :] = pot[...]
     ghost_entries = jnp.broadcast_to(up_to[GHOSTS // 128 - 1 : GHOSTS // 128, 127:128], (1, 128))
     longest = jnp.max(place) + 1.0
@@ -136,10 +134,11 @@
 
 def partition_table(cell_nodes, send_list, potential, cell_scale, node_count):
     shifted = jnp.where(cell_nodes >= NODES, cell_nodes - NODES, cell_nodes + GHOSTS)
-    keys = jnp.concatenate([shifted.reshape(-1), send_list.reshape(-1) + GHOSTS])
+    send = send_list + GHOSTS
+    keys = jnp.concatenate([shifted.reshape(-1), send.reshape(-1)])
     ordered = lax.sort(keys * 4096 + lax.iota(jnp.int32, ENTRIES))
     ordered = jnp.pad(ordered, (0, 4096 - ENTRIES), constant_values=PAD_NODE * 4096).reshape(32, 128)
-    slots = jnp.pad(cell_nodes, ((0, 0), (0, NPC_PAD - NPC))).reshape(CELLS * CELL_CHUNKS, 128)
+    slots = jnp.pad(shifted, ((0, 0), (0, NPC_PAD - NPC))).reshape(CELLS * CELL_CHUNKS, 128)
     vmem = pl.BlockSpec(memory_space=pltpu.VMEM)
     return pl.pallas_call(
         table_kernel,
@@ -151,7 +150,7 @@
             pltpu.VMEM((128, ENTRY_PAD), jnp.bfloat16),
         ],
         compiler_params=pltpu.CompilerParams(vmem_limit_bytes=16 * 1024 * 1024),
-    )(ordered, slots, send_list, potential.reshape(NODES // 128, 128), cell_scale.reshape(1, CELLS), node_count)
+    )(ordered, slots, send, potential.reshape(NODES // 128, 128), cell_scale.reshape(1, CELLS), node_count)
 
 
 def gathered_tables(own_table, vectors):

time: 258 us -> 257 us (level)
  no operation moved by 1% of the time
where the time goes in v7:
time: 257 us; the launch traced here: 256 us
  Pallas kernels  74.5 us (29%)
  blocking collectives  60.8 us (24%)
  starting transfers between devices  59.8 us (23%)
  waiting for transfers between devices  38.5 us (15%)
  other arithmetic  9.55 us (4%)
  local copies, waits for them, and re-layouts  6.45 us (3%)
  between operations  5.27 us (2%)
    pallas_call x2, Pallas kernels, run_filter(): pl.pallas_call(functools.partial(filter_kernel, step_count, last), out_sh...  73.4 us
    all_to_all x2, blocking collectives, next_step(): lax.all_to_all(operand, 'mesh', 0, 0, axis_index_groups=groups_of(PARTS,...  48.9 us
    all_to_all x2, starting transfers between devices, to_quarters(): lax.all_to_all(field, ('band', 'mesh'), 0, 0, axis_index_groups=quarters)  20.4 us
    ppermute x6, starting transfers between devices, swapped(): return lax.ppermute(block, axis, [(i ^ distance, i) for i in range(size)])  18.9 us
    all_to_all x2, waiting for transfers between devices, to_quarters(): lax.all_to_all(field, ('band', 'mesh'), 0, 0, axis_index_groups=quarters)  18 us
    all_to_all x1, blocking collectives, body(): lax.all_to_all(partial, 'mesh', 0, 0, axis_index_groups=plane).sum(0)  11.9 us
    all_to_all x1, waiting for transfers between devices, next_step(): lax.all_to_all(operand, 'mesh', 0, 0, axis_index_groups=groups_of(PARTS,...  11.4 us
    all_to_all x1, starting transfers between devices, body(): lax.all_to_all(partial, ('band', 'mesh'), 0, 0, axis_index_groups=along_z)  10.1 us
  transfers between devices with their start and end apart: 11, of which 6 were waited for; matrix products, arithmetic and copies ran while one was open for 1% of the time, Pallas kernels for 5%

profile of v7, /device:TPU:1, one launch (start us, length us, event | category | flops | bytes accessed | tf_op | source)
XLA Modules:
  0.0 256.4 jit_solution(9339623082200991452)
XLA Ops:
  0.7 0.7 add_select_fusion
  1.4 0.1 reshape.73
  1.5 0.7 add_bitcast_fusion
  2.2 5.9 %sort.14 = (s32[3256]{0:T(1024)S(1)}, s32[3256]{0:T(1024)}) sort(s32[3256]{0:T(1024)S(1)} %fusion.18, s32[3256]{0:T(1024)S(1)} %iota.7), dimensions={0}, to_apply=%region_0.1 | sort | flops 39072 | bytes 52096 | tf_op jit(solution)/shard_map/sort | solution.py:139
  8.8 1.0 fusion.20
  9.9 1.1 shard_map.95
  11.1 41.3 %all_to_all.40 = f32[4,248,128]{2,1,0:T(8,128)S(1)} all-to-all(f32[4,248,128]{2,1,0:T(8,128)S(1)} %pad_maximum_fusion.2), channel_id=1, replica_groups={{0,8,16,24},{1,9,17,25},{2,10,18,26},{3,11,19,27},{4,12,20,28},{5,13,21..., dimensions={0} | all-to-all | bytes 1015808 | tf_op jit(solution)/shard_map/all_to_all | solution.py:161
  52.5 0.1 fusion
  52.5 1.2 pad_maximum_fusion.1
  53.7 4.3 %all-to-all-start.1 = ((f32[4,4,152,128]{3,2,1,0:T(8,128)}), f32[4,4,152,128]{3,2,1,0:T(8,128)S(1)}, u32[]{:S(2)}, u32[]{:S(2)}) async-start(f32[4,4,152,128]{3,2,1,0:T(8,128)} %pad_maximum_fusion.1), calls=%async_computation.1 | async-start | bytes 2490368 | tf_op jit(solution)/shard_map/all_to_all | solution.py:161
  58.0 0.6 fusion.21
  62.2 0.1 stack.94.coef
  62.3 11.4 %all-to-all-done.1 = f32[4,4,152,128]{3,2,1,0:T(8,128)S(1)} async-done(((f32[4,4,152,128]{3,2,1,0:T(8,128)}), f32[4,4,152,128]{3,2,1,0:T(8,128)S(1)}, u32[]{:S(2)}, u32[]{:S(2)}) %all-to-all-start.1) | async-done | bytes 1245216 | tf_op jit(solution)/shard_map/all_to_all | solution.py:161
  74.0 0.1 pad_maximum_fusion
  74.2 0.2 copy.56
  74.3 7.6 %all_to_all.41 = f32[2,4,4,136,128]{4,3,1,2,0:T(8,128)S(1)} all-to-all(f32[2,4,4,136,128]{4,3,1,2,0:T(8,128)S(1)} %copy.56), channel_id=1, replica_groups={{0,1},{2,3},{4,5},{6,7},{8,9},{10,11},{12,13},{14,15},{16,17},{18,19},{..., dimensions={0} | all-to-all | bytes 4456448 | tf_op jit(solution)/shard_map/all_to_all | solution.py:161
  81.9 0.2 copy.57
  82.1 0.4 copy.94
  82.5 61.4 %shard_map.96.field = f32[128,4,128]{2,1,0:T(4,128)} custom-call(f32[8]{0:T(128)S(1)} %stack.94.coef, f32[32,17408]{1,0:T(8,128)S(1)} %bitcast.87, f32[8,128]{1,0:T(8,128)S(1)} %broadcast_in_dim.6.field, f32[384,384]{1,0:T(8,128)S(1)} %pad.15.matrix), custom_call_target="tpu_custom_call" | custom-call | flops 89999998976 | bytes 300000000 | tf_op jit(solution)/shard_map/pallas_call | solution.py:408
  143.9 11.5 %all-to-all-start.3 = ((f32[128,4,128]{2,1,0:T(4,128)}), f32[128,4,128]{2,1,0:T(4,128)S(1)}, u32[]{:S(2)}, u32[]{:S(2)}) async-start(f32[128,4,128]{2,1,0:T(4,128)} %shard_map.96.field), calls=%async_computation.3 | async-start | bytes 524288 | tf_op jit(solution)/shard_map/all_to_all | solution.py:462
  155.4 12.0 %shard_map.97 = f32[128,4,128]{2,1,0:T(4,128)} custom-call(f32[8]{0:T(128)S(1)} %stack.94.coef, f32[32,17408]{1,0:T(8,128)S(1)} %bitcast.88, f32[128,4,128]{2,1,0:T(4,128)} %shard_map.96.field, f32[384,384]{1,0:T(8,128)S(1)} %pad.15.matrix), custom_call_target="tpu_custom_call" | custom-call | flops 15000000512 | bytes 50000000 | tf_op jit(solution)/shard_map/pallas_call | solution.py:408
  167.4 7.8 %all-to-all-done.3 = f32[128,4,128]{2,1,0:T(4,128)S(1)} async-done(((f32[128,4,128]{2,1,0:T(4,128)}), f32[128,4,128]{2,1,0:T(4,128)S(1)}, u32[]{:S(2)}, u32[]{:S(2)}) %all-to-all-start.3) | async-done | bytes 262176 | tf_op jit(solution)/shard_map/all_to_all | solution.py:462
  175.3 8.9 %all-to-all-start.4 = ((f32[128,4,128]{2,1,0:T(4,128)}), f32[128,4,128]{2,1,0:T(4,128)S(1)}, u32[]{:S(2)}, u32[]{:S(2)}) async-start(f32[128,4,128]{2,1,0:T(4,128)} %shard_map.97), calls=%async_computation.4 | async-start | bytes 524288 | tf_op jit(solution)/shard_map/all_to_all | solution.py:462
  184.2 3.1 %collective-permute-start = (f32[128,512]{1,0:T(8,128)S(1)}, f32[128,512]{1,0:T(8,128)S(1)}, u32[]{:S(2)}, u32[]{:S(2)}) collective-permute-start(f32[128,512]{1,0:T(8,128)S(1)} %bitcast.97), channel_id=1, source_target_pairs={{128,0},{160,32},{192,64},{224,96},{0,128},{32,160},{64,192},{96,2... | collective-permute-start | bytes 786440 | tf_op jit(solution)/shard_map/ppermute | solution.py:63
  187.3 3.7 %collective-permute-start.5 = (f32[128,512]{1,0:T(8,128)S(1)}, f32[128,512]{1,0:T(8,128)S(1)}, u32[]{:S(2)}, u32[]{:S(2)}) collective-permute-start(f32[128,512]{1,0:T(8,128)S(1)} %bitcast.98), channel_id=1, source_target_pairs={{384,0},{416,32},{448,64},{480,96},{256,128},{288,160},{320,192},{... | collective-permute-start | bytes 786440 | tf_op jit(solution)/shard_map/ppermute | solution.py:63
  191.1 2.8 %collective-permute-start.4 = (f32[128,512]{1,0:T(8,128)S(1)}, f32[128,512]{1,0:T(8,128)S(1)}, u32[]{:S(2)}, u32[]{:S(2)}) collective-permute-start(f32[128,512]{1,0:T(8,128)S(1)} %bitcast.99), channel_id=1, source_target_pairs={{256,0},{288,32},{320,64},{352,96},{384,128},{416,160},{448,192},{... | collective-permute-start | bytes 786440 | tf_op jit(solution)/shard_map/ppermute | solution.py:63
  193.9 10.2 %all-to-all-done.4 = f32[128,4,128]{2,1,0:T(4,128)S(1)} async-done(((f32[128,4,128]{2,1,0:T(4,128)}), f32[128,4,128]{2,1,0:T(4,128)S(1)}, u32[]{:S(2)}, u32[]{:S(2)}) %all-to-all-start.4) | async-done | bytes 262176 | tf_op jit(solution)/shard_map/all_to_all | solution.py:462
  204.1 0.4 convolution_bitcast_fusion
  204.4 0.4 fusion.7
  204.8 0.4 fusion.3
  205.2 0.4 select_select_fusion.4
  205.9 0.2 maximum_bitcast_fusion.1
  206.2 0.1 reshape.82
  206.3 0.2 copy.64
  206.5 11.9 %all_to_all.42 = f32[8,4,4,512]{3,2,1,0:T(4,128)S(1)} all-to-all(f32[8,4,4,512]{3,2,1,0:T(4,128)S(1)} %copy.64), channel_id=1, replica_groups={{0,1,2,3,4,5,6,7},{8,9,10,11,12,13,14,15},{16,17,18,19,20,21,22,23},{24..., dimensions={0} | all-to-all | bytes 524288 | tf_op jit(solution)/shard_map/all_to_all | solution.py:480
  218.4 0.7 broadcast_in_dim.7
  219.1 10.1 %all-to-all-start.6 = ((f32[16,4,512]{2,1,0:T(4,128)}), f32[16,4,512]{2,1,0:T(4,128)S(1)}, u32[]{:S(2)}, u32[]{:S(2)}) async-start(f32[16,4,512]{2,1,0:T(4,128)} %bitcast.34), calls=%async_computation.6 | async-start | bytes 262144 | tf_op jit(solution)/shard_map/all_to_all | solution.py:484
  229.3 3.2 %collective-permute-start.1 = (f32[32,512]{1,0:T(8,128)S(1)}, f32[32,512]{1,0:T(8,128)S(1)}, u32[]{:S(2)}, u32[]{:S(2)}) collective-permute-start(f32[32,512]{1,0:T(8,128)S(1)} %get-tuple-element.30), channel_id=1, source_target_pairs={{32,0},{0,32},{96,64},{64,96},{160,128},{128,160},{224,192},{192,2... | collective-permute-start | bytes 196616 | tf_op jit(solution)/shard_map/ppermute | solution.py:63
  232.5 4.0 %collective-permute-start.2 = (f32[32,512]{1,0:T(8,128)S(1)}, f32[32,512]{1,0:T(8,128)S(1)}, u32[]{:S(2)}, u32[]{:S(2)}) collective-permute-start(f32[32,512]{1,0:T(8,128)S(1)} %get-tuple-element.29), channel_id=1, source_target_pairs={{64,0},{96,32},{0,64},{32,96},{192,128},{224,160},{128,192},{160,2... | collective-permute-start | bytes 196616 | tf_op jit(solution)/shard_map/ppermute | solution.py:63
  236.5 2.1 collective-permute-start.3
  238.6 3.0 %all-to-all-done.6 = f32[16,4,512]{2,1,0:T(4,128)S(1)} async-done(((f32[16,4,512]{2,1,0:T(4,128)}), f32[16,4,512]{2,1,0:T(4,128)S(1)}, u32[]{:S(2)}, u32[]{:S(2)}) %all-to-all-start.6) | async-done | bytes 131104 | tf_op jit(solution)/shard_map/all_to_all | solution.py:484
  241.7 2.2 collective-permute-done.3
  244.2 0.6 broadcast_in_dim.8
  244.8 6.0 %all-to-all-start.7 = ((f32[8,4,512]{2,1,0:T(4,128)}), f32[8,4,512]{2,1,0:T(4,128)S(1)}, u32[]{:S(2)}, u32[]{:S(2)}) async-start(f32[8,4,512]{2,1,0:T(4,128)} %broadcast_in_dim.8), calls=%async_computation.7 | async-start | bytes 131072 | tf_op jit(solution)/shard_map/all_to_all | solution.py:59
  250.8 0.3 pad_maximum_fusion.6
  251.1 0.8 copy.73
  251.9 3.8 %all-to-all-done.7 = f32[8,4,512]{2,1,0:T(4,128)S(1)} async-done(((f32[8,4,512]{2,1,0:T(4,128)}), f32[8,4,512]{2,1,0:T(4,128)S(1)}, u32[]{:S(2)}, u32[]{:S(2)}) %all-to-all-start.7) | async-done | bytes 65568 | tf_op jit(solution)/shard_map/all_to_all | solution.py:59
  255.7 0.7 reshape.85
  (46 shorter events, 1.3 us)
Async XLA Ops:
  0.6 9.2 %copy-start = (f32[2048]{0:T(1024)S(1)}, f32[2048]{0:T(1024)}, u32[]{:S(2)}) copy-start(f32[2048]{0:T(1024)} %param.9) | copy-start | bytes 24580
  0.6 9.2 %copy-start.1 = (f32[8]{0:T(128)S(1)}, f32[8]{0:T(128)}, u32[]{:S(2)}) copy-start(f32[8]{0:T(128)} %param.10) | copy-start | bytes 100
  53.7 4.3 %copy-start.3 = (f32[3]{0:T(128)S(1)}, f32[3]{0:T(128)}, u32[]{:S(2)}) copy-start(f32[3]{0:T(128)} %param.15) | copy-start | bytes 40
  53.7 8.5 %copy-start.2 = (f32[343,343]{1,0:T(8,128)S(1)}, f32[343,343]{1,0:T(8,128)}, u32[]{:S(2)}) copy-start(f32[343,343]{1,0:T(8,128)} %param.11) | copy-start | bytes 1411792
  53.7 20.0 %all-to-all-start.1 = ((f32[4,4,152,128]{3,2,1,0:T(8,128)}), f32[4,4,152,128]{3,2,1,0:T(8,128)S(1)}, u32[]{:S(2)}, u32[]{:S(2)}) async-start(f32[4,4,152,128]{3,2,1,0:T(8,128)} %pad_maximum_fusion.1), calls=%async_computation.1 | async-start | bytes 2490368 | tf_op jit(solution)/shard_map/all_to_all | solution.py:161
  143.9 31.4 %all-to-all-start.3 = ((f32[128,4,128]{2,1,0:T(4,128)}), f32[128,4,128]{2,1,0:T(4,128)S(1)}, u32[]{:S(2)}, u32[]{:S(2)}) async-start(f32[128,4,128]{2,1,0:T(4,128)} %shard_map.96.field), calls=%async_computation.3 | async-start | bytes 524288 | tf_op jit(solution)/shard_map/all_to_all | solution.py:462
  175.3 28.8 %all-to-all-start.4 = ((f32[128,4,128]{2,1,0:T(4,128)}), f32[128,4,128]{2,1,0:T(4,128)S(1)}, u32[]{:S(2)}, u32[]{:S(2)}) async-start(f32[128,4,128]{2,1,0:T(4,128)} %shard_map.97), calls=%async_computation.4 | async-start | bytes 524288 | tf_op jit(solution)/shard_map/all_to_all | solution.py:462
  184.2 20.2 %collective-permute-start = (f32[128,512]{1,0:T(8,128)S(1)}, f32[128,512]{1,0:T(8,128)S(1)}, u32[]{:S(2)}, u32[]{:S(2)}) collective-permute-start(f32[128,512]{1,0:T(8,128)S(1)} %bitcast.97), channel_id=1, source_target_pairs={{128,0},{160,32},{192,64},{224,96},{0,128},{32,160},{64,192},{96,2... | collective-permute-start | bytes 786440 | tf_op jit(solution)/shard_map/ppermute | solution.py:63
  187.3 17.5 %collective-permute-start.5 = (f32[128,512]{1,0:T(8,128)S(1)}, f32[128,512]{1,0:T(8,128)S(1)}, u32[]{:S(2)}, u32[]{:S(2)}) collective-permute-start(f32[128,512]{1,0:T(8,128)S(1)} %bitcast.98), channel_id=1, source_target_pairs={{384,0},{416,32},{448,64},{480,96},{256,128},{288,160},{320,192},{... | collective-permute-start | bytes 786440 | tf_op jit(solution)/shard_map/ppermute | solution.py:63
  191.1 14.1 %collective-permute-start.4 = (f32[128,512]{1,0:T(8,128)S(1)}, f32[128,512]{1,0:T(8,128)S(1)}, u32[]{:S(2)}, u32[]{:S(2)}) collective-permute-start(f32[128,512]{1,0:T(8,128)S(1)} %bitcast.99), channel_id=1, source_target_pairs={{256,0},{288,32},{320,64},{352,96},{384,128},{416,160},{448,192},{... | collective-permute-start | bytes 786440 | tf_op jit(solution)/shard_map/ppermute | solution.py:63
  219.1 22.5 %all-to-all-start.6 = ((f32[16,4,512]{2,1,0:T(4,128)}), f32[16,4,512]{2,1,0:T(4,128)S(1)}, u32[]{:S(2)}, u32[]{:S(2)}) async-start(f32[16,4,512]{2,1,0:T(4,128)} %bitcast.34), calls=%async_computation.6 | async-start | bytes 262144 | tf_op jit(solution)/shard_map/all_to_all | solution.py:484
  229.3 12.4 %collective-permute-start.1 = (f32[32,512]{1,0:T(8,128)S(1)}, f32[32,512]{1,0:T(8,128)S(1)}, u32[]{:S(2)}, u32[]{:S(2)}) collective-permute-start(f32[32,512]{1,0:T(8,128)S(1)} %get-tuple-element.30), channel_id=1, source_target_pairs={{32,0},{0,32},{96,64},{64,96},{160,128},{128,160},{224,192},{192,2... | collective-permute-start | bytes 196616 | tf_op jit(solution)/shard_map/ppermute | solution.py:63
  232.5 9.2 %collective-permute-start.2 = (f32[32,512]{1,0:T(8,128)S(1)}, f32[32,512]{1,0:T(8,128)S(1)}, u32[]{:S(2)}, u32[]{:S(2)}) collective-permute-start(f32[32,512]{1,0:T(8,128)S(1)} %get-tuple-element.29), channel_id=1, source_target_pairs={{64,0},{96,32},{0,64},{32,96},{192,128},{224,160},{128,192},{160,2... | collective-permute-start | bytes 196616 | tf_op jit(solution)/shard_map/ppermute | solution.py:63
  236.5 7.3 %collective-permute-start.3 = (f32[32,512]{1,0:T(8,128)S(1)}, f32[32,512]{1,0:T(8,128)S(1)}, u32[]{:S(2)}, u32[]{:S(2)}) collective-permute-start(f32[32,512]{1,0:T(8,128)S(1)} %get-tuple-element.28), channel_id=1, source_target_pairs={{96,0},{64,32},{32,64},{0,96},{224,128},{192,160},{160,192},{128,2... | collective-permute-start | bytes 196616 | tf_op jit(solution)/shard_map/ppermute | solution.py:63
  244.8 10.9 %all-to-all-start.7 = ((f32[8,4,512]{2,1,0:T(4,128)}), f32[8,4,512]{2,1,0:T(4,128)S(1)}, u32[]{:S(2)}, u32[]{:S(2)}) async-start(f32[8,4,512]{2,1,0:T(4,128)} %broadcast_in_dim.8), calls=%async_computation.7 | async-start | bytes 131072 | tf_op jit(solution)/shard_map/all_to_all | solution.py:59
